TPU v7x, 256 devices: a whole 4x4x8 slice. The times are simulated.
256 devices in a mesh: lat: 16 (over z, core), lon: 16 (over y, x).
Axes of the slice: x: 4, y: 4, z: 8, core: 2. Of those that a mesh axis runs over, the one named last changes fastest.
Arguments:
- tile_counts: int32 [16, 16], P('lat', 'lon'), may hold values from 1 to 2, as said below
- obs_pos: float32 [16, 16, 3, 1024], P('lat', 'lon'), as said below
- innovation: float32 [16, 16, 3, 1024], P('lat', 'lon'), may hold values from -6 to 6
- bg_std_obs: float32 [16, 16, 3, 1024], P('lat', 'lon'), may hold values from 0.05 to 0.2
- obs_std: float32 [16, 16, 3, 1024], P('lat', 'lon'), may hold values from 0.3 to 1
- channel_corr: float32 [3, 3], replicated, as said below
- bg_std_grid: float32 [16, 16, 3, 512], P('lat', 'lon'), may hold values from 0.05 to 0.2
Outputs:
- analysis_weights: float32 [16, 16, 3, 1024], P('lat', 'lon')
- increment: float32 [16, 16, 3, 512], P('lat', 'lon')
Inputs may be any that keep to these rules, and one draw needn't show every extreme that they name: Region (i, j) holds tile_counts[i, j] live tiles of 512 observations at its first slots; the other slots are padding. Some region holds 2 tiles in every draw. `obs_pos`: unit vectors; every slot of region (i, j), padding too, lies in that region: sine of latitude in -0.9 + 1.8 i / 16 to -0.9 + 1.8 (i + 1) / 16, longitude in 2 pi j / 16 to 2 pi (j + 1) / 16. `channel_corr`: Symmetric, unit diagonal, off-diagonal entries between 0.3 and 0.7.
All inputs are finite; a program needn't handle non-finite values.
Results may differ from a plain program's by a relative error of at most 0.0003.
Values sent between devices are 32-bit elements; how exact they have to be, the bound alone decides.
No kernel may reach another device: no remote copies, remote signals or barrier semaphores. Data moves between devices by JAX's collectives and lax.ppermute only.
A program may use at most 64 MiB of HBM per device.

v0:
```python
import math

import jax
import jax.numpy as jnp
from jax import lax
from jax.sharding import PartitionSpec as P

OBS_TILE = 512
GRID_ROWS = 16
ITERS = 3


def extended(cells, sides, width):
    for axis, dim in sides:
        count = lax.axis_size(axis)
        head = lax.slice_in_dim(cells, 0, width, axis=dim)
        tail = lax.slice_in_dim(cells, cells.shape[dim] - width, cells.shape[dim], axis=dim)
        cells = jnp.concatenate(
            [
                lax.ppermute(tail, axis, [(i, (i + 1) % count) for i in range(count)]),
                cells,
                lax.ppermute(head, axis, [((i + 1) % count, i) for i in range(count)]),
            ],
            axis=dim,
        )
    return cells


def gaspari(dist2, half):
    z = jnp.sqrt(dist2) / half
    inner = (((-0.25 * z + 0.5) * z + 0.625) * z - 5.0 / 3.0) * z * z + 1.0
    safe = jnp.maximum(z, 1.0)
    outer = (
        ((((z / 12.0 - 0.5) * z + 0.625) * z + 5.0 / 3.0) * z - 5.0) * z + 4.0 - 2.0 / (3.0 * safe)
    )
    return jnp.where(z <= 1.0, inner, jnp.where(z < 2.0, outer, 0.0))


def pair_block(targets, source_pos, source_val, half):
    dist2 = jnp.zeros((targets.shape[1], source_pos.shape[1]), jnp.float32)
    for comp in range(3):
        delta = targets[comp][:, None] - source_pos[comp][None, :]
        dist2 = dist2 + delta * delta
    rho = gaspari(dist2, half)
    return jnp.einsum("cj,ij->ci", source_val, rho, precision=lax.Precision.HIGHEST)


def source_tiles(near_pos, near_val):
    tiles = near_pos.shape[2] // OBS_TILE
    tile_pos = (
        near_pos.reshape(9, 3, tiles, OBS_TILE)
        .transpose(0, 2, 1, 3)
        .reshape(9 * tiles, 3, OBS_TILE)
    )
    tile_val = (
        near_val.reshape(9, 3, tiles, OBS_TILE)
        .transpose(0, 2, 1, 3)
        .reshape(9 * tiles, 3, OBS_TILE)
    )
    return (tile_pos, tile_val)


def correlate_scan(targets, tile_pos, tile_val, half):
    start = jnp.zeros((3, targets.shape[1]), jnp.float32)

    def step(acc, item):
        return (acc + pair_block(targets, item[0], item[1], half), None)

    acc, _ = lax.scan(step, start, (tile_pos, tile_val))
    return acc


def squares_total(residual):
    return lax.psum(jnp.sum(residual * residual), ("lat", "lon"))


def per_device(tile_counts, obs_pos, innovation, bg_std_obs, obs_std, channel_corr, bg_std_grid):
    bands = lax.axis_size("lat")
    sectors = lax.axis_size("lon")
    half = 0.3 / bands
    count = tile_counts[0, 0]
    position = obs_pos[0, 0]
    slots = position.shape[1]
    live = (jnp.arange(slots, dtype=jnp.int32) < count * OBS_TILE).astype(jnp.float32)[None, :]
    spread = bg_std_obs[0, 0]
    variance = obs_std[0, 0] * obs_std[0, 0]

    def near_field(values):
        both = jnp.concatenate([position, values], axis=0)[None, None]
        wide = extended(both, (("lat", 0), ("lon", 1)), 1).reshape(9, 6, slots)
        return (wide[:, :3], wide[:, 3:])

    weights = jnp.zeros((3, slots), jnp.float32)
    residual = live * innovation[0, 0]
    direction = residual
    norm_now = squares_total(residual)
    for step in range(ITERS):
        observe_near_pos, observe_near_val = near_field(spread * direction)
        observe_tile_pos, observe_tile_val = source_tiles(observe_near_pos, observe_near_val)
        operate_acc = correlate_scan(position, observe_tile_pos, observe_tile_val, half)
        mixed = jnp.dot(channel_corr, operate_acc, precision=lax.Precision.HIGHEST)
        image = live * (spread * mixed + variance * direction)
        alpha = norm_now / lax.psum(jnp.sum(direction * image), ("lat", "lon"))
        weights = weights + alpha * direction
        residual = residual - alpha * image
        norm_next = squares_total(residual)
        direction = residual + norm_next / norm_now * direction
        norm_now = norm_next
    cells = bg_std_grid.shape[3]
    columns = cells // GRID_ROWS
    cell = jnp.arange(cells, dtype=jnp.int32)
    frac_lat = ((cell // columns).astype(jnp.float32) + 0.5) / GRID_ROWS
    frac_lon = ((cell % columns).astype(jnp.float32) + 0.5) / columns
    band = lax.axis_index("lat").astype(jnp.float32)
    sector = lax.axis_index("lon").astype(jnp.float32)
    sinlat = -0.9 + 1.8 * (band + frac_lat) / bands
    longitude = 2.0 * math.pi * (sector + frac_lon) / sectors
    coslat = jnp.sqrt(1.0 - sinlat * sinlat)
    grid_pos = jnp.stack([coslat * jnp.cos(longitude), coslat * jnp.sin(longitude), sinlat], axis=0)
    near_pos, near_val = near_field(spread * weights)
    tile_pos, tile_val = source_tiles(near_pos, near_val)
    acc = correlate_scan(grid_pos, tile_pos, tile_val, half)
    increment = bg_std_grid[0, 0] * jnp.dot(channel_corr, acc, precision=lax.Precision.HIGHEST)
    return (weights[None, None], increment[None, None])


def solution(mesh):
    placed = (
        P("lat", "lon"),
        P("lat", "lon", None, None),
        P("lat", "lon", None, None),
        P("lat", "lon", None, None),
        P("lat", "lon", None, None),
        P(),
        P("lat", "lon", None, None),
    )
    return jax.shard_map(
        per_device,
        mesh=mesh,
        in_specs=placed,
        out_specs=(P("lat", "lon", None, None), P("lat", "lon", None, None)),
        check_vma=False,
    )
```

profile of v0, /device:TPU:1, one launch (start us, length us, event | category | flops | bytes accessed | tf_op | source)
XLA Modules:
  0.0 768.3 jit_solution(10847894990328998232)
XLA Ops:
  16.5 91.5 %while.54 = (s32[]{:T(128)}, f32[3,1024]{1,0:T(4,128)S(1)}, f32[18,3,512]{2,1,0:T(4,128)S(1)}, f32[3,1024]{1,0:T(4,128)S(1)}, f32[18,3,512]{2,1,0:T(4,128)S(1)}, /*index=5*/s32[]{:T(128)}, s32[]{:T(128)}, s32[]{}, s32[]{}) while((s32[]{:T(128)}, f32[3,1024]{1,0:T(4,128)S(1)}, f32[18,3,512]{2,1,0:T(4,128)S(1)}, ...), condition=%wide.region_3.4_spmd.clone, body=%wide.region_2.3_spmd.clone.sunk | while | flops 37754884 | bytes 92303 | solution.py:69
  16.6 5.0 fusion.371
  21.7 5.0 fusion.371
  26.7 5.0 fusion.371
  31.8 5.0 fusion.371
  36.9 5.0 fusion.371
  42.0 5.0 fusion.371
  47.1 5.0 fusion.371
  52.1 5.0 fusion.371
  57.2 5.0 fusion.371
  62.3 5.0 fusion.371
  67.4 5.0 fusion.371
  72.5 5.0 fusion.371
  77.6 5.0 fusion.371
  82.6 5.0 fusion.371
  87.7 5.0 fusion.371
  92.8 5.0 fusion.371
  97.9 5.0 fusion.371
  103.0 5.0 fusion.371
  108.8 80.8 %all-reduce = (f32[]{:T(128)}, f32[]{:T(128)}) all-reduce(f32[]{:T(128)} %get-tuple-element.442, f32[]{:T(128)} %get-tuple-element.441), channel_id=1, replica_groups=mesh['lat'=16,'lon'=16] {'lat','lon'}, use_global_device_ids=true, to_apply=%region_1.0 | all-reduce | flops 2 | bytes 16 | tf_op jit(solution)/shard_map/psum | solution.py:74
  191.6 72.4 %psum.44 = f32[]{:T(128)} all-reduce(f32[]{:T(128)} %multiply_reduce_fusion.2), channel_id=1, replica_groups=mesh['lat'=16,'lon'=16] {'lat','lon'}, use_global_device_ids=true, to_apply=%region_7.8 | all-reduce | flops 1 | bytes 8 | tf_op jit(solution)/shard_map/psum | solution.py:74
  279.5 91.5 %while.55 = (s32[]{:T(128)}, f32[3,1024]{1,0:T(4,128)S(1)}, f32[18,3,512]{2,1,0:T(4,128)S(1)}, f32[3,1024]{1,0:T(4,128)S(1)}, f32[18,3,512]{2,1,0:T(4,128)S(1)}, /*index=5*/s32[]{:T(128)}, s32[]{:T(128)}, s32[]{}, s32[]{}) while((s32[]{:T(128)}, f32[3,1024]{1,0:T(4,128)S(1)}, f32[18,3,512]{2,1,0:T(4,128)S(1)}, ...), condition=%wide.region_9.10_spmd.clone, body=%wide.region_8.9_spmd.clone.sunk | while | flops 37754884 | bytes 92303 | solution.py:69
  284.7 5.0 fusion.375
  294.8 5.0 fusion.375
  371.8 75.8 %psum.45 = f32[]{:T(128)} all-reduce(f32[]{:T(128)} %get-tuple-element.529), channel_id=1, replica_groups=mesh['lat'=16,'lon'=16] {'lat','lon'}, use_global_device_ids=true, to_apply=%region_11.12 | all-reduce | flops 1 | bytes 8 | tf_op jit(solution)/shard_map/psum | solution.py:103
  449.6 73.1 %psum.46 = f32[]{:T(128)} all-reduce(f32[]{:T(128)} %multiply_reduce_fusion), channel_id=1, replica_groups=mesh['lat'=16,'lon'=16] {'lat','lon'}, use_global_device_ids=true, to_apply=%region_13.14 | all-reduce | flops 1 | bytes 8 | tf_op jit(solution)/shard_map/psum | solution.py:74
  536.8 91.5 %while.56 = (s32[]{:T(128)}, f32[3,1024]{1,0:T(4,128)S(1)}, f32[18,3,512]{2,1,0:T(4,128)S(1)}, f32[3,1024]{1,0:T(4,128)S(1)}, f32[18,3,512]{2,1,0:T(4,128)S(1)}, /*index=5*/s32[]{:T(128)}, s32[]{:T(128)}, s32[]{}, s32[]{}) while((s32[]{:T(128)}, f32[3,1024]{1,0:T(4,128)S(1)}, f32[18,3,512]{2,1,0:T(4,128)S(1)}, ...), condition=%wide.region_15.16_spmd.clone, body=%wide.region_14.15_spmd.clone.sunk | while | flops 37754884 | bytes 92303 | solution.py:69
  603.0 5.0 fusion.379
  613.1 5.0 fusion.379
  623.3 5.0 fusion.379
  629.1 77.0 %psum.47 = f32[]{:T(128)} all-reduce(f32[]{:T(128)} %fusion.332), channel_id=1, replica_groups=mesh['lat'=16,'lon'=16] {'lat','lon'}, use_global_device_ids=true, to_apply=%region_17.18 | all-reduce | flops 1 | bytes 8 | tf_op jit(solution)/shard_map/psum | solution.py:103
  718.7 48.8 %while.57 = (s32[]{:T(128)}, f32[3,512]{1,0:T(4,128)S(1)}, f32[18,3,512]{2,1,0:T(4,128)S(1)}, f32[18,3,512]{2,1,0:T(4,128)S(1)}, f32[]{:T(128)}, /*index=5*/f32[]{:T(128)}, s32[]{:T(128)}, s32[]{:T(128)}, s32[]{}, s32[]{}) while((s32[]{:T(128)}, f32[3,512]{1,0:T(4,128)S(1)}, ...), condition=%wide.region_19.20_spmd.clone.clone.clone, body=%wide.region_18.19_spmd.clone.clone.clone.sunk | while | flops 18904068 | bytes 53415 | solution.py:69
  (302 shorter events, 262.9 us)
Async XLA Ops:
  0.6 107.4 %copy-start = (f32[3,3]{1,0:T(4,128)S(1)}, f32[3,3]{1,0:T(4,128)}, u32[]{:S(2)}) copy-start(f32[3,3]{1,0:T(4,128)} %param.20) | copy-start | bytes 112
  2.8 4.1 collective-permute-start
  5.8 3.3 collective-permute-start.1
  9.2 7.0 collective-permute-start.2
  10.5 5.7 collective-permute-start.3
  16.5 91.5 %copy-start.1 = (f32[1,1,3,1024]{3,1,2,0:T(1,128)S(1)}, f32[1,1,3,1024]{3,1,2,0:T(1,128)}, u32[]{:S(2)}) copy-start(f32[1,1,3,1024]{3,1,2,0:T(1,128)} %param.17) | copy-start | bytes 36868
  16.5 91.5 %copy-start.2 = (f32[1,1,3,1024]{3,1,2,0:T(1,128)S(1)}, f32[1,1,3,1024]{3,1,2,0:T(1,128)}, u32[]{:S(2)}) copy-start(f32[1,1,3,1024]{3,1,2,0:T(1,128)} %param.18) | copy-start | bytes 36868
  16.5 91.5 %copy-start.4 = (f32[1,1,3,1024]{3,1,2,0:T(1,128)S(1)}, f32[1,1,3,1024]{3,1,2,0:T(1,128)}, u32[]{:S(2)}) copy-start(f32[1,1,3,1024]{3,1,2,0:T(1,128)} %param.19) | copy-start | bytes 36868
  265.3 3.4 collective-permute-start.4
  267.7 3.3 collective-permute-start.5
  271.0 8.2 %collective-permute-start.6 = (f32[3,1,6,1024]{3,2,1,0:T(8,128)S(1)}, f32[3,1,6,1024]{3,2,1,0:T(8,128)S(1)}, u32[]{:S(2)}, u32[]{:S(2)}) collective-permute-start(f32[3,1,6,1024]{3,2,1,0:T(8,128)S(1)} %pad_maximum_fusion.13), channel_id=1, source_target_pairs={{0,1},{1,2},{2,3},{3,4},{4,5},{5,6},{6,7},{7,8},{8,9},{9,10},{10,1... | collective-permute-start | bytes 221192 | tf_op jit(solution)/shard_map/ppermute | solution.py:20
  271.5 7.7 %collective-permute-start.7 = (f32[3,1,6,1024]{3,2,1,0:T(8,128)S(1)}, f32[3,1,6,1024]{3,2,1,0:T(8,128)S(1)}, u32[]{:S(2)}, u32[]{:S(2)}) collective-permute-start(f32[3,1,6,1024]{3,2,1,0:T(8,128)S(1)} %pad_maximum_fusion.13), channel_id=1, source_target_pairs={{1,0},{2,1},{3,2},{4,3},{5,4},{6,5},{7,6},{8,7},{9,8},{10,9},{11,1... | collective-permute-start | bytes 221192 | tf_op jit(solution)/shard_map/ppermute | solution.py:22
  524.1 2.6 collective-permute-start.8
  525.7 3.3 collective-permute-start.9
  529.0 7.5 collective-permute-start.10
  529.6 6.9 collective-permute-start.11
  707.4 1.9 collective-permute-start.12
  708.2 3.3 collective-permute-start.13
  711.5 6.9 collective-permute-start.14
  711.6 6.8 collective-permute-start.15
  718.7 48.8 %copy-start.3 = (f32[1,1,3,512]{3,1,2,0:T(1,128)S(1)}, f32[1,1,3,512]{3,1,2,0:T(1,128)}, u32[]{:S(2)}) copy-start(f32[1,1,3,512]{3,1,2,0:T(1,128)} %param.21) | copy-start | bytes 18436
where the time goes:
time: 771 us; the launch traced here: 768 us
  blocking collectives  379 us (49%)
  matrix products  319 us (41%)
  starting transfers between devices  28.1 us (4%)
  waiting for transfers between devices  21.9 us (3%)
  between operations  8.34 us (1%)
    dot_general x72, matrix products, pair_block(): jnp.einsum('cj,ij->ci', source_val, rho, precision=lax.Precision.HIGHEST)  317 us
    psum x3, blocking collectives, squares_total(): return lax.psum(jnp.sum(residual * residual), ('lat', 'lon'))  226 us
    psum x2, blocking collectives, per_device(): alpha = norm_now / lax.psum(jnp.sum(direction * image), ('lat', 'lon'))  153 us
    ppermute x8, starting transfers between devices, extended(): lax.ppermute(head, axis, [((i + 1) % count, i) for i in range(count)])  18 us
  transfers between devices with their start and end apart: 16, of which 12 were waited for; matrix products, arithmetic and copies ran while one was open for 0% of the time, Pallas kernels for 0%

commit v1 on v0

v1 whole, which is shorter than its diff:
```python
import math

import jax
import jax.numpy as jnp
import numpy as np
from jax import lax
from jax.experimental import pallas as pl
from jax.experimental.pallas import tpu as pltpu
from jax.sharding import PartitionSpec as P

OBS_TILE = 512
GRID_ROWS = 16
BLK = 128
SHIFT = 0.5
FAR = 64.0
NT = (((1,), (1,)), ((), ()))
NN = (((1,), (0,)), ((), ()))
F32 = jnp.float32
BF16 = jnp.bfloat16
VLIM = 48 * 1024 * 1024


def split3(x):
    hi = x.astype(BF16)
    rest = x - hi.astype(F32)
    mid = rest.astype(BF16)
    low = (rest - mid.astype(F32)).astype(BF16)
    return jnp.concatenate([hi, mid, low], axis=0)


def col_of(row):
    return jnp.transpose(jnp.broadcast_to(row, (8, row.shape[1])))[:, 0:1]


def rank_of(key, slots):
    col = col_of(key)
    parts = []
    for j in range(slots // BLK):
        kj = key[:, j * BLK : (j + 1) * BLK]
        total = jnp.zeros((8, BLK), F32)
        for i in range(slots // BLK):
            ki = jnp.broadcast_to(col[i * BLK : (i + 1) * BLK, :], (BLK, BLK))
            if i < j:
                before = ki <= kj
            elif i > j:
                before = ki < kj
            else:
                first = lax.broadcasted_iota(jnp.int32, (BLK, BLK), 0) < lax.broadcasted_iota(
                    jnp.int32, (BLK, BLK), 1
                )
                before = (ki < kj) | ((ki == kj) & first)
            ones = jnp.where(before, 1.0, 0.0).astype(F32)
            total = total + jnp.sum(ones.reshape(BLK // 8, 8, BLK), axis=0)
        parts.append(jnp.sum(total, axis=0, keepdims=True))
    return jnp.concatenate(parts, axis=1)


def onehot_of(rank, slots):
    place = lax.broadcasted_iota(jnp.int32, (slots, slots), 0).astype(F32)
    return jnp.where(place == rank, 1.0, 0.0).astype(BF16)


def sort_kernel(count, frame, pos, innov, bg, std, hb_out, own_out, rank_out):
    slots = pos.shape[3]
    live_n = count[0, 0] * OBS_TILE
    lane = lax.broadcasted_iota(jnp.int32, (1, slots), 1)
    live = lane < live_n
    px, py, pz = pos[0, 0, 0:1, :], pos[0, 0, 1:2, :], pos[0, 0, 2:3, :]
    key = jnp.where(live, pz, 10.0)
    first = rank_of(key, slots)
    strip = jnp.where(first * 2.0 >= live_n.astype(F32), 8.0, 0.0)
    east = frame[0:1, 0:1] * px + frame[0:1, 1:2] * py
    east = east * lax.rsqrt(jnp.maximum(1.0 - pz * pz, 1e-6)) * (0.3 / 16)
    rank = rank_of(jnp.where(live, strip + east, 100.0), slots)
    rank_out[...] = rank
    maskf = jnp.where(live, 1.0, 0.0).astype(F32)
    where3 = jnp.where(live, pos[0, 0], FAR)
    dev = bg[0, 0] * maskf
    start = innov[0, 0] * maskf
    var = std[0, 0] * std[0, 0] * maskf
    pad = jnp.zeros((4, slots), F32)
    vals = jnp.concatenate([where3, dev, start, var, pad], axis=0)
    got = lax.dot_general(split3(vals), onehot_of(rank, slots), NT, preferred_element_type=F32)
    got = got[0:16] + got[16:32] + got[32:48]
    dev, start = got[3:6], got[6:9]
    own_out[...] = got
    hb_out[...] = jnp.concatenate([dev * start, got[0:3], pad[0:2]], axis=0)


def rho_of(tcol, sx, sy, sz):
    dx, dy, dz = tcol[0] - sx, tcol[1] - sy, tcol[2] - sz
    s = dx * dx + dy * dy + dz * dz
    r = lax.rsqrt(jnp.maximum(s, 1e-30))
    z = s * r
    inner = s * (((-0.25 * z + 0.5) * z + 0.625) * z - 5.0 / 3.0) + 1.0
    t = jnp.maximum(2.0 - z, 0.0)
    t = t * t
    u = z + 1.0
    outer = (t * t) * (u * u * (1.0 / 12.0) - 0.125) * r
    return jnp.where(s <= 1.0, inner, outer)


def to_frame(tile, row, frame):
    q = None
    for k in range(3):
        term = frame[:, k : k + 1] * (tile[row + k : row + k + 1, :] - frame[:, 3 + k : 4 + k])
        q = term if q is None else q + term
    return q


def boxes(tile):
    return jnp.min(tile, axis=1, keepdims=True), jnp.max(tile, axis=1, keepdims=True)


def correlate(halo, fields, frame, target_tiles, q_ref, v_ref, tcol, pair, mask_v, mask_s, sem, acc):
    nt = len(target_tiles)
    per = halo[0].shape[2] // BLK
    nf = len(fields)
    lane = lax.broadcasted_iota(jnp.int32, (8, BLK), 1)
    low = jnp.full((8, BLK), 1e6, F32)
    high = jnp.full((8, BLK), 1e6, F32)
    for c in range(3):
        for a in range(3):
            r = c * 3 + a
            q = to_frame(halo[c][a], 3, frame)
            for b in range(per):
                tile = q[:, b * BLK : (b + 1) * BLK]
                q_ref[r * per + b] = tile
                lo, hi = boxes(tile)
                low = jnp.where(lane == r * per + b, lo, low)
                high = jnp.where(lane == r * per + b, hi, high)
            for f in range(nf):
                for b in range(per):
                    v = split3(fields[f][c][a, :, b * BLK : (b + 1) * BLK])
                    v = jnp.concatenate([v, jnp.zeros((8, BLK), BF16)], axis=0)
                    v_ref[r * per + b, 32 * f : 32 * f + 32, 0:BLK] = v
                    v_ref[r * per + b, 32 * f : 32 * f + 32, BLK : 2 * BLK] = v
    bits = jnp.zeros((1, BLK), jnp.int32)
    for t in range(nt):
        tile = target_tiles[t]
        lo, hi = boxes(tile)
        gap = jnp.maximum(jnp.maximum(lo - high, low - hi), 0.0)
        gap2 = jnp.sum(gap * gap, axis=0, keepdims=True)
        far = jnp.sum(lo * lo, axis=0, keepdims=True)
        bits = bits + jnp.where((gap2 < 4.001) & (far < 1e6), 1 << t, 0)
        turned = jnp.transpose(tile)
        for k in range(3):
            tcol[t, k] = jnp.broadcast_to(turned[:, k : k + 1], (BLK, BLK))
        acc[t] = jnp.zeros(acc.shape[1:], F32)
    mask_v[...] = jnp.broadcast_to(bits, (8, BLK))
    copy = pltpu.make_async_copy(mask_v, mask_s, sem)
    copy.start()
    copy.wait()

    def source(n, _):
        word = mask_s[0, n]

        @pl.when(word != 0)
        def _():
            def target(t, _):
                @pl.when(((word >> t) & 1) != 0)
                def _():
                    q = q_ref[n]
                    sx, sy, sz = q[0:1], q[1:2], q[2:3]
                    for i in range(0, BLK, 32):
                        rho = rho_of([tcol[t, k, i : i + 32] for k in range(3)], sx, sy, sz)
                        hi = rho.astype(BF16)
                        pair[i : i + 32, 0:BLK] = hi
                        pair[i : i + 32, BLK : 2 * BLK] = (rho - hi.astype(F32)).astype(BF16)
                    out = lax.dot_general(v_ref[n], pair[...], NT, preferred_element_type=F32)
                    for f in range(nf):
                        o = out[32 * f : 32 * f + 32]
                        acc[t, f] += o[0:8] + o[8:16] + o[16:24]

                return 0

            lax.fori_loop(0, nt, target, 0)

        return 0

    lax.fori_loop(0, 9 * per, source, 0)


def mix(corr, acc):
    return jnp.concatenate(
        [
            corr[c, 0] * acc[0:1] + corr[c, 1] * acc[1:2] + corr[c, 2] * acc[2:3]
            for c in range(3)
        ],
        axis=0,
    )


def operate(refs, acc, own, corr, field):
    total = jnp.concatenate([acc[t, 0] for t in range(acc.shape[0])], axis=1)
    dev, var = own[3:6], own[9:12]
    return dev * mix(corr, total) + var * field


def apply_kernel(corr, frame, hm, hw, he, um, uw, ue, own, field, u_out, img_out, nxt_out, *scratch):
    q_ref, v_ref, tcol, pair, mask_v, mask_s, sem, acc = scratch
    frame = frame[...]
    per = hm.shape[2] // BLK
    q = to_frame(hm[1], 3, frame)
    targets = [q[:, t * BLK : (t + 1) * BLK] for t in range(per)]
    correlate((hm, hw, he), [(um, uw, ue)], frame, targets, *scratch)
    mine = own[...]
    image = operate(None, acc, mine, corr, field[...])
    nxt = image - SHIFT * field[...]
    img_out[...] = image
    nxt_out[...] = nxt
    u_out[...] = jnp.concatenate([mine[3:6] * nxt, jnp.zeros((5, nxt.shape[1]), F32)], axis=0)


def gram_kernel(b0, b1, b2, a0, a1, a2, out):
    pairs = [(b0, a0), (b0, a1), (b0, a2), (b1, a1), (b1, a2), (b2, a2), (b0, b0), (b1, b0), (b2, b0)]
    lane = lax.broadcasted_iota(jnp.int32, (1, BLK), 1)
    row = jnp.zeros((1, BLK), F32)
    for k, (x, y) in enumerate(pairs):
        prod = x[...] * y[...]
        total = jnp.sum(jnp.sum(prod, axis=0, keepdims=True), axis=1, keepdims=True)
        row = jnp.where(lane == k, total, row)
    out[...] = row


def grid_kernel(corr, frame, gpos, hm, hw, he, um, uw, ue, xm, xw, xe, bgg, rank, b1, b2, g_out, w_out, *scratch):
    acc = scratch[-1]
    frame = frame[...]
    nt = gpos.shape[1] // BLK
    q = to_frame(gpos[...], 0, frame)
    targets = [q[:, t * BLK : (t + 1) * BLK] for t in range(nt)]
    correlate(
        (hm, hw, he), [(hm, hw, he), (um, uw, ue), (xm, xw, xe)], frame, targets, *scratch
    )
    for f in range(3):
        total = jnp.concatenate([acc[t, f] for t in range(nt)], axis=1)
        g_out[f] = bgg[0, 0] * mix(corr, total)
    slots = rank.shape[1]
    vals = jnp.concatenate([b1[...], b2[...], jnp.zeros((10, slots), F32)], axis=0)
    back = lax.dot_general(split3(vals), onehot_of(rank[...], slots), NN, preferred_element_type=F32)
    back = back[0:16] + back[16:32] + back[32:48]
    w_out[0] = back[0:3]
    w_out[1] = back[3:6]


def final_kernel(count, parts, innov, w, g, w_out, g_out):
    sums = jnp.sum(parts[...], axis=0, keepdims=True)
    lane = lax.broadcasted_iota(jnp.int32, sums.shape, 1)
    m00, m01, m02, m11, m12, m22, g0, g1, g2 = [
        jnp.sum(jnp.where(lane == k, sums, 0.0), axis=1, keepdims=True) for k in range(9)
    ]
    l10, l20 = m01 / m00, m02 / m00
    d1 = m11 - l10 * m01
    e12 = m12 - l10 * m02
    ok1 = d1 > 1e-6 * m11
    safe1 = jnp.where(ok1, d1, 1.0)
    l21 = jnp.where(ok1, e12 / safe1, 0.0)
    d2 = m22 - l20 * m02 - l21 * e12
    ok2 = ok1 & (d2 > 1e-6 * m22)
    y1 = g1 - l10 * g0
    y2 = g2 - l20 * g0 - l21 * y1
    c2 = jnp.where(ok2, y2 / jnp.where(ok2, d2, 1.0), 0.0)
    c1 = jnp.where(ok1, y1 / safe1, 0.0) - l21 * c2
    c0 = g0 / m00 - l10 * c1 - l20 * c2
    slots = innov.shape[3]
    live = lax.broadcasted_iota(jnp.int32, (1, slots), 1) < count[0, 0] * OBS_TILE
    w_out[0, 0] = c0 * jnp.where(live, innov[0, 0], 0.0) + c1 * w[0] + c2 * w[1]
    g_out[0, 0] = c0 * g[0] + c1 * g[1] + c2 * g[2]


def spread_halo(block):
    nl, nn = lax.axis_size("lat"), lax.axis_size("lon")

    def ring(x, axis, count, step):
        return lax.ppermute(x, axis, [(i, (i + step) % count) for i in range(count)])

    mid = jnp.stack([ring(block, "lat", nl, 1), block, ring(block, "lat", nl, -1)])
    return mid, ring(mid, "lon", nn, 1), ring(mid, "lon", nn, -1)


def frames(bands, sectors):
    table = np.zeros((bands, sectors, 8, 8), np.float64)
    half = 0.3 / bands
    for i in range(bands):
        s = -0.9 + 1.8 * (i + 0.5) / bands
        c = math.sqrt(1.0 - s * s)
        for j in range(sectors):
            lam = 2.0 * math.pi * (j + 0.5) / sectors
            cl, sl = math.cos(lam), math.sin(lam)
            table[i, j, :3, :3] = np.array([[-sl, cl, 0.0], [-s * cl, -s * sl, c], [c * cl, c * sl, s]]) / half
            table[i, j, :, 3:6] = [c * cl, c * sl, s]
    return table.astype(np.float32)


def scratch_for(nt, nf, sources):
    return [
        pltpu.VMEM((sources, 8, BLK), F32),
        pltpu.VMEM((sources, 32 * nf, 2 * BLK), BF16),
        pltpu.VMEM((nt, 3, BLK, BLK), F32),
        pltpu.VMEM((BLK, 2 * BLK), BF16),
        pltpu.VMEM((8, BLK), jnp.int32),
        pltpu.SMEM((8, BLK), jnp.int32),
        pltpu.SemaphoreType.DMA,
        pltpu.VMEM((nt, nf, 8, BLK), F32),
    ]


VM = pl.BlockSpec(memory_space=pltpu.VMEM)
SM = pl.BlockSpec(memory_space=pltpu.SMEM)


def call(kernel, name, ins, outs, scratch, flops):
    return pl.pallas_call(
        kernel,
        out_shape=[jax.ShapeDtypeStruct(s, F32) for s in outs],
        in_specs=ins,
        out_specs=[VM] * len(outs),
        scratch_shapes=scratch,
        name=name,
        compiler_params=pltpu.CompilerParams(vmem_limit_bytes=VLIM),
        cost_estimate=pl.CostEstimate(flops=flops, bytes_accessed=1 << 20, transcendentals=0),
    )


def per_device(tile_counts, obs_pos, innovation, bg_std_obs, obs_std, channel_corr, bg_std_grid):
    bands, sectors = lax.axis_size("lat"), lax.axis_size("lon")
    band, sector = lax.axis_index("lat"), lax.axis_index("lon")
    slots = obs_pos.shape[3]
    cells = bg_std_grid.shape[3]
    sources = 9 * slots // BLK
    frame = lax.dynamic_slice(
        jnp.asarray(frames(bands, sectors)), (band, sector, 0, 0), (1, 1, 8, 8)
    ).reshape(8, 8)

    hb, own, rank = call(
        sort_kernel, "sort", [SM] + [VM] * 5, [(8, slots), (16, slots), (1, slots)], [], 10**8
    )(tile_counts, frame, obs_pos, innovation, bg_std_obs, obs_std)
    near = spread_halo(hb)
    apply = call(
        apply_kernel,
        "apply",
        [SM] + [VM] * 9,
        [(8, slots), (3, slots), (3, slots)],
        scratch_for(slots // BLK, 1, sources),
        10**9,
    )
    b0 = own[6:9]
    u1, a0, b1 = apply(channel_corr, frame, *near, *near, own, b0)
    near1 = spread_halo(u1)
    u2, a1, b2 = apply(channel_corr, frame, *near, *near1, own, b1)
    near2 = spread_halo(u2)
    _, a2, _ = apply(channel_corr, frame, *near, *near2, own, b2)
    (sums,) = call(gram_kernel, "gram", [VM] * 6, [(1, BLK)], [], 10**6)(b0, b1, b2, a0, a1, a2)
    copies = jnp.broadcast_to(sums[:, :16], (bands * sectors, 16))
    parts = lax.all_to_all(copies, ("lat", "lon"), 0, 0, tiled=True)

    columns = cells // GRID_ROWS
    cell = jnp.arange(cells, dtype=jnp.int32)
    frac_lat = ((cell // columns).astype(F32) + 0.5) / GRID_ROWS
    frac_lon = ((cell % columns).astype(F32) + 0.5) / columns
    sinlat = -0.9 + 1.8 * (band.astype(F32) + frac_lat) / bands
    longitude = 2.0 * math.pi * (sector.astype(F32) + frac_lon) / sectors
    coslat = jnp.sqrt(1.0 - sinlat * sinlat)
    grid_pos = jnp.stack([coslat * jnp.cos(longitude), coslat * jnp.sin(longitude), sinlat], axis=0)
    parts_g, parts_w = call(
        grid_kernel,
        "grid",
        [SM] + [VM] * 15,
        [(3, 3, cells), (2, 3, slots)],
        scratch_for(cells // BLK, 3, sources),
        10**9,
    )(channel_corr, frame, grid_pos, *near, *near1, *near2, bg_std_grid, rank, b1, b2)
    return tuple(
        call(
            final_kernel,
            "final",
            [SM] + [VM] * 4,
            [(1, 1, 3, slots), (1, 1, 3, cells)],
            [],
            10**6,
        )(tile_counts, parts, innovation, parts_w, parts_g)
    )


def solution(mesh):
    spec = P("lat", "lon", None, None)
    return jax.shard_map(
        per_device,
        mesh=mesh,
        in_specs=(P("lat", "lon"), spec, spec, spec, spec, P(), spec),
        out_specs=(spec, spec),
        check_vma=False,
    )
```

time: 771 us -> 147 us (0.19)
  the two profiles are of different devices: /device:TPU:1 before, /device:TPU:107 now
where the time goes in v1:
time: 147 us; the launch traced here: 144 us
  Pallas kernels  93.9 us (64%)
  starting transfers between devices  31.5 us (21%)
  waiting for transfers between devices  12.5 us (9%)
  local copies, waits for them, and re-layouts  4.82 us (3%)
    pallas_call x1, Pallas kernels, per_device(): _, a2, _ = apply(channel_corr, frame, *near, *near2, own, b2)  24.6 us
    pallas_call x1, Pallas kernels, per_device(): u2, a1, b2 = apply(channel_corr, frame, *near, *near1, own, b1)  23.9 us
    pallas_call x1, Pallas kernels, per_device(): u1, a0, b1 = apply(channel_corr, frame, *near, *near, own, b0)  23.9 us
    pallas_call x1, Pallas kernels, per_device(): call(grid_kernel, 'grid', [SM] + [VM] * 15, [(3, 3, cells), (2, 3, slots)...  19 us
    all_to_all x1, starting transfers between devices, per_device(): parts = lax.all_to_all(copies, ('lat', 'lon'), 0, 0, tiled=True)  17.5 us
    ppermute x12, starting transfers between devices, ring(): lax.ppermute(x, axis, [(i, (i + step) % count) for i in range(count)])  14 us
    ppermute x12, waiting for transfers between devices, ring(): lax.ppermute(x, axis, [(i, (i + step) % count) for i in range(count)])  12.5 us
  transfers between devices with their start and end apart: 13, of which 9 were waited for; matrix products, arithmetic and copies ran while one was open for 0% of the time, Pallas kernels for 13%

profile of v1, /device:TPU:107, one launch (start us, length us, event | category | flops | bytes accessed | tf_op | source)
XLA Modules:
  0.0 144.3 jit_solution(17088053265779077609)
XLA Ops:
  1.3 0.7 copy-done.2
  2.1 0.7 copy-done.3
  2.8 0.7 copy-done.4
  3.5 0.7 dynamic-slice_bitcast_fusion.frame
  4.2 2.1 %sort.1 = (f32[8,1024]{1,0:T(8,128)S(1)}, f32[16,1024]{1,0:T(8,128)S(1)}, f32[1,1024]{1,0:T(1,128)S(1)}) custom-call(s32[1,1]{1,0:T(1,128)S(6)} %copy.26.count, f32[8,8]{1,0:T(8,128)S(1)} %dynamic-slice_bitcast_fusion.frame, f32[1,1,3,1024]{3,2,1,0:T(4,128)S(1)} %copy.18.pos, f32[1,1,3,1024]{3,2,1,0:T(4,128)S(1)} %copy.19.innov, ...), custom_call_target="tpu_custom_call" | custom-call | flops 100000000 | bytes 1048576 | tf_op jit(solution)/shard_map/sort/pallas_call | solution.py:335
  6.3 0.7 collective-permute-start.1
  7.0 2.8 %collective-permute-start = (f32[8,1024]{1,0:T(8,128)S(1)}, f32[8,1024]{1,0:T(8,128)S(1)}, u32[]{:S(2)}, u32[]{:S(2)}) collective-permute-start(f32[8,1024]{1,0:T(8,128)S(1)} %get-tuple-element.15), channel_id=1, source_target_pairs={{0,16},{16,32},{32,48},{48,64},{64,80},{80,96},{96,112},{112,128},... | collective-permute-start | bytes 98312 | tf_op jit(solution)/shard_map/ppermute | solution.py:275
  9.7 1.6 %collective-permute-done.1 = f32[8,1024]{1,0:T(8,128)S(1)} collective-permute-done((f32[8,1024]{1,0:T(8,128)S(1)}, f32[8,1024]{1,0:T(8,128)S(1)}, u32[]{:S(2)}, u32[]{:S(2)}) %collective-permute-start.1) | collective-permute-done | bytes 32800 | tf_op jit(solution)/shard_map/ppermute | solution.py:275
  11.3 0.3 collective-permute-start.3
  11.7 1.2 collective-permute-start.2
  12.9 2.8 %collective-permute-done.3.he.ue = f32[3,8,1024]{2,1,0:T(8,128)S(1)} collective-permute-done((f32[3,8,1024]{2,1,0:T(8,128)S(1)}, f32[3,8,1024]{2,1,0:T(8,128)S(1)}, u32[]{:S(2)}, u32[]{:S(2)}) %collective-permute-start.3) | collective-permute-done | bytes 98336 | tf_op jit(solution)/shard_map/ppermute | solution.py:275
  15.7 0.9 collective-permute-done.2.hw.uw
  16.6 23.9 %apply.3 = (f32[8,1024]{1,0:T(8,128)S(1)}, f32[3,1024]{1,0:T(4,128)S(1)}, f32[3,1024]{1,0:T(4,128)S(1)}) custom-call(f32[3,3]{1,0:T(4,128)S(1)} %copy-done, f32[8,8]{1,0:T(8,128)S(1)} %dynamic-slice_bitcast_fusion.frame, f32[3,8,1024]{2,1,0:T(8,128)S(1)} %pad_maximum_fusion.hm.um, f32[3,8,1024]{2,1,0:T(8,128)S(1)} %collective-permute-done.2.hw.uw, ...), custom_call_target="tpu_custom_call" | custom-call | flops 1000000000 | bytes 1048576 | tf_op jit(solution)/shard_map/apply/pallas_call | solution.py:348
  40.6 2.9 %collective-permute-start.4 = (f32[8,1024]{1,0:T(8,128)S(1)}, f32[8,1024]{1,0:T(8,128)S(1)}, u32[]{:S(2)}, u32[]{:S(2)}) collective-permute-start(f32[8,1024]{1,0:T(8,128)S(1)} %get-tuple-element.17), channel_id=1, source_target_pairs={{0,16},{16,32},{32,48},{48,64},{64,80},{80,96},{96,112},{112,128},... | collective-permute-start | bytes 98312 | tf_op jit(solution)/shard_map/ppermute | solution.py:275
  43.5 1.6 %collective-permute-done.5 = f32[8,1024]{1,0:T(8,128)S(1)} collective-permute-done((f32[8,1024]{1,0:T(8,128)S(1)}, f32[8,1024]{1,0:T(8,128)S(1)}, u32[]{:S(2)}, u32[]{:S(2)}) %collective-permute-start.5) | collective-permute-done | bytes 32800 | tf_op jit(solution)/shard_map/ppermute | solution.py:275
  45.2 1.5 %collective-permute-start.6 = (f32[3,8,1024]{2,1,0:T(8,128)S(1)}, f32[3,8,1024]{2,1,0:T(8,128)S(1)}, u32[]{:S(2)}, u32[]{:S(2)}) collective-permute-start(f32[3,8,1024]{2,1,0:T(8,128)S(1)} %pad_maximum_fusion.1.um), channel_id=1, source_target_pairs={{0,1},{1,2},{2,3},{3,4},{4,5},{5,6},{6,7},{7,8},{8,9},{9,10},{10,1... | collective-permute-start | bytes 294920 | tf_op jit(solution)/shard_map/ppermute | solution.py:275
  46.7 1.9 %collective-permute-done.7.ue = f32[3,8,1024]{2,1,0:T(8,128)S(1)} collective-permute-done((f32[3,8,1024]{2,1,0:T(8,128)S(1)}, f32[3,8,1024]{2,1,0:T(8,128)S(1)}, u32[]{:S(2)}, u32[]{:S(2)}) %collective-permute-start.7) | collective-permute-done | bytes 98336 | tf_op jit(solution)/shard_map/ppermute | solution.py:275
  48.7 0.1 collective-permute-done.6.uw
  48.7 23.9 %apply.4 = (f32[8,1024]{1,0:T(8,128)S(1)}, f32[3,1024]{1,0:T(4,128)S(1)}, f32[3,1024]{1,0:T(4,128)S(1)}) custom-call(f32[3,3]{1,0:T(4,128)S(1)} %copy-done, f32[8,8]{1,0:T(8,128)S(1)} %dynamic-slice_bitcast_fusion.frame, f32[3,8,1024]{2,1,0:T(8,128)S(1)} %pad_maximum_fusion.hm.um, f32[3,8,1024]{2,1,0:T(8,128)S(1)} %collective-permute-done.2.hw.uw, ...), custom_call_target="tpu_custom_call" | custom-call | flops 1000000000 | bytes 1048576 | tf_op jit(solution)/shard_map/apply/pallas_call | solution.py:350
  72.7 2.9 %collective-permute-start.8 = (f32[8,1024]{1,0:T(8,128)S(1)}, f32[8,1024]{1,0:T(8,128)S(1)}, u32[]{:S(2)}, u32[]{:S(2)}) collective-permute-start(f32[8,1024]{1,0:T(8,128)S(1)} %get-tuple-element.21), channel_id=1, source_target_pairs={{0,16},{16,32},{32,48},{48,64},{64,80},{80,96},{96,112},{112,128},... | collective-permute-start | bytes 98312 | tf_op jit(solution)/shard_map/ppermute | solution.py:275
  75.8 1.5 %collective-permute-done.9 = f32[8,1024]{1,0:T(8,128)S(1)} collective-permute-done((f32[8,1024]{1,0:T(8,128)S(1)}, f32[8,1024]{1,0:T(8,128)S(1)}, u32[]{:S(2)}, u32[]{:S(2)}) %collective-permute-start.9) | collective-permute-done | bytes 32800 | tf_op jit(solution)/shard_map/ppermute | solution.py:275
  77.4 1.5 %collective-permute-start.10 = (f32[3,8,1024]{2,1,0:T(8,128)S(1)}, f32[3,8,1024]{2,1,0:T(8,128)S(1)}, u32[]{:S(2)}, u32[]{:S(2)}) collective-permute-start(f32[3,8,1024]{2,1,0:T(8,128)S(1)} %pad_maximum_fusion.2.um.xm), channel_id=1, source_target_pairs={{0,1},{1,2},{2,3},{3,4},{4,5},{5,6},{6,7},{7,8},{8,9},{9,10},{10,1... | collective-permute-start | bytes 294920 | tf_op jit(solution)/shard_map/ppermute | solution.py:275
  78.8 2.0 %collective-permute-done.11.ue.xe = f32[3,8,1024]{2,1,0:T(8,128)S(1)} collective-permute-done((f32[3,8,1024]{2,1,0:T(8,128)S(1)}, f32[3,8,1024]{2,1,0:T(8,128)S(1)}, u32[]{:S(2)}, u32[]{:S(2)}) %collective-permute-start.11) | collective-permute-done | bytes 98336 | tf_op jit(solution)/shard_map/ppermute | solution.py:275
  80.8 0.1 collective-permute-done.10.uw.xw
  80.9 24.6 %apply.5 = (f32[8,1024]{1,0:T(8,128)}, f32[3,1024]{1,0:T(4,128)S(1)}, f32[3,1024]{1,0:T(4,128)}) custom-call(f32[3,3]{1,0:T(4,128)S(1)} %copy-done, f32[8,8]{1,0:T(8,128)S(1)} %dynamic-slice_bitcast_fusion.frame, f32[3,8,1024]{2,1,0:T(8,128)S(1)} %pad_maximum_fusion.hm.um, f32[3,8,1024]{2,1,0:T(8,128)S(1)} %collective-permute-done.2.hw.uw, ...), custom_call_target="tpu_custom_call" | custom-call | flops 1000000000 | bytes 1048576 | tf_op jit(solution)/shard_map/apply/pallas_call | solution.py:352
  105.5 0.2 gram.1
  105.7 0.7 broadcast_in_dim.2
  106.4 17.5 %all-to-all-start = ((f32[256,1,16]{2,1,0:T(1,128)}), f32[256,1,16]{2,1,0:T(1,128)S(1)}, u32[]{:S(2)}, u32[]{:S(2)}) async-start(f32[256,1,16]{2,1,0:T(1,128)} %broadcast_in_dim.2), calls=%async_computation | async-start | bytes 262144 | tf_op jit(solution)/shard_map/all_to_all | solution.py:355
  123.9 19.0 %grid.1 = (f32[3,3,512]{2,1,0:T(4,128)S(1)}, f32[2,3,1024]{2,1,0:T(4,128)S(1)}) custom-call(f32[3,3]{1,0:T(4,128)S(1)} %copy-done, f32[8,8]{1,0:T(8,128)S(1)} %dynamic-slice_bitcast_fusion.frame, f32[3,512]{1,0:T(4,128)S(1)} %pad_maximum_fusion.3.gpos, f32[3,8,1024]{2,1,0:T(8,128)S(1)} %pad_maximum_fusion.hm.um, ...), custom_call_target="tpu_custom_call" | custom-call | flops 1000000000 | bytes 1048576 | tf_op jit(solution)/shard_map/grid/pallas_call | solution.py:365
  142.9 0.2 final.1
  143.1 0.6 copy.24
  143.7 0.6 copy.25
  (30 shorter events, 0.5 us)
Async XLA Ops:
  0.6 0.7 copy-start.1
  1.3 0.7 copy-start.2
  2.0 0.7 copy-start.3
  2.8 0.7 copy-start.4
  6.3 5.0 %collective-permute-start.1 = (f32[8,1024]{1,0:T(8,128)S(1)}, f32[8,1024]{1,0:T(8,128)S(1)}, u32[]{:S(2)}, u32[]{:S(2)}) collective-permute-start(f32[8,1024]{1,0:T(8,128)S(1)} %get-tuple-element.15), channel_id=1, source_target_pairs={{0,240},{16,0},{32,16},{48,32},{64,48},{80,64},{96,80},{112,96},{1... | collective-permute-start | bytes 98312 | tf_op jit(solution)/shard_map/ppermute | solution.py:275
  7.0 4.3 %collective-permute-start = (f32[8,1024]{1,0:T(8,128)S(1)}, f32[8,1024]{1,0:T(8,128)S(1)}, u32[]{:S(2)}, u32[]{:S(2)}) collective-permute-start(f32[8,1024]{1,0:T(8,128)S(1)} %get-tuple-element.15), channel_id=1, source_target_pairs={{0,16},{16,32},{32,48},{48,64},{64,80},{80,96},{96,112},{112,128},... | collective-permute-start | bytes 98312 | tf_op jit(solution)/shard_map/ppermute | solution.py:275
  11.3 4.4 %collective-permute-start.3 = (f32[3,8,1024]{2,1,0:T(8,128)S(1)}, f32[3,8,1024]{2,1,0:T(8,128)S(1)}, u32[]{:S(2)}, u32[]{:S(2)}) collective-permute-start(f32[3,8,1024]{2,1,0:T(8,128)S(1)} %pad_maximum_fusion.hm.um), channel_id=1, source_target_pairs={{0,15},{1,0},{2,1},{3,2},{4,3},{5,4},{6,5},{7,6},{8,7},{9,8},{10,9... | collective-permute-start | bytes 294920 | tf_op jit(solution)/shard_map/ppermute | solution.py:275
  11.7 4.9 %collective-permute-start.2 = (f32[3,8,1024]{2,1,0:T(8,128)S(1)}, f32[3,8,1024]{2,1,0:T(8,128)S(1)}, u32[]{:S(2)}, u32[]{:S(2)}) collective-permute-start(f32[3,8,1024]{2,1,0:T(8,128)S(1)} %pad_maximum_fusion.hm.um), channel_id=1, source_target_pairs={{0,1},{1,2},{2,3},{3,4},{4,5},{5,6},{6,7},{7,8},{8,9},{9,10},{10,1... | collective-permute-start | bytes 294920 | tf_op jit(solution)/shard_map/ppermute | solution.py:275
  12.9 3.7 %copy-start = (f32[3,3]{1,0:T(4,128)S(1)}, f32[3,3]{1,0:T(4,128)}, u32[]{:S(2)}) copy-start(f32[3,3]{1,0:T(4,128)} %corr.7) | copy-start | bytes 112
  40.5 4.6 %collective-permute-start.5 = (f32[8,1024]{1,0:T(8,128)S(1)}, f32[8,1024]{1,0:T(8,128)S(1)}, u32[]{:S(2)}, u32[]{:S(2)}) collective-permute-start(f32[8,1024]{1,0:T(8,128)S(1)} %get-tuple-element.17), channel_id=1, source_target_pairs={{0,240},{16,0},{32,16},{48,32},{64,48},{80,64},{96,80},{112,96},{1... | collective-permute-start | bytes 98312 | tf_op jit(solution)/shard_map/ppermute | solution.py:275
  40.6 4.5 %collective-permute-start.4 = (f32[8,1024]{1,0:T(8,128)S(1)}, f32[8,1024]{1,0:T(8,128)S(1)}, u32[]{:S(2)}, u32[]{:S(2)}) collective-permute-start(f32[8,1024]{1,0:T(8,128)S(1)} %get-tuple-element.17), channel_id=1, source_target_pairs={{0,16},{16,32},{32,48},{48,64},{64,80},{80,96},{96,112},{112,128},... | collective-permute-start | bytes 98312 | tf_op jit(solution)/shard_map/ppermute | solution.py:275
  45.1 3.5 %collective-permute-start.7 = (f32[3,8,1024]{2,1,0:T(8,128)S(1)}, f32[3,8,1024]{2,1,0:T(8,128)S(1)}, u32[]{:S(2)}, u32[]{:S(2)}) collective-permute-start(f32[3,8,1024]{2,1,0:T(8,128)S(1)} %pad_maximum_fusion.1.um), channel_id=1, source_target_pairs={{0,15},{1,0},{2,1},{3,2},{4,3},{5,4},{6,5},{7,6},{8,7},{9,8},{10,9... | collective-permute-start | bytes 294920 | tf_op jit(solution)/shard_map/ppermute | solution.py:275
  45.2 3.5 %collective-permute-start.6 = (f32[3,8,1024]{2,1,0:T(8,128)S(1)}, f32[3,8,1024]{2,1,0:T(8,128)S(1)}, u32[]{:S(2)}, u32[]{:S(2)}) collective-permute-start(f32[3,8,1024]{2,1,0:T(8,128)S(1)} %pad_maximum_fusion.1.um), channel_id=1, source_target_pairs={{0,1},{1,2},{2,3},{3,4},{4,5},{5,6},{6,7},{7,8},{8,9},{9,10},{10,1... | collective-permute-start | bytes 294920 | tf_op jit(solution)/shard_map/ppermute | solution.py:275
  48.7 27.0 %copy-start.5 = (f32[1,1,3,512]{3,1,2,0:T(1,128)S(1)}, f32[1,1,3,512]{3,1,2,0:T(1,128)}, u32[]{:S(2)}) copy-start(f32[1,1,3,512]{3,1,2,0:T(1,128)} %param.14) | copy-start | bytes 18436
  72.7 4.6 %collective-permute-start.9 = (f32[8,1024]{1,0:T(8,128)S(1)}, f32[8,1024]{1,0:T(8,128)S(1)}, u32[]{:S(2)}, u32[]{:S(2)}) collective-permute-start(f32[8,1024]{1,0:T(8,128)S(1)} %get-tuple-element.21), channel_id=1, source_target_pairs={{0,240},{16,0},{32,16},{48,32},{64,48},{80,64},{96,80},{112,96},{1... | collective-permute-start | bytes 98312 | tf_op jit(solution)/shard_map/ppermute | solution.py:275
  72.7 4.5 %collective-permute-start.8 = (f32[8,1024]{1,0:T(8,128)S(1)}, f32[8,1024]{1,0:T(8,128)S(1)}, u32[]{:S(2)}, u32[]{:S(2)}) collective-permute-start(f32[8,1024]{1,0:T(8,128)S(1)} %get-tuple-element.21), channel_id=1, source_target_pairs={{0,16},{16,32},{32,48},{48,64},{64,80},{80,96},{96,112},{112,128},... | collective-permute-start | bytes 98312 | tf_op jit(solution)/shard_map/ppermute | solution.py:275
  77.3 3.5 %collective-permute-start.11 = (f32[3,8,1024]{2,1,0:T(8,128)S(1)}, f32[3,8,1024]{2,1,0:T(8,128)S(1)}, u32[]{:S(2)}, u32[]{:S(2)}) collective-permute-start(f32[3,8,1024]{2,1,0:T(8,128)S(1)} %pad_maximum_fusion.2.um.xm), channel_id=1, source_target_pairs={{0,15},{1,0},{2,1},{3,2},{4,3},{5,4},{6,5},{7,6},{8,7},{9,8},{10,9... | collective-permute-start | bytes 294920 | tf_op jit(solution)/shard_map/ppermute | solution.py:275
  77.4 3.6 %collective-permute-start.10 = (f32[3,8,1024]{2,1,0:T(8,128)S(1)}, f32[3,8,1024]{2,1,0:T(8,128)S(1)}, u32[]{:S(2)}, u32[]{:S(2)}) collective-permute-start(f32[3,8,1024]{2,1,0:T(8,128)S(1)} %pad_maximum_fusion.2.um.xm), channel_id=1, source_target_pairs={{0,1},{1,2},{2,3},{3,4},{4,5},{5,6},{6,7},{7,8},{8,9},{9,10},{10,1... | collective-permute-start | bytes 294920 | tf_op jit(solution)/shard_map/ppermute | solution.py:275
  106.4 36.5 %all-to-all-start = ((f32[256,1,16]{2,1,0:T(1,128)}), f32[256,1,16]{2,1,0:T(1,128)S(1)}, u32[]{:S(2)}, u32[]{:S(2)}) async-start(f32[256,1,16]{2,1,0:T(1,128)} %broadcast_in_dim.2), calls=%async_computation | async-start | bytes 262144 | tf_op jit(solution)/shard_map/all_to_all | solution.py:355

commit v2 on v1

v2 whole, which is shorter than its diff:
```python
import functools
import math

import jax
import jax.numpy as jnp
import numpy as np
from jax import lax
from jax.experimental import pallas as pl
from jax.experimental.pallas import tpu as pltpu
from jax.sharding import PartitionSpec as P

OBS_TILE = 512
GRID_ROWS = 16
BLK = 128
SHIFT = 0.5
FAR = 64.0
NT = (((1,), (1,)), ((), ()))
NN = (((1,), (0,)), ((), ()))
F32 = jnp.float32
BF16 = jnp.bfloat16
VLIM = 8 * 1024 * 1024
UNROLL = 8
ROWS = 32
GROUP = 4
KEPT = 96
CELLS = 512


def split3(x):
    hi = x.astype(BF16)
    rest = x - hi.astype(F32)
    mid = rest.astype(BF16)
    low = (rest - mid.astype(F32)).astype(BF16)
    return jnp.concatenate([hi, mid, low], axis=0)


def col_of(row):
    return jnp.transpose(jnp.broadcast_to(row, (8, row.shape[1])))[:, 0:1]


def rank_of(key, slots):
    col = col_of(key)
    parts = []
    for j in range(slots // BLK):
        kj = key[:, j * BLK : (j + 1) * BLK]
        total = jnp.zeros((8, BLK), F32)
        for i in range(slots // BLK):
            ki = jnp.broadcast_to(col[i * BLK : (i + 1) * BLK, :], (BLK, BLK))
            if i < j:
                before = ki <= kj
            elif i > j:
                before = ki < kj
            else:
                first = lax.broadcasted_iota(jnp.int32, (BLK, BLK), 0) < lax.broadcasted_iota(
                    jnp.int32, (BLK, BLK), 1
                )
                before = (ki < kj) | ((ki == kj) & first)
            ones = jnp.where(before, 1.0, 0.0).astype(F32)
            total = total + jnp.sum(ones.reshape(BLK // 8, 8, BLK), axis=0)
        parts.append(jnp.sum(total, axis=0, keepdims=True))
    return jnp.concatenate(parts, axis=1)


def onehot_of(rank, slots):
    place = lax.broadcasted_iota(jnp.int32, (slots, slots), 0).astype(F32)
    return jnp.where(place == rank, 1.0, 0.0).astype(BF16)


def angle_of(x):
    x2 = x * x
    return x * (1.0 + x2 * (1.0 / 6.0 + x2 * (3.0 / 40.0 + x2 * (15.0 / 336.0))))


def sort_kernel(
    count, table, pos_in, innov_in, bg_in, std_in,
    hb_out, dev_out, var_out, b0_out, rank_out, frame_out, bounds_out,
    pos, innov, bg, std, sems,
):
    bands, sectors = lax.axis_size("lat"), lax.axis_size("lon")
    band, sector = lax.axis_index("lat"), lax.axis_index("lon")
    pairs = [
        (table.at[band, sector], frame_out),
        (pos_in, pos),
        (innov_in, innov),
        (bg_in, bg),
        (std_in, std),
    ]
    copies = [pltpu.make_async_copy(x, y, sems.at[k]) for k, (x, y) in enumerate(pairs)]
    for copy in copies:
        copy.start()
    for copy in copies:
        copy.wait()

    def rows(ref):
        return jnp.concatenate([ref[0], ref[1], ref[2]], axis=0)

    slots = pos.shape[2]
    per = slots // BLK
    frame = frame_out[...]
    live_n = count[0, 0] * OBS_TILE
    lane = lax.broadcasted_iota(jnp.int32, (1, slots), 1)
    live = lane < live_n
    px, py, pz = pos[0], pos[1], pos[2]
    key = jnp.where(live, pz, 10.0)
    first = rank_of(key, slots)
    strip = jnp.where(first * 2.0 >= live_n.astype(F32), 8.0, 0.0)
    east = frame[2:3, 6:7] * px + frame[3:4, 6:7] * py
    sine = east * lax.rsqrt(jnp.maximum(px * px + py * py, 1e-6))
    rank = rank_of(jnp.where(live, strip + sine, 100.0), slots)
    rank_out[...] = rank
    maskf = jnp.where(live, 1.0, 0.0).astype(F32)
    where3 = jnp.where(live, rows(pos), FAR)
    dev = rows(bg) * maskf
    start = rows(innov) * maskf
    var = rows(std)
    var = var * var * maskf
    sine = jnp.where(live, sine, 0.0)
    vals = jnp.concatenate([where3, dev, start, var, sine, jnp.zeros((3, slots), F32)], axis=0)
    got = lax.dot_general(split3(vals), onehot_of(rank, slots), NT, preferred_element_type=F32)
    got = got[0:16] + got[16:32] + got[32:48]
    dev, start = got[3:6], got[6:9]
    dev_out[...] = dev
    b0_out[...] = start
    var_out[...] = got[9:12]

    z = jnp.concatenate(blocks(got[2:3]), axis=0)
    angle = angle_of(jnp.concatenate(blocks(got[12:13]), axis=0))
    bounds = [
        jnp.min(z, axis=1, keepdims=True),
        jnp.max(z, axis=1, keepdims=True),
        jnp.min(angle, axis=1, keepdims=True),
        jnp.max(angle, axis=1, keepdims=True),
    ]
    sub = lax.broadcasted_iota(jnp.int32, (per, BLK), 0)
    col = lax.broadcasted_iota(jnp.int32, (per, BLK), 1)

    def spread(x, index):
        return jnp.sum(jnp.where(sub == index, x, 0.0), axis=0, keepdims=True)

    as_source = [spread(x, col & 7) for x in bounds]
    pad = jnp.zeros((1, slots - 4 * BLK), F32)
    hb_out[...] = jnp.concatenate(
        [dev * start, got[0:3], jnp.concatenate(as_source + [pad], axis=1), jnp.zeros((1, slots), F32)],
        axis=0,
    )
    as_target = [spread(x, col >> 3) for x in bounds]
    lane = lax.broadcasted_iota(jnp.int32, (1, BLK), 1)
    t = ((lane - 64) >> 3).astype(F32)
    tall = 1.0 * BLK * GRID_ROWS / CELLS
    floor = -0.9 + 1.8 * band.astype(F32) / bands
    step = 1.8 / bands / GRID_ROWS
    half_width = math.pi / sectors
    grid = [
        floor + step * (t * tall + 0.25),
        floor + step * (t * tall + tall - 0.25),
        jnp.full((1, BLK), -half_width, F32),
        jnp.full((1, BLK), half_width, F32),
    ]
    grid_end = 64 + 8 * (CELLS // BLK)
    rows = [
        jnp.where(lane < 64, x, jnp.where(lane < grid_end, g, 100.0)) for x, g in zip(as_target, grid)
    ]
    bounds_out[...] = jnp.concatenate(rows + [jnp.zeros((4, BLK), F32)], axis=0)


def blocks(wide):
    return [wide[:, b * BLK : (b + 1) * BLK] for b in range(wide.shape[1] // BLK)]


def active_words(source, target, bands):
    slo, shi, wlo, whi = source
    tlo, thi, vlo, vhi = target

    def radius(z):
        return jnp.sqrt(jnp.maximum(1.0 - z * z, 0.0))

    below, above = jnp.minimum(shi, thi), jnp.maximum(slo, tlo)
    fall = radius(below) - radius(above)
    apart = above - below
    lat = jnp.where(apart > 0.0, apart * apart + fall * fall, 0.0)
    gap = jnp.maximum(jnp.maximum(wlo, vlo) - jnp.minimum(whi, vhi), 0.0)
    gap2 = gap * gap
    small = radius(jnp.maximum(jnp.abs(slo), jnp.abs(shi))) * radius(
        jnp.maximum(jnp.abs(tlo), jnp.abs(thi))
    )
    bound = lat + gap2 * (1.0 - gap2 * (1.0 / 12.0)) * small
    reach = (0.6 / bands) ** 2
    lane = lax.broadcasted_iota(jnp.int32, bound.shape, 1)
    active = (bound < reach * 1.002 + 1e-6) & (tlo < 50.0)
    word = jnp.where(active, jnp.left_shift(jnp.full(lane.shape, 1, jnp.int32), (lane >> 3) & 7), 0)
    for shift in (8, 16, 32):
        word = word + pltpu.roll(word, BLK - shift, 1)
    return word


def source_bounds(tiles, shifts):
    rows = []
    for k in range(4):
        parts = []
        for tile, shift in zip(tiles, shifts):
            row = tile[6:7, k * BLK : (k + 1) * BLK]
            parts.append(row + shift if k >= 2 else row)
        rows.append(jnp.concatenate(parts, axis=0))
    return rows


def to_smem(words, mask_v, mask_s, sem):
    mask_v[0 : words.shape[0], :] = words
    copy = pltpu.make_async_copy(mask_v, mask_s, sem)
    copy.start()
    copy.wait()


def list_pairs(mask_s, column, regions, first, pairs, count, below=False):
    def source(i, count):
        r, b = i >> 3, i & 7

        def take(state):
            word, k = state
            bit = word & -word
            pairs[0, k] = (first * 8 + i) * 8 + (31 - lax.clz(bit))
            return word ^ bit, k + 1

        word = mask_s[r, column + b]
        if below:
            word = word & (jnp.left_shift(1, b) - 1)
        return lax.while_loop(lambda state: state[0] != 0, take, (word, count))[1]

    return lax.fori_loop(0, 8 * regions, source, count)


def close_list(pairs, count):
    for k in range(UNROLL):
        pairs[0, count + k] = 0
    pairs[0, pairs.shape[1] - 1] = count


def rho_of(tcol, sx, sy, sz):
    dx, dy, dz = tcol[0] - sx, tcol[1] - sy, tcol[2] - sz
    s = dx * dx + dy * dy + dz * dz
    r = lax.rsqrt(jnp.maximum(s, 1e-30))
    z = s * r
    inner = s * (((-0.25 * z + 0.5) * z + 0.625) * z - 5.0 / 3.0) + 1.0
    t = jnp.maximum(2.0 - z, 0.0)
    t = t * t
    u = z + 1.0
    outer = (t * t) * (u * u * (1.0 / 12.0) - 0.125) * r
    return jnp.where(s <= 1.0, inner, outer)


def to_frame(tile, row, frame):
    q = None
    for k in range(3):
        term = frame[:, k : k + 1] * (tile[row + k : row + k + 1, :] - frame[:, 3 + k : 4 + k])
        q = term if q is None else q + term
    return q


def set_columns(targets, tcol):
    for t, tile in enumerate(targets):
        turned = jnp.transpose(tile)
        for k in range(3):
            tcol[t, k] = jnp.broadcast_to(turned[:, k : k + 1], (BLK, BLK))


def fill_rows(q, tcol, t, out):
    sx, sy, sz = q[0:1], q[1:2], q[2:3]
    for i in range(0, BLK, ROWS):
        rho = rho_of([tcol[t, k, i : i + ROWS] for k in range(3)], sx, sy, sz)
        hi = rho.astype(BF16)
        out[i : i + ROWS, 0:BLK] = hi
        out[i : i + ROWS, BLK : 2 * BLK] = (rho - hi.astype(F32)).astype(BF16)


def fill_pair(entry, q_ref, tcol, out):
    fill_rows(q_ref[entry >> 3], tcol, entry & 7, out)


def fill_cache(count, pairs, q_ref, tcol, cache, first):
    room = cache.shape[0] - UNROLL - first
    kept = jnp.minimum(count, room)

    def fill(p, _):
        fill_pair(pairs[0, p], q_ref, tcol, cache.at[first + p])
        return 0

    lax.fori_loop(0, kept, fill, 0)
    for k in range(UNROLL):
        cache[first + kept + k] = jnp.zeros(cache.shape[1:], BF16)


def parts_of(tile):
    hi = tile.astype(BF16).astype(F32)
    rest = tile - hi
    mid = rest.astype(BF16).astype(F32)
    return [hi, mid, rest - mid]


def set_values(tile, v_ref, first):
    v = jnp.concatenate(parts_of(tile) + [jnp.zeros(tile.shape, F32)], axis=0).astype(BF16)
    for b, part in enumerate(blocks(v)):
        v_ref[first + b, :, 0:BLK] = part
        v_ref[first + b, :, BLK : 2 * BLK] = part


def add_parts(out):
    return out[0:8] + out[8:16] + out[16:24]


def own_fill_kernel(frame, hb, bounds, q_out, tcol_out, pairs_out, cache_out, mask_v, mask_s, sem):
    tile = hb[...]
    tiles = blocks(to_frame(tile, 3, frame[...]))
    per = len(tiles)
    for b, part in enumerate(tiles):
        q_out[b] = part
    words = active_words(
        source_bounds([tile], [0.0]), [bounds[k : k + 1, :] for k in range(4)], lax.axis_size("lat")
    )
    mask_v[0:1, :] = words
    copy = pltpu.make_async_copy(mask_v, mask_s, sem)
    copy.start()
    set_columns(tiles, tcol_out)
    copy.wait()
    count = list_pairs(mask_s, 0, 1, 0, pairs_out, 0, below=True)
    close_list(pairs_out, count)

    def diagonal(b, _):
        fill_pair(b * 9, q_out, tcol_out, cache_out.at[b])
        return 0

    lax.fori_loop(0, per, diagonal, 0)
    fill_cache(count, pairs_out, q_out, tcol_out, cache_out, per)


def own_times_kernel(pairs, cache, u, acc, v_ref):
    set_values(u[...], v_ref, 0)
    per = acc.shape[0]
    for b in range(per):
        acc[b] = add_parts(lax.dot_general(v_ref[b], cache[b], NT, preferred_element_type=F32))
    count = pairs[0, pairs.shape[1] - 1]

    def group(i, _):
        outs = []
        for k in range(UNROLL // 2):
            p = i * (UNROLL // 2) + k
            n, t = pairs[0, p] >> 3, pairs[0, p] & 7
            rho = cache[per + p]
            ahead = lax.dot_general(v_ref[n], rho, NT, preferred_element_type=F32)
            back = lax.dot_general(v_ref[t, :, 0:BLK], rho, NN, preferred_element_type=F32)
            outs.append((ahead, back[:, 0:BLK] + back[:, BLK : 2 * BLK]))
        for k in range(UNROLL // 2):
            p = i * (UNROLL // 2) + k
            n, t = pairs[0, p] >> 3, pairs[0, p] & 7
            acc[t] += add_parts(outs[k][0])
            acc[n] += add_parts(outs[k][1])
        return 0

    half = UNROLL // 2
    lax.fori_loop(0, (count + half - 1) // half, group, 0)


OTHERS = [(0, 0), (0, 2), (1, 0), (1, 1), (1, 2), (2, 0), (2, 1), (2, 2)]


def near_fill_kernel(
    frame, bounds, tcol, hm, hw, he, q_out, pairs_out, cells_out, cache_out, mask_v, mask_s, sem
):
    halo = (hm, hw, he)
    per = hm.shape[2] // BLK
    turn = 2.0 * math.pi / lax.axis_size("lon")
    where = [(0, 1)] + OTHERS
    tiles = [halo[c][a] for c, a in where]
    words = active_words(
        source_bounds(tiles, [(0.0, -turn, turn)[c] for c, a in where]),
        [bounds[k : k + 1, :] for k in range(4)],
        lax.axis_size("lat"),
    )
    mask_v[0 : len(where), :] = words
    copy = pltpu.make_async_copy(mask_v, mask_s, sem)
    copy.start()
    turned = frame[...]
    for r in range(1, len(where)):
        for b, part in enumerate(blocks(to_frame(tiles[r], 3, turned))):
            q_out[(r - 1) * per + b] = part
    copy.wait()
    count = list_pairs(mask_s.at[1 : len(where)], 0, len(where) - 1, 0, pairs_out, 0)
    close_list(pairs_out, count)
    fill_cache(count, pairs_out, q_out, tcol, cache_out, 0)
    close_list(cells_out, list_pairs(mask_s, 64, len(where), 0, cells_out, 0))


def mix(corr, total):
    out = None
    for c in range(3):
        term = corr[:, c : c + 1] * total[c : c + 1, :]
        out = term if out is None else out + term
    return out


def near_times_kernel(
    pairs, corr, cache, q_ref, tcol, acc_own, um, uw, ue, dev, var, field,
    u_out, img_out, nxt_out, v_ref, acc, pair,
):
    halo = (um, uw, ue)
    per = acc.shape[0]
    for k, (c, a) in enumerate(OTHERS):
        set_values(halo[c][a], v_ref, k * per)
    acc[...] = acc_own[...]
    count = pairs[0, pairs.shape[1] - 1]
    kept = jnp.minimum(count, cache.shape[0] - UNROLL)

    def group(i, _):
        outs = []
        for k in range(UNROLL):
            p = i * UNROLL + k
            n = pairs[0, p] >> 3
            outs.append(lax.dot_general(v_ref[n], cache[p], NT, preferred_element_type=F32))
        for k in range(UNROLL):
            acc[pairs[0, i * UNROLL + k] & 7] += add_parts(outs[k])
        return 0

    lax.fori_loop(0, (kept + UNROLL - 1) // UNROLL, group, 0)

    def extra(p, _):
        entry = pairs[0, p]
        fill_pair(entry, q_ref, tcol, pair)
        out = lax.dot_general(v_ref[entry >> 3], pair[...], NT, preferred_element_type=F32)
        acc[entry & 7] += add_parts(out)
        return 0

    lax.fori_loop(kept, count, extra, 0)
    total = jnp.concatenate([acc[t] for t in range(per)], axis=1)
    field = field[...]
    dev = dev[...]
    image = dev * mix(corr, total) + var[...] * field
    nxt = image - SHIFT * field
    img_out[...] = image
    nxt_out[...] = nxt
    u_out[...] = jnp.concatenate([dev * nxt, jnp.zeros((5, nxt.shape[1]), F32)], axis=0)


def gram_kernel(b0, b1, b2, a0, a1, a2, out):
    pairs = [(b0, a0), (b0, a1), (b0, a2), (b1, a1), (b1, a2), (b2, a2), (b0, b0), (b1, b0), (b2, b0)]
    rows = []
    for x, y in pairs:
        prod = blocks(x[...] * y[...])
        while len(prod) > 1:
            prod = [prod[k] + prod[k + 1] for k in range(0, len(prod), 2)]
        rows.append(jnp.sum(prod[0], axis=0, keepdims=True))
    rows.append(jnp.zeros((16 - len(rows), BLK), F32))
    totals = jnp.sum(jnp.concatenate(rows, axis=0), axis=1, keepdims=True)
    sub = lax.broadcasted_iota(jnp.int32, (16, 16), 0)
    col = lax.broadcasted_iota(jnp.int32, (16, 16), 1)
    row = jnp.sum(jnp.where(sub == col, totals, 0.0), axis=0, keepdims=True)
    out[...] = jnp.broadcast_to(row[None], out.shape)


def pack_kernel(q_own, q_near, u0, u1, u2, *refs):
    out = refs[-1]
    fields = [refs[3 * f : 3 * f + 3] for f in range(3)]
    per = q_own.shape[0]
    for f, u in enumerate((u0, u1, u2)):
        for r, (c, a) in enumerate([(0, 1)] + OTHERS):
            tile = u[...] if r == 0 else fields[f][c][a]
            for b, part in enumerate(blocks(tile)):
                out[r * per + b, 3 * f : 3 * f + 3, :] = part[0:3]
    for b in range(per):
        out[b, 9:12, :] = q_own[b, 0:3, :]
    for n in range(q_near.shape[0]):
        out[per + n, 9:12, :] = q_near[n, 0:3, :]
    for n in range(out.shape[0]):
        out[n, 12:16, :] = jnp.zeros((4, BLK), F32)


def grid_kernel(pairs, corr, frame, packed, bgg, g_out, tcol, rho, acc):
    cells = g_out.shape[2]
    columns = cells // GRID_ROWS
    bands, sectors = lax.axis_size("lat"), lax.axis_size("lon")
    cell = lax.broadcasted_iota(jnp.int32, (8, cells), 1)
    row = lax.broadcasted_iota(jnp.int32, (8, cells), 0)
    frac_lat = ((cell // columns).astype(F32) + 0.5) / GRID_ROWS
    frac_lon = ((cell % columns).astype(F32) + 0.5) / columns
    band, sector = frame[0:1, 6:7], frame[1:2, 6:7]
    sinlat = -0.9 + 1.8 * (band + frac_lat) / bands
    longitude = 2.0 * math.pi * (sector + frac_lon) / sectors
    coslat = jnp.sqrt(1.0 - sinlat * sinlat)
    point = jnp.where(row == 0, coslat * jnp.cos(longitude), coslat * jnp.sin(longitude))
    point = jnp.where(row == 2, sinlat, point)
    set_columns(blocks(to_frame(point, 0, frame[...])), tcol)
    acc[...] = jnp.zeros(acc.shape, F32)
    count = pairs[0, pairs.shape[1] - 1]

    def group(i, _):
        outs = []
        for k in range(GROUP):
            p = i * GROUP + k
            entry = pairs[0, p]
            near = packed[entry >> 3]
            fill_rows(near[9:12], tcol, entry & 7, rho.at[k])
            near = near * jnp.where(p < count, 1.0, 0.0).astype(F32)
            v = jnp.concatenate(parts_of(near), axis=0).astype(BF16)
            v = jnp.concatenate([v, v], axis=1)
            outs.append(lax.dot_general(v, rho[k], NT, preferred_element_type=F32))
        for k in range(GROUP):
            out = outs[k]
            acc[pairs[0, i * GROUP + k] & 7] += out[0:16] + out[16:32] + out[32:48]
        return 0

    lax.fori_loop(0, (count + GROUP - 1) // GROUP, group, 0)
    total = jnp.concatenate([acc[t] for t in range(acc.shape[0])], axis=1)
    dev = jnp.concatenate([bgg[0], bgg[1], bgg[2]], axis=0)
    for f in range(3):
        g_out[f] = dev * mix(corr, total[3 * f : 3 * f + 3])


def unsort_kernel(rank, b1, b2, w_out):
    slots = rank.shape[1]
    vals = jnp.concatenate([b1[...], b2[...], jnp.zeros((10, slots), F32)], axis=0)
    back = lax.dot_general(split3(vals), onehot_of(rank[...], slots), NN, preferred_element_type=F32)
    back = back[0:16] + back[16:32] + back[32:48]
    w_out[0] = back[0:3]
    w_out[1] = back[3:6]


def final_kernel(count, parts, innov, w, g, w_out, g_out, w_buf, g_buf, sems):
    sums = parts[...]
    while sums.shape[0] > 1:
        half = sums.shape[0] // 2
        sums = sums[:half] + sums[half:]
    sums = sums[0]
    lane = lax.broadcasted_iota(jnp.int32, sums.shape, 1)
    m00, m01, m02, m11, m12, m22, g0, g1, g2 = [
        jnp.sum(jnp.where(lane == k, sums, 0.0), axis=1, keepdims=True) for k in range(9)
    ]
    l10, l20 = m01 / m00, m02 / m00
    d1 = m11 - l10 * m01
    e12 = m12 - l10 * m02
    ok1 = d1 > 1e-6 * m11
    safe1 = jnp.where(ok1, d1, 1.0)
    l21 = jnp.where(ok1, e12 / safe1, 0.0)
    d2 = m22 - l20 * m02 - l21 * e12
    ok2 = ok1 & (d2 > 1e-6 * m22)
    y1 = g1 - l10 * g0
    y2 = g2 - l20 * g0 - l21 * y1
    c2 = jnp.where(ok2, y2 / jnp.where(ok2, d2, 1.0), 0.0)
    c1 = jnp.where(ok1, y1 / safe1, 0.0) - l21 * c2
    c0 = g0 / m00 - l10 * c1 - l20 * c2
    slots = innov.shape[2]
    live = lax.broadcasted_iota(jnp.int32, (1, slots), 1) < count[0, 0] * OBS_TILE
    for k in range(3):
        first = jnp.where(live, innov[k], 0.0)
        w_buf[k] = c0 * first + c1 * w[0, k : k + 1] + c2 * w[1, k : k + 1]
        g_buf[k] = c0 * g[0, k : k + 1] + c1 * g[1, k : k + 1] + c2 * g[2, k : k + 1]
    copies = [
        pltpu.make_async_copy(w_buf, w_out, sems.at[0]),
        pltpu.make_async_copy(g_buf, g_out, sems.at[1]),
    ]
    for copy in copies:
        copy.start()
    for copy in copies:
        copy.wait()


def ring(x, axis, step):
    count = lax.axis_size(axis)
    return lax.ppermute(x, axis, [(i, (i + step) % count) for i in range(count)])


def frames(bands, sectors):
    table = np.zeros((bands, sectors, 8, 8), np.float64)
    half = 0.3 / bands
    for i in range(bands):
        s = -0.9 + 1.8 * (i + 0.5) / bands
        c = math.sqrt(1.0 - s * s)
        for j in range(sectors):
            lam = 2.0 * math.pi * (j + 0.5) / sectors
            cl, sl = math.cos(lam), math.sin(lam)
            table[i, j, :3, :3] = np.array([[-sl, cl, 0.0], [-s * cl, -s * sl, c], [c * cl, c * sl, s]]) / half
            table[i, j, :, 3:6] = [c * cl, c * sl, s]
            table[i, j, :4, 6] = [i, j, -sl, cl]
    return table.astype(np.float32)


VM = pl.BlockSpec(memory_space=pltpu.VMEM)
SM = pl.BlockSpec(memory_space=pltpu.SMEM)
HB = pl.BlockSpec(memory_space=pltpu.HBM)
MASKS = [pltpu.VMEM((16, BLK), jnp.int32), pltpu.SMEM((16, BLK), jnp.int32), pltpu.SemaphoreType.DMA]
PAIR = pltpu.VMEM((BLK, 2 * BLK), BF16)


def arr(*shape, dtype=F32):
    return jax.ShapeDtypeStruct(shape, dtype)


def call(kernel, name, ins, outs, scratch, flops, out_specs=None, vmem=VLIM):
    return pl.pallas_call(
        kernel,
        out_shape=outs,
        in_specs=ins,
        out_specs=[VM] * len(outs) if out_specs is None else out_specs,
        scratch_shapes=scratch,
        name=name,
        compiler_params=pltpu.CompilerParams(vmem_limit_bytes=vmem),
        cost_estimate=pl.CostEstimate(flops=flops, bytes_accessed=1 << 20, transcendentals=0),
    )


def tie(first, *rest):
    return lax.optimization_barrier((first, *rest))[0]


def per_device(tile_counts, obs_pos, innovation, bg_std_obs, obs_std, channel_corr, bg_std_grid):
    bands, sectors = lax.axis_size("lat"), lax.axis_size("lon")
    slots = obs_pos.shape[3]
    cells = bg_std_grid.shape[3]
    per = slots // BLK
    grids = cells // BLK
    table = jnp.asarray(frames(bands, sectors))

    def flat(x):
        return x.reshape(3, 1, x.shape[3])

    obs_in = pltpu.VMEM((3, 1, slots), F32)
    three = arr(3, slots)
    hb, dev, var, b0, rank, frame, bounds = call(
        sort_kernel,
        "sort",
        [SM] + [HB] * 5,
        [arr(8, slots), three, three, three, arr(1, slots), arr(8, 8), arr(8, BLK)],
        [obs_in] * 4 + [pltpu.SemaphoreType.DMA((5,))],
        10**8,
        vmem=60 * 1024 * 1024,
    )(tile_counts, table, flat(obs_pos), flat(innovation), flat(bg_std_obs), flat(obs_std))

    def exchange(block, beside, after):
        south, north = ring(block, "lat", 1), ring(block, "lat", -1)
        first = beside()
        mid = tie(jnp.stack([south, block, north]), first)
        west, east = ring(mid, "lon", 1), ring(mid, "lon", -1)
        second = after(first)
        west, east, second = lax.optimization_barrier((west, east, second))
        return (mid, west, east), first, second

    off = per * (per - 1) // 2

    def own_fill():
        return call(
            own_fill_kernel,
            "own_fill",
            [VM] * 3,
            [
                arr(per, 8, BLK),
                arr(per, 3, BLK, BLK),
                arr(1, off + BLK, dtype=jnp.int32),
                arr(per + off + UNROLL, BLK, 2 * BLK, dtype=BF16),
            ],
            MASKS,
            10**9,
            [VM, VM, SM, VM],
        )(frame, hb, bounds)

    def own_times(filled, u):
        return call(
            own_times_kernel,
            "own_times",
            [SM] + [VM] * 2,
            [arr(per, 8, BLK)],
            [pltpu.VMEM((per, 32, 2 * BLK), BF16)],
            10**8,
        )(*filled[2:], u)[0]

    near0, filled, acc = exchange(hb, own_fill, lambda filled: own_times(filled, hb))
    q_own, tcol = filled[:2]
    full = 8 * per * per
    q_near, pairs_near, pairs_cells, cache_near = call(
        near_fill_kernel,
        "near_fill",
        [VM] * 6,
        [
            arr(8 * per, 8, BLK),
            arr(1, full + BLK, dtype=jnp.int32),
            arr(1, 9 * per * (cells // BLK) + BLK, dtype=jnp.int32),
            arr(min(full, KEPT) + UNROLL, BLK, 2 * BLK, dtype=BF16),
        ],
        MASKS,
        10**9,
        [VM, SM, SM, VM],
    )(frame, bounds, tcol, *near0)

    def near_times(halo, acc, field):
        return call(
            near_times_kernel,
            "near_times",
            [SM] + [VM] * 11,
            [arr(8, slots), three, three],
            [pltpu.VMEM((8 * per, 32, 2 * BLK), BF16), pltpu.VMEM((per, 8, BLK), F32), PAIR],
            10**8,
        )(pairs_near, channel_corr, cache_near, q_near, tcol, acc, *halo, dev, var, field)

    u1, a0, b1 = near_times(near0, acc, b0)
    near1, acc, _ = exchange(u1, lambda: own_times(filled, u1), lambda acc: acc)
    u2, a1, b2 = near_times(near1, acc, b1)
    near2, acc, _ = exchange(u2, lambda: own_times(filled, u2), lambda acc: acc)
    _, a2, _ = near_times(near2, acc, b2)
    (packed,) = call(
        pack_kernel, "pack", [VM] * 14, [arr(9 * per, 16, BLK)], [], 10**7
    )(q_own, q_near, hb, u1, u2, *near0, *near1, *near2)
    (copies,) = call(gram_kernel, "gram", [VM] * 6, [arr(bands * sectors, 1, 16)], [], 10**6)(
        b0, b1, b2, a0, a1, a2
    )
    copies, packed = lax.optimization_barrier((copies, packed))
    parts = lax.all_to_all(copies, ("lat", "lon"), 0, 0, tiled=True)
    (parts_g,) = call(
        grid_kernel,
        "grid",
        [SM] + [VM] * 4,
        [arr(3, 3, cells)],
        [
            pltpu.VMEM((cells // BLK, 3, BLK, BLK), F32),
            pltpu.VMEM((GROUP, BLK, 2 * BLK), BF16),
            pltpu.VMEM((cells // BLK, 16, BLK), F32),
        ],
        10**9,
    )(pairs_cells, channel_corr, frame, packed, flat(bg_std_grid))
    (parts_w,) = call(unsort_kernel, "unsort", [VM] * 3, [arr(2, 3, slots)], [], 10**8)(rank, b1, b2)
    weights, increment = call(
        final_kernel,
        "final",
        [SM] + [VM] * 4,
        [arr(3, 1, slots), arr(3, 1, cells)],
        [obs_in, pltpu.VMEM((3, 1, cells), F32), pltpu.SemaphoreType.DMA((2,))],
        10**6,
        [HB, HB],
    )(tile_counts, parts, flat(innovation), parts_w, parts_g)
    return weights.reshape(1, 1, 3, slots), increment.reshape(1, 1, 3, cells)


def solution(mesh):
    spec = P("lat", "lon", None, None)
    return jax.shard_map(
        per_device,
        mesh=mesh,
        in_specs=(P("lat", "lon"), spec, spec, spec, spec, P(), spec),
        out_specs=(spec, spec),
        check_vma=False,
    )
```

time: 147 us -> 91.8 us (0.62)
  the two profiles are of different devices: /device:TPU:107 before, /device:TPU:1 now
where the time goes in v2:
time: 91.8 us; the launch traced here: 91.7 us
  starting transfers between devices  29.7 us (32%)
  Pallas kernels  29.6 us (32%)
  waiting for transfers between devices  28.7 us (31%)
  local copies, waits for them, and re-layouts  2.19 us (2%)
  between operations  1.52 us (2%)
    ppermute x12, waiting for transfers between devices, ring(): lax.ppermute(x, axis, [(i, (i + step) % count) for i in range(count)])  20.8 us
    ppermute x12, starting transfers between devices, ring(): lax.ppermute(x, axis, [(i, (i + step) % count) for i in range(count)])  20.5 us
    all_to_all x1, starting transfers between devices, per_device(): parts = lax.all_to_all(copies, ('lat', 'lon'), 0, 0, tiled=True)  9.23 us
    all_to_all x1, waiting for transfers between devices, per_device(): parts = lax.all_to_all(copies, ('lat', 'lon'), 0, 0, tiled=True)  7.87 us
    pallas_call x1, Pallas kernels, per_device(): call(near_fill_kernel, 'near_fill', [VM] * 6, [arr(8 * per, 8, BLK), arr(...  5.98 us
    pallas_call x3, Pallas kernels, near_times(): call(near_times_kernel, 'near_times', [SM] + [VM] * 11, [arr(8, slots), t...  5.46 us
    pallas_call x1, Pallas kernels, per_device(): call(grid_kernel, 'grid', [SM] + [VM] * 4, [arr(3, 3, cells)], [pltpu.VME...  5.32 us
    pallas_call x3, Pallas kernels, own_times(): call(own_times_kernel, 'own_times', [SM] + [VM] * 2, [arr(per, 8, BLK)],...  3.87 us
  transfers between devices with their start and end apart: 13, of which 8 were waited for; matrix products, arithmetic and copies ran while one was open for 0% of the time, Pallas kernels for 14%

profile of v2, /device:TPU:1, one launch (start us, length us, event | category | flops | bytes accessed | tf_op | source)
XLA Modules:
  0.0 91.7 jit_solution(2502179737545177971)
XLA Ops:
  1.3 3.6 %sort.1 = (f32[8,1024]{1,0:T(8,128)}, f32[3,1024]{1,0:T(4,128)}, f32[3,1024]{1,0:T(4,128)}, f32[3,1024]{1,0:T(4,128)}, f32[1,1024]{1,0:T(1,128)}, /*index=5*/f32[8,8]{1,0:T(8,128)}, f32[8,128]{1,0:T(8,128)}) custom-call(s32[1,1]{1,0:T(1,128)S(6)} %copy.12.count, f32[16,16,8,8]{3,2,1,0:T(8,128)} %constant.2.clone.table, f32[3,1,1024]{2,1,0:T(1,128)} %bitcast.32, ...), custom_call_target="tpu_custom_call" | custom-call | flops 100000000 | bytes 1048576 | tf_op jit(solution)/shard_map/sort/pallas_call | solution.py:625
  4.9 3.3 %collective-permute-start.1 = (f32[8,1024]{1,0:T(8,128)}, f32[8,1024]{1,0:T(8,128)S(1)}, u32[]{:S(2)}, u32[]{:S(2)}) collective-permute-start(f32[8,1024]{1,0:T(8,128)} %get-tuple-element.41.hb.u.u0), channel_id=1, source_target_pairs={{0,240},{16,0},{32,16},{48,32},{64,48},{80,64},{96,80},{112,96},{1... | collective-permute-start | bytes 98312 | tf_op jit(solution)/shard_map/ppermute | solution.py:566
  8.2 0.8 copy-done
  9.0 0.7 copy-done.8
  9.7 0.7 copy-done.11
  10.3 3.1 %own_fill.1 = (f32[8,8,128]{2,1,0:T(8,128)S(1)}, f32[8,3,128,128]{3,2,1,0:T(8,128)S(1)}, s32[1,156]{1,0:T(1,128)S(1)}, bf16[44,128,256]{2,1,0:T(8,128)(2,1)S(1)}) custom-call(f32[8,8]{1,0:T(8,128)S(1)} %copy-done.8, f32[8,1024]{1,0:T(8,128)S(1)} %copy-done, f32[8,128]{1,0:T(8,128)S(1)} %copy-done.11), custom_call_target="tpu_custom_call" | custom-call | flops 1000000000 | bytes 1048576 | tf_op jit(solution)/shard_map/own_fill/pallas_call | solution.py:647
  13.5 6.5 %collective-permute-start.3 = (f32[3,8,1024]{2,1,0:T(8,128)S(1)}, f32[3,8,1024]{2,1,0:T(8,128)S(1)}, u32[]{:S(2)}, u32[]{:S(2)}) collective-permute-start(f32[3,8,1024]{2,1,0:T(8,128)S(1)} %pad_maximum_fusion.hm.um.refs_0_), channel_id=1, source_target_pairs={{0,15},{1,0},{2,1},{3,2},{4,3},{5,4},{6,5},{7,6},{8,7},{9,8},{10,9... | collective-permute-start | bytes 294920 | tf_op jit(solution)/shard_map/ppermute | solution.py:566
  20.1 1.3 %own_times.3.acc_own = f32[8,8,128]{2,1,0:T(8,128)S(1)} custom-call(s32[1,156]{1,0:T(1,128)S(1)} %get-tuple-element.44.pairs, bf16[44,128,256]{2,1,0:T(8,128)(2,1)S(1)} %get-tuple-element.45.cache, f32[8,1024]{1,0:T(8,128)S(1)} %copy-done.1), custom_call_target="tpu_custom_call" | custom-call | flops 100000000 | bytes 1048576 | tf_op jit(solution)/shard_map/own_times/pallas_call | solution.py:663
  21.4 0.3 collective-permute-done.3.he.ue.refs_2_
  21.7 5.1 %collective-permute-done.2.hw.uw.refs_1_ = f32[3,8,1024]{2,1,0:T(8,128)S(1)} collective-permute-done((f32[3,8,1024]{2,1,0:T(8,128)S(1)}, f32[3,8,1024]{2,1,0:T(8,128)S(1)}, u32[]{:S(2)}, u32[]{:S(2)}) %collective-permute-start.2) | collective-permute-done | bytes 98336 | tf_op jit(solution)/shard_map/ppermute | solution.py:566
  26.9 6.0 %near_fill.1 = (f32[64,8,128]{2,1,0:T(8,128)S(1)}, s32[1,640]{1,0:T(1,128)S(1)}, s32[1,416]{1,0:T(1,128)S(1)}, bf16[104,128,256]{2,1,0:T(8,128)(2,1)S(1)}) custom-call(f32[8,8]{1,0:T(8,128)S(1)} %copy-done.9, f32[8,128]{1,0:T(8,128)S(1)} %copy-done.11, f32[8,3,128,128]{3,2,1,0:T(8,128)S(1)} %get-tuple-element.42.tcol, ...), custom_call_target="tpu_custom_call" | custom-call | flops 1000000000 | bytes 1048576 | tf_op jit(solution)/shard_map/near_fill/pallas_call | solution.py:675
  32.9 1.6 %near_times.3 = (f32[8,1024]{1,0:T(8,128)S(1)}, f32[3,1024]{1,0:T(4,128)S(1)}, f32[3,1024]{1,0:T(4,128)S(1)}) custom-call(s32[1,640]{1,0:T(1,128)S(1)} %get-tuple-element.49.pairs, f32[3,3]{1,0:T(4,128)S(1)} %copy-done.6, bf16[104,128,256]{2,1,0:T(8,128)(2,1)S(1)} %get-tuple-element.50.cache, f32[64,8,128]{2,1,0:T(8,128)S(1)} %get-tuple-element.51.q_ref.q_near, ...), custom_call_target="tpu_custom_call" | custom-call | flops 100000000 | bytes 1048576 | tf_op jit(solution)/shard_map/near_times/pallas_call | solution.py:691
  34.5 2.6 %collective-permute-start.5 = (f32[8,1024]{1,0:T(8,128)S(1)}, f32[8,1024]{1,0:T(8,128)S(1)}, u32[]{:S(2)}, u32[]{:S(2)}) collective-permute-start(f32[8,1024]{1,0:T(8,128)S(1)} %get-tuple-element.56.u.u1), channel_id=1, source_target_pairs={{0,240},{16,0},{32,16},{48,32},{64,48},{80,64},{96,80},{112,96},{1... | collective-permute-start | bytes 98312 | tf_op jit(solution)/shard_map/ppermute | solution.py:566
  37.1 1.3 %own_times.4.acc_own = f32[8,8,128]{2,1,0:T(8,128)S(1)} custom-call(s32[1,156]{1,0:T(1,128)S(1)} %get-tuple-element.44.pairs, bf16[44,128,256]{2,1,0:T(8,128)(2,1)S(1)} %get-tuple-element.45.cache, f32[8,1024]{1,0:T(8,128)S(1)} %get-tuple-element.56.u.u1), custom_call_target="tpu_custom_call" | custom-call | flops 100000000 | bytes 1048576 | tf_op jit(solution)/shard_map/own_times/pallas_call | solution.py:663
  38.4 3.9 %collective-permute-done.4 = f32[8,1024]{1,0:T(8,128)S(1)} collective-permute-done((f32[8,1024]{1,0:T(8,128)S(1)}, f32[8,1024]{1,0:T(8,128)S(1)}, u32[]{:S(2)}, u32[]{:S(2)}) %collective-permute-start.4) | collective-permute-done | bytes 32800 | tf_op jit(solution)/shard_map/ppermute | solution.py:566
  42.7 1.2 %collective-permute-start.6 = (f32[3,8,1024]{2,1,0:T(8,128)S(1)}, f32[3,8,1024]{2,1,0:T(8,128)S(1)}, u32[]{:S(2)}, u32[]{:S(2)}) collective-permute-start(f32[3,8,1024]{2,1,0:T(8,128)S(1)} %pad_maximum_fusion.1.um.refs_3_), channel_id=1, source_target_pairs={{0,1},{1,2},{2,3},{3,4},{4,5},{5,6},{6,7},{7,8},{8,9},{9,10},{10,1... | collective-permute-start | bytes 294920 | tf_op jit(solution)/shard_map/ppermute | solution.py:566
  43.9 2.0 %collective-permute-done.7.ue.refs_5_ = f32[3,8,1024]{2,1,0:T(8,128)S(1)} collective-permute-done((f32[3,8,1024]{2,1,0:T(8,128)S(1)}, f32[3,8,1024]{2,1,0:T(8,128)S(1)}, u32[]{:S(2)}, u32[]{:S(2)}) %collective-permute-start.7) | collective-permute-done | bytes 98336 | tf_op jit(solution)/shard_map/ppermute | solution.py:566
  45.9 3.6 %collective-permute-done.6.uw.refs_4_ = f32[3,8,1024]{2,1,0:T(8,128)S(1)} collective-permute-done((f32[3,8,1024]{2,1,0:T(8,128)S(1)}, f32[3,8,1024]{2,1,0:T(8,128)S(1)}, u32[]{:S(2)}, u32[]{:S(2)}) %collective-permute-start.6) | collective-permute-done | bytes 98336 | tf_op jit(solution)/shard_map/ppermute | solution.py:566
  49.5 1.6 %near_times.4 = (f32[8,1024]{1,0:T(8,128)S(1)}, f32[3,1024]{1,0:T(4,128)S(1)}, f32[3,1024]{1,0:T(4,128)S(1)}) custom-call(s32[1,640]{1,0:T(1,128)S(1)} %get-tuple-element.49.pairs, f32[3,3]{1,0:T(4,128)S(1)} %copy-done.6, bf16[104,128,256]{2,1,0:T(8,128)(2,1)S(1)} %get-tuple-element.50.cache, f32[64,8,128]{2,1,0:T(8,128)S(1)} %get-tuple-element.51.q_ref.q_near, ...), custom_call_target="tpu_custom_call" | custom-call | flops 100000000 | bytes 1048576 | tf_op jit(solution)/shard_map/near_times/pallas_call | solution.py:691
  51.1 5.0 %collective-permute-start.9 = (f32[8,1024]{1,0:T(8,128)S(1)}, f32[8,1024]{1,0:T(8,128)S(1)}, u32[]{:S(2)}, u32[]{:S(2)}) collective-permute-start(f32[8,1024]{1,0:T(8,128)S(1)} %get-tuple-element.63.u.u2), channel_id=1, source_target_pairs={{0,240},{16,0},{32,16},{48,32},{64,48},{80,64},{96,80},{112,96},{1... | collective-permute-start | bytes 98312 | tf_op jit(solution)/shard_map/ppermute | solution.py:566
  56.1 1.3 %own_times.5.acc_own = f32[8,8,128]{2,1,0:T(8,128)S(1)} custom-call(s32[1,156]{1,0:T(1,128)S(1)} %get-tuple-element.44.pairs, bf16[44,128,256]{2,1,0:T(8,128)(2,1)S(1)} %get-tuple-element.45.cache, f32[8,1024]{1,0:T(8,128)S(1)} %get-tuple-element.63.u.u2), custom_call_target="tpu_custom_call" | custom-call | flops 100000000 | bytes 1048576 | tf_op jit(solution)/shard_map/own_times/pallas_call | solution.py:663
  57.5 1.0 %collective-permute-start.11 = (f32[3,8,1024]{2,1,0:T(8,128)S(1)}, f32[3,8,1024]{2,1,0:T(8,128)S(1)}, u32[]{:S(2)}, u32[]{:S(2)}) collective-permute-start(f32[3,8,1024]{2,1,0:T(8,128)S(1)} %pad_maximum_fusion.2.um.refs_6_), channel_id=1, source_target_pairs={{0,15},{1,0},{2,1},{3,2},{4,3},{5,4},{6,5},{7,6},{8,7},{9,8},{10,9... | collective-permute-start | bytes 294920 | tf_op jit(solution)/shard_map/ppermute | solution.py:566
  58.5 0.5 collective-permute-start.10
  59.0 0.4 unsort.1.w
  59.5 1.6 %collective-permute-done.11.ue.refs_8_ = f32[3,8,1024]{2,1,0:T(8,128)S(1)} collective-permute-done((f32[3,8,1024]{2,1,0:T(8,128)S(1)}, f32[3,8,1024]{2,1,0:T(8,128)S(1)}, u32[]{:S(2)}, u32[]{:S(2)}) %collective-permute-start.11) | collective-permute-done | bytes 98336 | tf_op jit(solution)/shard_map/ppermute | solution.py:566
  61.0 4.2 %collective-permute-done.10.uw.refs_7_ = f32[3,8,1024]{2,1,0:T(8,128)S(1)} collective-permute-done((f32[3,8,1024]{2,1,0:T(8,128)S(1)}, f32[3,8,1024]{2,1,0:T(8,128)S(1)}, u32[]{:S(2)}, u32[]{:S(2)}) %collective-permute-start.10) | collective-permute-done | bytes 98336 | tf_op jit(solution)/shard_map/ppermute | solution.py:566
  65.3 2.2 %near_times.5 = (f32[8,1024]{1,0:T(8,128)}, f32[3,1024]{1,0:T(4,128)S(1)}, f32[3,1024]{1,0:T(4,128)}) custom-call(s32[1,640]{1,0:T(1,128)S(1)} %get-tuple-element.49.pairs, f32[3,3]{1,0:T(4,128)S(1)} %copy-done.6, bf16[104,128,256]{2,1,0:T(8,128)(2,1)S(1)} %get-tuple-element.50.cache, f32[64,8,128]{2,1,0:T(8,128)S(1)} %get-tuple-element.51.q_ref.q_near, ...), custom_call_target="tpu_custom_call" | custom-call | flops 100000000 | bytes 1048576 | tf_op jit(solution)/shard_map/near_times/pallas_call | solution.py:691
  67.6 0.8 gram.1
  68.4 9.2 %all-to-all-start = ((f32[256,1,16]{2,1,0:T(1,128)}), f32[256,1,16]{2,1,0:T(1,128)S(1)}, u32[]{:S(2)}, u32[]{:S(2)}) async-start(f32[256,1,16]{2,1,0:T(1,128)} %gram.1), calls=%async_computation | async-start | bytes 262144 | tf_op jit(solution)/shard_map/all_to_all | solution.py:712
  77.7 5.3 %grid.1.g = f32[3,3,512]{2,1,0:T(4,128)S(1)} custom-call(s32[1,416]{1,0:T(1,128)S(1)} %get-tuple-element.70.pairs, f32[3,3]{1,0:T(4,128)S(1)} %copy-done.6, f32[8,8]{1,0:T(8,128)S(1)} %copy-done.9, f32[72,16,128]{2,1,0:T(8,128)S(1)} %pack.1.packed, f32[3,1,512]{2,1,0:T(1,128)S(1)} %bitcast.25), custom_call_target="tpu_custom_call" | custom-call | flops 1000000000 | bytes 1048576 | tf_op jit(solution)/shard_map/grid/pallas_call | solution.py:713
  83.0 7.9 %all-to-all-done.parts = f32[256,1,16]{2,1,0:T(1,128)S(1)} async-done(((f32[256,1,16]{2,1,0:T(1,128)}), f32[256,1,16]{2,1,0:T(1,128)S(1)}, u32[]{:S(2)}, u32[]{:S(2)}) %all-to-all-start) | async-done | bytes 16416 | tf_op jit(solution)/shard_map/all_to_all | solution.py:712
  90.9 0.8 final.1
  (35 shorter events, 0.5 us)
Async XLA Ops:
  4.9 8.5 %collective-permute-start.1 = (f32[8,1024]{1,0:T(8,128)}, f32[8,1024]{1,0:T(8,128)S(1)}, u32[]{:S(2)}, u32[]{:S(2)}) collective-permute-start(f32[8,1024]{1,0:T(8,128)} %get-tuple-element.41.hb.u.u0), channel_id=1, source_target_pairs={{0,240},{16,0},{32,16},{48,32},{64,48},{80,64},{96,80},{112,96},{1... | collective-permute-start | bytes 98312 | tf_op jit(solution)/shard_map/ppermute | solution.py:566
  8.2 5.3 %collective-permute-start = (f32[8,1024]{1,0:T(8,128)}, f32[8,1024]{1,0:T(8,128)S(1)}, u32[]{:S(2)}, u32[]{:S(2)}) collective-permute-start(f32[8,1024]{1,0:T(8,128)} %get-tuple-element.41.hb.u.u0), channel_id=1, source_target_pairs={{0,16},{16,32},{32,48},{48,64},{64,80},{80,96},{96,112},{112,128},... | collective-permute-start | bytes 98312 | tf_op jit(solution)/shard_map/ppermute | solution.py:566
  8.2 0.8 copy-start
  9.0 0.7 copy-start.8
  9.7 0.7 copy-start.11
  10.3 3.1 %copy-start.1 = (f32[8,1024]{1,0:T(8,128)S(1)}, f32[8,1024]{1,0:T(8,128)}, u32[]{:S(2)}) copy-start(f32[8,1024]{1,0:T(8,128)} %get-tuple-element.41.hb.u.u0) | copy-start | bytes 98308
  10.3 16.5 %copy-start.9 = (f32[8,8]{1,0:T(8,128)S(1)}, f32[8,8]{1,0:T(8,128)}, u32[]{:S(2)}) copy-start(f32[8,8]{1,0:T(8,128)} %get-tuple-element.39.frame) | copy-start | bytes 772
  13.5 19.4 %copy-start.2 = (f32[3,1024]{1,0:T(4,128)S(1)}, f32[3,1024]{1,0:T(4,128)}, u32[]{:S(2)}) copy-start(f32[3,1024]{1,0:T(4,128)} %get-tuple-element.53.dev) | copy-start | bytes 36868
  13.5 19.4 %copy-start.3 = (f32[3,1024]{1,0:T(4,128)S(1)}, f32[3,1024]{1,0:T(4,128)}, u32[]{:S(2)}) copy-start(f32[3,1024]{1,0:T(4,128)} %get-tuple-element.54.var) | copy-start | bytes 36868
  13.5 19.4 %copy-start.4 = (f32[3,1024]{1,0:T(4,128)S(1)}, f32[3,1024]{1,0:T(4,128)}, u32[]{:S(2)}) copy-start(f32[3,1024]{1,0:T(4,128)} %get-tuple-element.38.field.b0) | copy-start | bytes 36868
  13.5 19.4 %copy-start.6 = (f32[3,3]{1,0:T(4,128)S(1)}, f32[3,3]{1,0:T(4,128)}, u32[]{:S(2)}) copy-start(f32[3,3]{1,0:T(4,128)} %corr.7) | copy-start | bytes 112
  13.5 8.2 %collective-permute-start.3 = (f32[3,8,1024]{2,1,0:T(8,128)S(1)}, f32[3,8,1024]{2,1,0:T(8,128)S(1)}, u32[]{:S(2)}, u32[]{:S(2)}) collective-permute-start(f32[3,8,1024]{2,1,0:T(8,128)S(1)} %pad_maximum_fusion.hm.um.refs_0_), channel_id=1, source_target_pairs={{0,15},{1,0},{2,1},{3,2},{4,3},{5,4},{6,5},{7,6},{8,7},{9,8},{10,9... | collective-permute-start | bytes 294920 | tf_op jit(solution)/shard_map/ppermute | solution.py:566
  20.1 6.8 %collective-permute-start.2 = (f32[3,8,1024]{2,1,0:T(8,128)S(1)}, f32[3,8,1024]{2,1,0:T(8,128)S(1)}, u32[]{:S(2)}, u32[]{:S(2)}) collective-permute-start(f32[3,8,1024]{2,1,0:T(8,128)S(1)} %pad_maximum_fusion.hm.um.refs_0_), channel_id=1, source_target_pairs={{0,1},{1,2},{2,3},{3,4},{4,5},{5,6},{6,7},{7,8},{8,9},{9,10},{10,1... | collective-permute-start | bytes 294920 | tf_op jit(solution)/shard_map/ppermute | solution.py:566
  34.5 3.9 %collective-permute-start.5 = (f32[8,1024]{1,0:T(8,128)S(1)}, f32[8,1024]{1,0:T(8,128)S(1)}, u32[]{:S(2)}, u32[]{:S(2)}) collective-permute-start(f32[8,1024]{1,0:T(8,128)S(1)} %get-tuple-element.56.u.u1), channel_id=1, source_target_pairs={{0,240},{16,0},{32,16},{48,32},{64,48},{80,64},{96,80},{112,96},{1... | collective-permute-start | bytes 98312 | tf_op jit(solution)/shard_map/ppermute | solution.py:566
  37.1 5.3 %collective-permute-start.4 = (f32[8,1024]{1,0:T(8,128)S(1)}, f32[8,1024]{1,0:T(8,128)S(1)}, u32[]{:S(2)}, u32[]{:S(2)}) collective-permute-start(f32[8,1024]{1,0:T(8,128)S(1)} %get-tuple-element.56.u.u1), channel_id=1, source_target_pairs={{0,16},{16,32},{32,48},{48,64},{64,80},{80,96},{96,112},{112,128},... | collective-permute-start | bytes 98312 | tf_op jit(solution)/shard_map/ppermute | solution.py:566
  42.4 3.5 %collective-permute-start.7 = (f32[3,8,1024]{2,1,0:T(8,128)S(1)}, f32[3,8,1024]{2,1,0:T(8,128)S(1)}, u32[]{:S(2)}, u32[]{:S(2)}) collective-permute-start(f32[3,8,1024]{2,1,0:T(8,128)S(1)} %pad_maximum_fusion.1.um.refs_3_), channel_id=1, source_target_pairs={{0,15},{1,0},{2,1},{3,2},{4,3},{5,4},{6,5},{7,6},{8,7},{9,8},{10,9... | collective-permute-start | bytes 294920 | tf_op jit(solution)/shard_map/ppermute | solution.py:566
  42.7 6.8 %collective-permute-start.6 = (f32[3,8,1024]{2,1,0:T(8,128)S(1)}, f32[3,8,1024]{2,1,0:T(8,128)S(1)}, u32[]{:S(2)}, u32[]{:S(2)}) collective-permute-start(f32[3,8,1024]{2,1,0:T(8,128)S(1)} %pad_maximum_fusion.1.um.refs_3_), channel_id=1, source_target_pairs={{0,1},{1,2},{2,3},{3,4},{4,5},{5,6},{6,7},{7,8},{8,9},{9,10},{10,1... | collective-permute-start | bytes 294920 | tf_op jit(solution)/shard_map/ppermute | solution.py:566
  51.1 7.9 %copy-start.10 = (f32[1,1024]{1,0:T(1,128)S(1)}, f32[1,1024]{1,0:T(1,128)}, u32[]{:S(2)}) copy-start(f32[1,1024]{1,0:T(1,128)} %get-tuple-element.69.rank) | copy-start | bytes 12292
  51.1 6.3 %collective-permute-start.9 = (f32[8,1024]{1,0:T(8,128)S(1)}, f32[8,1024]{1,0:T(8,128)S(1)}, u32[]{:S(2)}, u32[]{:S(2)}) collective-permute-start(f32[8,1024]{1,0:T(8,128)S(1)} %get-tuple-element.63.u.u2), channel_id=1, source_target_pairs={{0,240},{16,0},{32,16},{48,32},{64,48},{80,64},{96,80},{112,96},{1... | collective-permute-start | bytes 98312 | tf_op jit(solution)/shard_map/ppermute | solution.py:566
  56.1 1.3 %collective-permute-start.8 = (f32[8,1024]{1,0:T(8,128)S(1)}, f32[8,1024]{1,0:T(8,128)S(1)}, u32[]{:S(2)}, u32[]{:S(2)}) collective-permute-start(f32[8,1024]{1,0:T(8,128)S(1)} %get-tuple-element.63.u.u2), channel_id=1, source_target_pairs={{0,16},{16,32},{32,48},{48,64},{64,80},{80,96},{96,112},{112,128},... | collective-permute-start | bytes 98312 | tf_op jit(solution)/shard_map/ppermute | solution.py:566
  57.5 3.5 %collective-permute-start.11 = (f32[3,8,1024]{2,1,0:T(8,128)S(1)}, f32[3,8,1024]{2,1,0:T(8,128)S(1)}, u32[]{:S(2)}, u32[]{:S(2)}) collective-permute-start(f32[3,8,1024]{2,1,0:T(8,128)S(1)} %pad_maximum_fusion.2.um.refs_6_), channel_id=1, source_target_pairs={{0,15},{1,0},{2,1},{3,2},{4,3},{5,4},{6,5},{7,6},{8,7},{9,8},{10,9... | collective-permute-start | bytes 294920 | tf_op jit(solution)/shard_map/ppermute | solution.py:566
  58.5 6.8 %collective-permute-start.10 = (f32[3,8,1024]{2,1,0:T(8,128)S(1)}, f32[3,8,1024]{2,1,0:T(8,128)S(1)}, u32[]{:S(2)}, u32[]{:S(2)}) collective-permute-start(f32[3,8,1024]{2,1,0:T(8,128)S(1)} %pad_maximum_fusion.2.um.refs_6_), channel_id=1, source_target_pairs={{0,1},{1,2},{2,3},{3,4},{4,5},{5,6},{6,7},{7,8},{8,9},{9,10},{10,1... | collective-permute-start | bytes 294920 | tf_op jit(solution)/shard_map/ppermute | solution.py:566
  59.5 18.2 %copy-start.7 = (f32[1,1,3,512]{3,1,2,0:T(1,128)S(1)}, f32[1,1,3,512]{3,1,2,0:T(1,128)}, u32[]{:S(2)}) copy-start(f32[1,1,3,512]{3,1,2,0:T(1,128)} %param.14) | copy-start | bytes 18436
  67.5 23.4 %copy-start.5 = (f32[1,1,3,1024]{3,1,2,0:T(1,128)S(1)}, f32[1,1,3,1024]{3,1,2,0:T(1,128)}, u32[]{:S(2)}) copy-start(f32[1,1,3,1024]{3,1,2,0:T(1,128)} %param.10) | copy-start | bytes 36868
  68.4 22.4 %all-to-all-start = ((f32[256,1,16]{2,1,0:T(1,128)}), f32[256,1,16]{2,1,0:T(1,128)S(1)}, u32[]{:S(2)}, u32[]{:S(2)}) async-start(f32[256,1,16]{2,1,0:T(1,128)} %gram.1), calls=%async_computation | async-start | bytes 262144 | tf_op jit(solution)/shard_map/all_to_all | solution.py:712

commit v3 on v2

--- a/solution.py
+++ b/solution.py
@@ -72,8 +72,8 @@
 
 
 def sort_kernel(
-    count, table, pos_in, innov_in, bg_in, std_in,
-    hb_out, dev_out, var_out, b0_out, rank_out, frame_out, bounds_out,
+    count, table, pos_in, innov_in, bg_in, std_in, bgg_in, corr_in,
+    hb_out, dev_out, var_out, b0_out, rank_out, frame_out, bounds_out, innov_out, bgg_out, corr_out,
     pos, innov, bg, std, sems,
 ):
     bands, sectors = lax.axis_size("lat"), lax.axis_size("lon")
@@ -84,12 +84,14 @@
         (innov_in, innov),
         (bg_in, bg),
         (std_in, std),
+        (bgg_in, bgg_out),
+        (corr_in, corr_out),
     ]
     copies = [pltpu.make_async_copy(x, y, sems.at[k]) for k, (x, y) in enumerate(pairs)]
     for copy in copies:
         copy.start()
-    for copy in copies:
-        copy.wait()
+    copies[0].wait()
+    copies[1].wait()
 
     def rows(ref):
         return jnp.concatenate([ref[0], ref[1], ref[2]], axis=0)
@@ -108,10 +110,13 @@
     sine = east * lax.rsqrt(jnp.maximum(px * px + py * py, 1e-6))
     rank = rank_of(jnp.where(live, strip + sine, 100.0), slots)
     rank_out[...] = rank
+    for copy in copies[2:]:
+        copy.wait()
     maskf = jnp.where(live, 1.0, 0.0).astype(F32)
     where3 = jnp.where(live, rows(pos), FAR)
     dev = rows(bg) * maskf
     start = rows(innov) * maskf
+    innov_out[...] = start
     var = rows(std)
     var = var * var * maskf
     sine = jnp.where(live, sine, 0.0)
@@ -167,7 +172,7 @@
     return [wide[:, b * BLK : (b + 1) * BLK] for b in range(wide.shape[1] // BLK)]
 
 
-def active_words(source, target, bands):
+def active_blocks(source, target, bands):
     slo, shi, wlo, whi = source
     tlo, thi, vlo, vhi = target
 
@@ -185,54 +190,54 @@
     )
     bound = lat + gap2 * (1.0 - gap2 * (1.0 / 12.0)) * small
     reach = (0.6 / bands) ** 2
-    lane = lax.broadcasted_iota(jnp.int32, bound.shape, 1)
-    active = (bound < reach * 1.002 + 1e-6) & (tlo < 50.0)
-    word = jnp.where(active, jnp.left_shift(jnp.full(lane.shape, 1, jnp.int32), (lane >> 3) & 7), 0)
-    for shift in (8, 16, 32):
-        word = word + pltpu.roll(word, BLK - shift, 1)
-    return word
-
-
-def source_bounds(tiles, shifts):
+    return (bound < reach * 1.002 + 1e-6) & (tlo < 50.0) & (slo < 50.0)
+
+
+def source_bounds(tiles, shifts, height):
     rows = []
     for k in range(4):
         parts = []
         for tile, shift in zip(tiles, shifts):
             row = tile[6:7, k * BLK : (k + 1) * BLK]
             parts.append(row + shift if k >= 2 else row)
+        parts.append(jnp.full((height - len(tiles), BLK), 100.0, F32))
         rows.append(jnp.concatenate(parts, axis=0))
     return rows
 
 
-def to_smem(words, mask_v, mask_s, sem):
-    mask_v[0 : words.shape[0], :] = words
-    copy = pltpu.make_async_copy(mask_v, mask_s, sem)
-    copy.start()
-    copy.wait()
-
-
-def list_pairs(mask_s, column, regions, first, pairs, count, below=False):
-    def source(i, count):
-        r, b = i >> 3, i & 7
-
-        def take(state):
-            word, k = state
-            bit = word & -word
-            pairs[0, k] = (first * 8 + i) * 8 + (31 - lax.clz(bit))
-            return word ^ bit, k + 1
-
-        word = mask_s[r, column + b]
-        if below:
-            word = word & (jnp.left_shift(1, b) - 1)
-        return lax.while_loop(lambda state: state[0] != 0, take, (word, count))[1]
-
-    return lax.fori_loop(0, 8 * regions, source, count)
-
-
-def close_list(pairs, count):
-    for k in range(UNROLL):
-        pairs[0, count + k] = 0
-    pairs[0, pairs.shape[1] - 1] = count
+def two_lists(active, source, target, regions):
+    height = active.shape[0]
+
+    def exact(x, y, dims):
+        return lax.dot_general(x.astype(BF16), y.astype(BF16), dims, preferred_element_type=F32)
+
+    def ones(mask):
+        return jnp.where(mask, 1.0, 0.0).astype(F32)
+
+    def iota(shape, dim):
+        return lax.broadcasted_iota(jnp.int32, shape, dim)
+
+    act = ones(active)
+    i, j = iota((BLK, BLK), 0), iota((BLK, BLK), 1)
+    same = ones((i >> 6) == (j >> 6))
+    ahead = ones(((i >> 6) == (j >> 6)) & (i < j))
+    above = ones(iota((height, height), 1) < iota((height, height), 0))
+    place = exact(act, ahead, NN) + exact(exact(above, act, NN), same, NN)
+    counts = exact(exact(jnp.ones((8, height), F32), act, NN), same, NN)[0:1]
+    lane = iota(active.shape, 1)
+    slot = jnp.where(active & (place < BLK), place + jnp.where(lane < 64, 0.0, 1.0 * BLK), -1.0)
+    index = iota((2 * BLK, BLK), 0).astype(F32)
+    picks = jnp.concatenate([ones(index == slot[r : r + 1]) for r in range(regions)], axis=1)
+    names = [
+        jnp.concatenate([x[r : r + 1].astype(F32) for r in range(regions)], axis=1)
+        for x in (source, target)
+    ]
+    names = jnp.concatenate(names + [jnp.zeros((6, regions * BLK), F32)], axis=0)
+    found = exact(names, picks, NT)
+    entries = found[0:1] * 8.0 + found[1:2]
+    return jnp.concatenate(
+        [entries[:, 0:BLK], entries[:, BLK : 2 * BLK], counts, jnp.zeros((5, BLK), F32)], axis=0
+    ).astype(jnp.int32)
 
 
 def rho_of(tcol, sx, sy, sz):
@@ -276,12 +281,12 @@
     fill_rows(q_ref[entry >> 3], tcol, entry & 7, out)
 
 
-def fill_cache(count, pairs, q_ref, tcol, cache, first):
+def fill_cache(count, lists, q_ref, tcol, cache, first):
     room = cache.shape[0] - UNROLL - first
     kept = jnp.minimum(count, room)
 
     def fill(p, _):
-        fill_pair(pairs[0, p], q_ref, tcol, cache.at[first + p])
+        fill_pair(lists[0, p], q_ref, tcol, cache.at[first + p])
         return 0
 
     lax.fori_loop(0, kept, fill, 0)
@@ -296,48 +301,53 @@
     return [hi, mid, rest - mid]
 
 
-def set_values(tile, v_ref, first):
-    v = jnp.concatenate(parts_of(tile) + [jnp.zeros(tile.shape, F32)], axis=0).astype(BF16)
+def set_values(rows, v_ref, first):
+    v = jnp.concatenate(parts_of(rows) + [jnp.zeros(rows.shape, F32)], axis=0).astype(BF16)
     for b, part in enumerate(blocks(v)):
         v_ref[first + b, :, 0:BLK] = part
         v_ref[first + b, :, BLK : 2 * BLK] = part
 
 
 def add_parts(out):
-    return out[0:8] + out[8:16] + out[16:24]
-
-
-def own_fill_kernel(frame, hb, bounds, q_out, tcol_out, pairs_out, cache_out, mask_v, mask_s, sem):
+    return out[0:8] + out[8:16]
+
+
+def total_of(acc):
+    wide = jnp.concatenate([acc[t] for t in range(acc.shape[0])], axis=1)
+    return wide[0:4] + wide[4:8]
+
+
+def own_fill_kernel(frame, hb, bounds, q_out, tcol_out, lists_out, cache_out, lists_v, sem):
     tile = hb[...]
     tiles = blocks(to_frame(tile, 3, frame[...]))
     per = len(tiles)
+    active = active_blocks(
+        source_bounds([tile], [0.0], 8), [bounds[k : k + 1, :] for k in range(4)], lax.axis_size("lat")
+    )
+    lane = lax.broadcasted_iota(jnp.int32, active.shape, 1)
+    source, target = lane & 7, (lane >> 3) & 7
+    lists_v[...] = two_lists(active & (lane < 64) & (target < source), source, target, 1)
+    copy = pltpu.make_async_copy(lists_v, lists_out, sem)
+    copy.start()
     for b, part in enumerate(tiles):
         q_out[b] = part
-    words = active_words(
-        source_bounds([tile], [0.0]), [bounds[k : k + 1, :] for k in range(4)], lax.axis_size("lat")
-    )
-    mask_v[0:1, :] = words
-    copy = pltpu.make_async_copy(mask_v, mask_s, sem)
-    copy.start()
     set_columns(tiles, tcol_out)
-    copy.wait()
-    count = list_pairs(mask_s, 0, 1, 0, pairs_out, 0, below=True)
-    close_list(pairs_out, count)
 
     def diagonal(b, _):
         fill_pair(b * 9, q_out, tcol_out, cache_out.at[b])
         return 0
 
     lax.fori_loop(0, per, diagonal, 0)
-    fill_cache(count, pairs_out, q_out, tcol_out, cache_out, per)
+    copy.wait()
+    fill_cache(lists_out[2, 0], lists_out, q_out, tcol_out, cache_out, per)
 
 
 def own_times_kernel(pairs, cache, u, acc, v_ref):
-    set_values(u[...], v_ref, 0)
+    set_values(u[0:4, :], v_ref, 0)
     per = acc.shape[0]
     for b in range(per):
         acc[b] = add_parts(lax.dot_general(v_ref[b], cache[b], NT, preferred_element_type=F32))
-    count = pairs[0, pairs.shape[1] - 1]
+    count = pairs[2, 0]
 
     def group(i, _):
         outs = []
@@ -363,30 +373,51 @@
 
 
 def near_fill_kernel(
-    frame, bounds, tcol, hm, hw, he, q_out, pairs_out, cells_out, cache_out, mask_v, mask_s, sem
+    frame, bounds, tcol, mid, south, north,
+    q_out, lists_out, long_out, cache_out, lists_v, mask_v, mask_s, sem, sem_long,
 ):
-    halo = (hm, hw, he)
-    per = hm.shape[2] // BLK
-    turn = 2.0 * math.pi / lax.axis_size("lon")
+    halo = (mid, south, north)
+    per = mid.shape[2] // BLK
+    turn = 2.0 * math.pi / lax.axis_size("lon") * frame[4:5, 6:7]
     where = [(0, 1)] + OTHERS
+    regions = len(where)
     tiles = [halo[c][a] for c, a in where]
-    words = active_words(
-        source_bounds(tiles, [(0.0, -turn, turn)[c] for c, a in where]),
+    active = active_blocks(
+        source_bounds(tiles, [(a - 1) * turn for c, a in where], 16),
         [bounds[k : k + 1, :] for k in range(4)],
         lax.axis_size("lat"),
     )
-    mask_v[0 : len(where), :] = words
-    copy = pltpu.make_async_copy(mask_v, mask_s, sem)
+    lane = lax.broadcasted_iota(jnp.int32, active.shape, 1)
+    region = lax.broadcasted_iota(jnp.int32, active.shape, 0)
+    active = active & ((lane >= 64) | (region > 0))
+    source = (lane & 7) + 8 * jnp.where(lane < 64, region - 1, region)
+    target = (lane >> 3) & 7
+    lists_v[...] = two_lists(active, source, target, regions)
+    copy = pltpu.make_async_copy(lists_v, lists_out, sem)
     copy.start()
     turned = frame[...]
-    for r in range(1, len(where)):
+    for r in range(1, regions):
         for b, part in enumerate(blocks(to_frame(tiles[r], 3, turned))):
             q_out[(r - 1) * per + b] = part
+    mask_v[...] = jnp.where(active, source * 8 + target + 1, 0)
     copy.wait()
-    count = list_pairs(mask_s.at[1 : len(where)], 0, len(where) - 1, 0, pairs_out, 0)
-    close_list(pairs_out, count)
-    fill_cache(count, pairs_out, q_out, tcol, cache_out, 0)
-    close_list(cells_out, list_pairs(mask_s, 64, len(where), 0, cells_out, 0))
+    count, count_cells = lists_out[2, 0], lists_out[2, 64]
+
+    @pl.when((count > KEPT) | (count_cells > KEPT))
+    def _():
+        again = pltpu.make_async_copy(mask_v, mask_s, sem_long)
+        again.start()
+        again.wait()
+        for half in range(2):
+
+            def step(i, k, half=half):
+                entry = mask_s[i >> 6, 64 * half + (i & 63)]
+                long_out[half, k] = entry - 1
+                return k + jnp.where(entry > 0, 1, 0)
+
+            lax.fori_loop(0, 64 * regions, step, 0)
+
+    fill_cache(count, lists_out, q_out, tcol, cache_out, 0)
 
 
 def mix(corr, total):
@@ -398,45 +429,45 @@
 
 
 def near_times_kernel(
-    pairs, corr, cache, q_ref, tcol, acc_own, um, uw, ue, dev, var, field,
-    u_out, img_out, nxt_out, v_ref, acc, pair,
+    last, lists, long, corr, cache, q_ref, tcol, acc_own, um, us, un, dev, var, field, *refs
 ):
-    halo = (um, uw, ue)
+    outs, (v_ref, acc, pair) = refs[:-3], refs[-3:]
+    halo = (um, us, un)
     per = acc.shape[0]
     for k, (c, a) in enumerate(OTHERS):
-        set_values(halo[c][a], v_ref, k * per)
+        set_values(halo[c][a, 0:4, :], v_ref, k * per)
     acc[...] = acc_own[...]
-    count = pairs[0, pairs.shape[1] - 1]
+    count = lists[2, 0]
     kept = jnp.minimum(count, cache.shape[0] - UNROLL)
 
     def group(i, _):
-        outs = []
+        found = []
         for k in range(UNROLL):
             p = i * UNROLL + k
-            n = pairs[0, p] >> 3
-            outs.append(lax.dot_general(v_ref[n], cache[p], NT, preferred_element_type=F32))
+            n = lists[0, p] >> 3
+            found.append(lax.dot_general(v_ref[n], cache[p], NT, preferred_element_type=F32))
         for k in range(UNROLL):
-            acc[pairs[0, i * UNROLL + k] & 7] += add_parts(outs[k])
+            acc[lists[0, i * UNROLL + k] & 7] += add_parts(found[k])
         return 0
 
     lax.fori_loop(0, (kept + UNROLL - 1) // UNROLL, group, 0)
 
     def extra(p, _):
-        entry = pairs[0, p]
+        entry = long[0, p]
         fill_pair(entry, q_ref, tcol, pair)
         out = lax.dot_general(v_ref[entry >> 3], pair[...], NT, preferred_element_type=F32)
         acc[entry & 7] += add_parts(out)
         return 0
 
     lax.fori_loop(kept, count, extra, 0)
-    total = jnp.concatenate([acc[t] for t in range(per)], axis=1)
     field = field[...]
     dev = dev[...]
-    image = dev * mix(corr, total) + var[...] * field
-    nxt = image - SHIFT * field
-    img_out[...] = image
-    nxt_out[...] = nxt
-    u_out[...] = jnp.concatenate([dev * nxt, jnp.zeros((5, nxt.shape[1]), F32)], axis=0)
+    image = dev * mix(corr, total_of(acc)) + var[...] * field
+    outs[0][...] = image
+    if not last:
+        nxt = image - SHIFT * field
+        outs[1][...] = nxt
+        outs[2][...] = jnp.concatenate([dev * nxt, jnp.zeros((1, nxt.shape[1]), F32)], axis=0)
 
 
 def gram_kernel(b0, b1, b2, a0, a1, a2, out):
@@ -455,13 +486,13 @@
     out[...] = jnp.broadcast_to(row[None], out.shape)
 
 
-def pack_kernel(q_own, q_near, u0, u1, u2, *refs):
+def pack_kernel(q_own, q_near, *refs):
     out = refs[-1]
     fields = [refs[3 * f : 3 * f + 3] for f in range(3)]
     per = q_own.shape[0]
-    for f, u in enumerate((u0, u1, u2)):
+    for f in range(3):
         for r, (c, a) in enumerate([(0, 1)] + OTHERS):
-            tile = u[...] if r == 0 else fields[f][c][a]
+            tile = fields[f][c][a, 0:4, :]
             for b, part in enumerate(blocks(tile)):
                 out[r * per + b, 3 * f : 3 * f + 3, :] = part[0:3]
     for b in range(per):
@@ -472,7 +503,7 @@
         out[n, 12:16, :] = jnp.zeros((4, BLK), F32)
 
 
-def grid_kernel(pairs, corr, frame, packed, bgg, g_out, tcol, rho, acc):
+def grid_kernel(lists, long, corr, frame, packed, bgg, g_out, tcol, rho, acc):
     cells = g_out.shape[2]
     columns = cells // GRID_ROWS
     bands, sectors = lax.axis_size("lat"), lax.axis_size("lon")
@@ -488,25 +519,35 @@
     point = jnp.where(row == 2, sinlat, point)
     set_columns(blocks(to_frame(point, 0, frame[...])), tcol)
     acc[...] = jnp.zeros(acc.shape, F32)
-    count = pairs[0, pairs.shape[1] - 1]
+    count = lists[2, 64]
+    short = jnp.minimum(count, KEPT)
+
+    def one(entry, weight, out):
+        near = packed[entry >> 3]
+        fill_rows(near[9:12], tcol, entry & 7, out)
+        v = jnp.concatenate(parts_of(near * weight), axis=0).astype(BF16)
+        v = jnp.concatenate([v, v], axis=1)
+        got = lax.dot_general(v, out[...], NT, preferred_element_type=F32)
+        return got[0:16] + got[16:32] + got[32:48]
 
     def group(i, _):
-        outs = []
+        found = []
         for k in range(GROUP):
             p = i * GROUP + k
-            entry = pairs[0, p]
-            near = packed[entry >> 3]
-            fill_rows(near[9:12], tcol, entry & 7, rho.at[k])
-            near = near * jnp.where(p < count, 1.0, 0.0).astype(F32)
-            v = jnp.concatenate(parts_of(near), axis=0).astype(BF16)
-            v = jnp.concatenate([v, v], axis=1)
-            outs.append(lax.dot_general(v, rho[k], NT, preferred_element_type=F32))
+            weight = jnp.where(p < short, 1.0, 0.0).astype(F32)
+            found.append(one(lists[1, p], weight, rho.at[k]))
         for k in range(GROUP):
-            out = outs[k]
-            acc[pairs[0, i * GROUP + k] & 7] += out[0:16] + out[16:32] + out[32:48]
+            acc[lists[1, i * GROUP + k] & 7] += found[k]
         return 0
 
-    lax.fori_loop(0, (count + GROUP - 1) // GROUP, group, 0)
+    lax.fori_loop(0, (short + GROUP - 1) // GROUP, group, 0)
+
+    def extra(p, _):
+        entry = long[1, p]
+        acc[entry & 7] += one(entry, 1.0, rho.at[0])
+        return 0
+
+    lax.fori_loop(short, count, extra, 0)
     total = jnp.concatenate([acc[t] for t in range(acc.shape[0])], axis=1)
     dev = jnp.concatenate([bgg[0], bgg[1], bgg[2]], axis=0)
     for f in range(3):
@@ -522,7 +563,7 @@
     w_out[1] = back[3:6]
 
 
-def final_kernel(count, parts, innov, w, g, w_out, g_out, w_buf, g_buf, sems):
+def final_kernel(parts, innov, w, g, w_out, g_out, w_buf, g_buf, sems):
     sums = parts[...]
     while sums.shape[0] > 1:
         half = sums.shape[0] // 2
@@ -545,11 +586,8 @@
     c2 = jnp.where(ok2, y2 / jnp.where(ok2, d2, 1.0), 0.0)
     c1 = jnp.where(ok1, y1 / safe1, 0.0) - l21 * c2
     c0 = g0 / m00 - l10 * c1 - l20 * c2
-    slots = innov.shape[2]
-    live = lax.broadcasted_iota(jnp.int32, (1, slots), 1) < count[0, 0] * OBS_TILE
     for k in range(3):
-        first = jnp.where(live, innov[k], 0.0)
-        w_buf[k] = c0 * first + c1 * w[0, k : k + 1] + c2 * w[1, k : k + 1]
+        w_buf[k] = c0 * innov[k : k + 1, :] + c1 * w[0, k : k + 1] + c2 * w[1, k : k + 1]
         g_buf[k] = c0 * g[0, k : k + 1] + c1 * g[1, k : k + 1] + c2 * g[2, k : k + 1]
     copies = [
         pltpu.make_async_copy(w_buf, w_out, sems.at[0]),
@@ -564,6 +602,15 @@
 def ring(x, axis, step):
     count = lax.axis_size(axis)
     return lax.ppermute(x, axis, [(i, (i + step) % count) for i in range(count)])
+
+
+def swap(x, axis, first, wrap):
+    count = lax.axis_size(axis)
+    pairs = []
+    for i in range(first, count, 2):
+        if i + 1 < count or wrap:
+            pairs += [(i, (i + 1) % count), ((i + 1) % count, i)]
+    return lax.ppermute(x, axis, pairs)
 
 
 def frames(bands, sectors):
@@ -577,14 +624,14 @@
             cl, sl = math.cos(lam), math.sin(lam)
             table[i, j, :3, :3] = np.array([[-sl, cl, 0.0], [-s * cl, -s * sl, c], [c * cl, c * sl, s]]) / half
             table[i, j, :, 3:6] = [c * cl, c * sl, s]
-            table[i, j, :4, 6] = [i, j, -sl, cl]
+            table[i, j, :5, 6] = [i, j, -sl, cl, 2 * (j % 2) - 1]
     return table.astype(np.float32)
 
 
 VM = pl.BlockSpec(memory_space=pltpu.VMEM)
 SM = pl.BlockSpec(memory_space=pltpu.SMEM)
 HB = pl.BlockSpec(memory_space=pltpu.HBM)
-MASKS = [pltpu.VMEM((16, BLK), jnp.int32), pltpu.SMEM((16, BLK), jnp.int32), pltpu.SemaphoreType.DMA]
+LISTS = pltpu.VMEM((8, BLK), jnp.int32)
 PAIR = pltpu.VMEM((BLK, 2 * BLK), BF16)
 
 
@@ -615,31 +662,34 @@
     cells = bg_std_grid.shape[3]
     per = slots // BLK
     grids = cells // BLK
-    table = jnp.asarray(frames(bands, sectors))
+    table = pltpu.with_memory_space_constraint(jnp.asarray(frames(bands, sectors)), pltpu.HBM)
 
     def flat(x):
-        return x.reshape(3, 1, x.shape[3])
+        return pltpu.with_memory_space_constraint(x.reshape(3, 1, x.shape[3]), pltpu.HBM)
 
     obs_in = pltpu.VMEM((3, 1, slots), F32)
     three = arr(3, slots)
-    hb, dev, var, b0, rank, frame, bounds = call(
+    hb, dev, var, b0, rank, frame, bounds, innov, bgg, corr = call(
         sort_kernel,
         "sort",
-        [SM] + [HB] * 5,
-        [arr(8, slots), three, three, three, arr(1, slots), arr(8, 8), arr(8, BLK)],
-        [obs_in] * 4 + [pltpu.SemaphoreType.DMA((5,))],
+        [SM] + [HB] * 7,
+        [arr(8, slots), three, three, three, arr(1, slots), arr(8, 8), arr(8, BLK), three]
+        + [arr(3, 1, cells), arr(3, 3)],
+        [obs_in] * 4 + [pltpu.SemaphoreType.DMA((7,))],
         10**8,
-        vmem=60 * 1024 * 1024,
-    )(tile_counts, table, flat(obs_pos), flat(innovation), flat(bg_std_obs), flat(obs_std))
+    )(
+        tile_counts, table, flat(obs_pos), flat(innovation), flat(bg_std_obs), flat(obs_std),
+        flat(bg_std_grid), pltpu.with_memory_space_constraint(channel_corr, pltpu.HBM),
+    )
 
     def exchange(block, beside, after):
-        south, north = ring(block, "lat", 1), ring(block, "lat", -1)
+        one, two = swap(block, "lon", 0, True), swap(block, "lon", 1, True)
         first = beside()
-        mid = tie(jnp.stack([south, block, north]), first)
-        west, east = ring(mid, "lon", 1), ring(mid, "lon", -1)
+        mid = tie(jnp.stack([one, block, two]), first)
+        three, four = ring(mid, "lat", 1), ring(mid, "lat", -1)
         second = after(first)
-        west, east, second = lax.optimization_barrier((west, east, second))
-        return (mid, west, east), first, second
+        three, four, second = lax.optimization_barrier((three, four, second))
+        return (mid, three, four), first, second
 
     off = per * (per - 1) // 2
 
@@ -651,10 +701,10 @@
             [
                 arr(per, 8, BLK),
                 arr(per, 3, BLK, BLK),
-                arr(1, off + BLK, dtype=jnp.int32),
+                arr(8, BLK, dtype=jnp.int32),
                 arr(per + off + UNROLL, BLK, 2 * BLK, dtype=BF16),
             ],
-            MASKS,
+            [LISTS, pltpu.SemaphoreType.DMA],
             10**9,
             [VM, VM, SM, VM],
         )(frame, hb, bounds)
@@ -665,46 +715,47 @@
             "own_times",
             [SM] + [VM] * 2,
             [arr(per, 8, BLK)],
-            [pltpu.VMEM((per, 32, 2 * BLK), BF16)],
+            [pltpu.VMEM((per, 16, 2 * BLK), BF16)],
             10**8,
         )(*filled[2:], u)[0]
 
     near0, filled, acc = exchange(hb, own_fill, lambda filled: own_times(filled, hb))
     q_own, tcol = filled[:2]
     full = 8 * per * per
-    q_near, pairs_near, pairs_cells, cache_near = call(
+    q_near, lists, long, cache_near = call(
         near_fill_kernel,
         "near_fill",
         [VM] * 6,
         [
             arr(8 * per, 8, BLK),
-            arr(1, full + BLK, dtype=jnp.int32),
-            arr(1, 9 * per * (cells // BLK) + BLK, dtype=jnp.int32),
+            arr(8, BLK, dtype=jnp.int32),
+            arr(2, 9 * per * per + BLK, dtype=jnp.int32),
             arr(min(full, KEPT) + UNROLL, BLK, 2 * BLK, dtype=BF16),
         ],
-        MASKS,
+        [LISTS, pltpu.VMEM((16, BLK), jnp.int32), pltpu.SMEM((16, BLK), jnp.int32)]
+        + [pltpu.SemaphoreType.DMA] * 2,
         10**9,
         [VM, SM, SM, VM],
     )(frame, bounds, tcol, *near0)
 
-    def near_times(halo, acc, field):
+    def near_times(halo, acc, field, last=False):
         return call(
-            near_times_kernel,
+            functools.partial(near_times_kernel, last),
             "near_times",
-            [SM] + [VM] * 11,
-            [arr(8, slots), three, three],
-            [pltpu.VMEM((8 * per, 32, 2 * BLK), BF16), pltpu.VMEM((per, 8, BLK), F32), PAIR],
+            [SM] * 2 + [VM] * 11,
+            [three] if last else [three, three, arr(4, slots)],
+            [pltpu.VMEM((8 * per, 16, 2 * BLK), BF16), pltpu.VMEM((per, 8, BLK), F32), PAIR],
             10**8,
-        )(pairs_near, channel_corr, cache_near, q_near, tcol, acc, *halo, dev, var, field)
-
-    u1, a0, b1 = near_times(near0, acc, b0)
+        )(lists, long, corr, cache_near, q_near, tcol, acc, *halo, dev, var, field)
+
+    a0, b1, u1 = near_times(near0, acc, b0)
     near1, acc, _ = exchange(u1, lambda: own_times(filled, u1), lambda acc: acc)
-    u2, a1, b2 = near_times(near1, acc, b1)
+    a1, b2, u2 = near_times(near1, acc, b1)
     near2, acc, _ = exchange(u2, lambda: own_times(filled, u2), lambda acc: acc)
-    _, a2, _ = near_times(near2, acc, b2)
+    (a2,) = near_times(near2, acc, b2, last=True)
     (packed,) = call(
-        pack_kernel, "pack", [VM] * 14, [arr(9 * per, 16, BLK)], [], 10**7
-    )(q_own, q_near, hb, u1, u2, *near0, *near1, *near2)
+        pack_kernel, "pack", [VM] * 11, [arr(9 * per, 16, BLK)], [], 10**7
+    )(q_own, q_near, *near0, *near1, *near2)
     (copies,) = call(gram_kernel, "gram", [VM] * 6, [arr(bands * sectors, 1, 16)], [], 10**6)(
         b0, b1, b2, a0, a1, a2
     )
@@ -713,7 +764,7 @@
     (parts_g,) = call(
         grid_kernel,
         "grid",
-        [SM] + [VM] * 4,
+        [SM] * 2 + [VM] * 4,
         [arr(3, 3, cells)],
         [
             pltpu.VMEM((cells // BLK, 3, BLK, BLK), F32),
@@ -721,17 +772,17 @@
             pltpu.VMEM((cells // BLK, 16, BLK), F32),
         ],
         10**9,
-    )(pairs_cells, channel_corr, frame, packed, flat(bg_std_grid))
+    )(lists, long, corr, frame, packed, bgg)
     (parts_w,) = call(unsort_kernel, "unsort", [VM] * 3, [arr(2, 3, slots)], [], 10**8)(rank, b1, b2)
     weights, increment = call(
         final_kernel,
         "final",
-        [SM] + [VM] * 4,
+        [VM] * 4,
         [arr(3, 1, slots), arr(3, 1, cells)],
         [obs_in, pltpu.VMEM((3, 1, cells), F32), pltpu.SemaphoreType.DMA((2,))],
         10**6,
         [HB, HB],
-    )(tile_counts, parts, flat(innovation), parts_w, parts_g)
+    )(parts, innov, parts_w, parts_g)
     return weights.reshape(1, 1, 3, slots), increment.reshape(1, 1, 3, cells)
 
 

time: 91.8 us -> 81 us (0.88)
  waiting for transfers between devices: 28.7 us -> 14 us
  starting transfers between devices: 29.7 us -> 37.7 us
  Pallas kernels: 29.6 us -> 27 us
  local copies, waits for them, and re-layouts: 2.19 us -> 0 us
    ppermute x12 -> x6, waiting for transfers between devices: 20.8 us -> 3.4 us  [ring(): lax.ppermute(x, axis, [(i, (i + step) % count) for i in range(count)])]
    ppermute x0 -> x6, starting transfers between devices: none -> 12.1 us  [swap(): return lax.ppermute(x, axis, pairs)]
    ppermute x12 -> x6, starting transfers between devices: 20.5 us -> 13 us  [ring(): lax.ppermute(x, axis, [(i, (i + step) % count) for i in range(count)])]
    ppermute x0 -> x6, waiting for transfers between devices: none -> 3.53 us  [swap(): return lax.ppermute(x, axis, pairs)]
    all_to_all x1, starting transfers between devices: 9.23 us -> 12.7 us  [per_device(): parts = lax.all_to_all(copies, ('lat', 'lon'), 0, 0, tiled=True)]
    unnamed x24 -> x0, local copies, waits for them, and re-layouts: 2.19 us -> none
    pallas_call x1, Pallas kernels: 5.98 us -> 4.2 us  [per_device(): call(near_fill_kernel, 'near_fill', [VM] * 6, [arr(8 * per, 8, BLK), arr(...]
  transfers between devices with their start and end apart: 13 -> 13, of which waited for: 8 -> 10; matrix products, arithmetic and copies ran while one was open for 0% -> 0% of each run, Pallas kernels for 14% -> 16%
where the time goes in v3:
time: 81 us; the launch traced here: 80.1 us
  starting transfers between devices  37.7 us (47%)
  Pallas kernels  27 us (33%)
  waiting for transfers between devices  14 us (17%)
  between operations  1.4 us (2%)
    ppermute x6, starting transfers between devices, ring(): lax.ppermute(x, axis, [(i, (i + step) % count) for i in range(count)])  13 us
    all_to_all x1, starting transfers between devices, per_device(): parts = lax.all_to_all(copies, ('lat', 'lon'), 0, 0, tiled=True)  12.7 us
    ppermute x6, starting transfers between devices, swap(): return lax.ppermute(x, axis, pairs)  12.1 us
    all_to_all x1, waiting for transfers between devices, per_device(): parts = lax.all_to_all(copies, ('lat', 'lon'), 0, 0, tiled=True)  7.04 us
    pallas_call x1, Pallas kernels, per_device(): call(grid_kernel, 'grid', [SM] * 2 + [VM] * 4, [arr(3, 3, cells)], [pltpu...  6 us
    pallas_call x3, Pallas kernels, near_times(): call(functools.partial(near_times_kernel, last), 'near_times', [SM] * 2 +...  4.95 us
    pallas_call x1, Pallas kernels, per_device(): call(near_fill_kernel, 'near_fill', [VM] * 6, [arr(8 * per, 8, BLK), arr(...  4.2 us
    pallas_call x3, Pallas kernels, own_times(): call(own_times_kernel, 'own_times', [SM] + [VM] * 2, [arr(per, 8, BLK)],...  3.89 us
  transfers between devices with their start and end apart: 13, of which 10 were waited for; matrix products, arithmetic and copies ran while one was open for 0% of the time, Pallas kernels for 16%

profile of v3, /device:TPU:1, one launch (start us, length us, event | category | flops | bytes accessed | tf_op | source)
XLA Modules:
  0.0 80.1 jit_solution(18404654861083697081)
XLA Ops:
  1.3 3.0 %sort.1 = (f32[8,1024]{1,0:T(8,128)S(1)}, f32[3,1024]{1,0:T(4,128)S(1)}, f32[3,1024]{1,0:T(4,128)S(1)}, f32[3,1024]{1,0:T(4,128)S(1)}, f32[1,1024]{1,0:T(1,128)S...) custom-call(s32[1,1]{1,0:T(1,128)S(6)} %copy.12.count, ...), custom_call_target="tpu_custom_call" | custom-call | flops 100000000 | bytes 1048576 | tf_op jit(solution)/shard_map/sort/pallas_call | solution.py:672
  4.3 5.8 %collective-permute-start.1 = (f32[8,1024]{1,0:T(8,128)S(1)}, f32[8,1024]{1,0:T(8,128)S(1)}, u32[]{:S(2)}, u32[]{:S(2)}) collective-permute-start(f32[8,1024]{1,0:T(8,128)S(1)} %get-tuple-element.43.hb.u), channel_id=1, source_target_pairs={{1,2},{2,1},{3,4},{4,3},{5,6},{6,5},{7,8},{8,7},{9,10},{10,9},{11,... | collective-permute-start | bytes 98312 | tf_op jit(solution)/shard_map/ppermute | solution.py:613
  10.2 2.7 %own_fill.1 = (f32[8,8,128]{2,1,0:T(8,128)S(1)}, f32[8,3,128,128]{3,2,1,0:T(8,128)S(1)}, s32[8,128]{1,0:T(8,128)S(1)}, bf16[44,128,256]{2,1,0:T(8,128)(2,1)S(1)}) custom-call(f32[8,8]{1,0:T(8,128)S(1)} %get-tuple-element.41.frame, f32[8,1024]{1,0:T(8,128)S(1)} %get-tuple-element.43.hb.u, f32[8,128]{1,0:T(8,128)S(1)} %get-tuple-element.42.bounds), custom_call_target="tpu_custom_call" | custom-call | flops 1000000000 | bytes 1048576 | tf_op jit(solution)/shard_map/own_fill/pallas_call | solution.py:697
  12.9 0.4 collective-permute-done
  13.2 1.8 %collective-permute-start.3 = (f32[3,8,1024]{2,1,0:T(8,128)S(1)}, f32[3,8,1024]{2,1,0:T(8,128)S(1)}, u32[]{:S(2)}, u32[]{:S(2)}) collective-permute-start(f32[3,8,1024]{2,1,0:T(8,128)S(1)} %pad_maximum_fusion.mid.um.refs_0_), channel_id=1, source_target_pairs={{0,240},{16,0},{32,16},{48,32},{64,48},{80,64},{96,80},{112,96},{1... | collective-permute-start | bytes 294920 | tf_op jit(solution)/shard_map/ppermute | solution.py:604
  15.1 2.0 %collective-permute-start.2 = (f32[3,8,1024]{2,1,0:T(8,128)S(1)}, f32[3,8,1024]{2,1,0:T(8,128)S(1)}, u32[]{:S(2)}, u32[]{:S(2)}) collective-permute-start(f32[3,8,1024]{2,1,0:T(8,128)S(1)} %pad_maximum_fusion.mid.um.refs_0_), channel_id=1, source_target_pairs={{0,16},{16,32},{32,48},{48,64},{64,80},{80,96},{96,112},{112,128},... | collective-permute-start | bytes 294920 | tf_op jit(solution)/shard_map/ppermute | solution.py:604
  17.0 1.3 %own_times.3.acc_own = f32[8,8,128]{2,1,0:T(8,128)S(1)} custom-call(s32[8,128]{1,0:T(8,128)S(1)} %get-tuple-element.46.pairs, bf16[44,128,256]{2,1,0:T(8,128)(2,1)S(1)} %get-tuple-element.47.cache, f32[8,1024]{1,0:T(8,128)S(1)} %get-tuple-element.43.hb.u), custom_call_target="tpu_custom_call" | custom-call | flops 100000000 | bytes 1048576 | tf_op jit(solution)/shard_map/own_times/pallas_call | solution.py:713
  18.4 1.0 %collective-permute-done.3.north.un.refs_2_ = f32[3,8,1024]{2,1,0:T(8,128)S(1)} collective-permute-done((f32[3,8,1024]{2,1,0:T(8,128)S(1)}, f32[3,8,1024]{2,1,0:T(8,128)S(1)}, u32[]{:S(2)}, u32[]{:S(2)}) %collective-permute-start.3) | collective-permute-done | bytes 98336 | tf_op jit(solution)/shard_map/ppermute | solution.py:604
  19.3 0.4 collective-permute-done.2.south.us.refs_1_
  19.7 4.2 %near_fill.1 = (f32[64,8,128]{2,1,0:T(8,128)S(1)}, s32[8,128]{1,0:T(8,128)S(1)}, s32[2,704]{1,0:T(2,128)S(1)}, bf16[104,128,256]{2,1,0:T(8,128)(2,1)S(1)}) custom-call(f32[8,8]{1,0:T(8,128)S(1)} %get-tuple-element.41.frame, f32[8,128]{1,0:T(8,128)S(1)} %get-tuple-element.42.bounds, f32[8,3,128,128]{3,2,1,0:T(8,128)S(1)} %get-tuple-element.44.tcol, ...), custom_call_target="tpu_custom_call" | custom-call | flops 1000000000 | bytes 1048576 | tf_op jit(solution)/shard_map/near_fill/pallas_call | solution.py:725
  23.9 1.6 %near_times.3 = (f32[3,1024]{1,0:T(4,128)S(1)}, f32[3,1024]{1,0:T(4,128)S(1)}, f32[4,1024]{1,0:T(4,128)S(1)}) custom-call(s32[8,128]{1,0:T(8,128)S(1)} %get-tuple-element.51.lists, s32[2,704]{1,0:T(2,128)S(1)} %get-tuple-element.52.long, f32[3,3]{1,0:T(4,128)S(1)} %get-tuple-element.53.corr, bf16[104,128,256]{2,1,0:T(8,128)(2,1)S(1)} %get-tuple-element.54.cache, ...), custom_call_target="tpu_custom_call" | custom-call | flops 100000000 | bytes 1048576 | tf_op jit(solution)/shard_map/near_times/pallas_call | solution.py:742
  25.6 3.1 %collective-permute-start.5 = (f32[4,1024]{1,0:T(4,128)S(1)}, f32[4,1024]{1,0:T(4,128)S(1)}, u32[]{:S(2)}, u32[]{:S(2)}) collective-permute-start(f32[4,1024]{1,0:T(4,128)S(1)} %get-tuple-element.60.u), channel_id=1, source_target_pairs={{1,2},{2,1},{3,4},{4,3},{5,6},{6,5},{7,8},{8,7},{9,10},{10,9},{11,... | collective-permute-start | bytes 49160 | tf_op jit(solution)/shard_map/ppermute | solution.py:613
  28.7 1.3 %own_times.4.acc_own = f32[8,8,128]{2,1,0:T(8,128)S(1)} custom-call(s32[8,128]{1,0:T(8,128)S(1)} %get-tuple-element.46.pairs, bf16[44,128,256]{2,1,0:T(8,128)(2,1)S(1)} %get-tuple-element.47.cache, f32[4,1024]{1,0:T(4,128)S(1)} %get-tuple-element.60.u), custom_call_target="tpu_custom_call" | custom-call | flops 100000000 | bytes 1048576 | tf_op jit(solution)/shard_map/own_times/pallas_call | solution.py:713
  30.0 1.6 %collective-permute-done.5 = f32[4,1024]{1,0:T(4,128)S(1)} collective-permute-done((f32[4,1024]{1,0:T(4,128)S(1)}, f32[4,1024]{1,0:T(4,128)S(1)}, u32[]{:S(2)}, u32[]{:S(2)}) %collective-permute-start.5) | collective-permute-done | bytes 16416 | tf_op jit(solution)/shard_map/ppermute | solution.py:613
  31.6 4.8 %collective-permute-start.7 = (f32[3,4,1024]{2,1,0:T(4,128)S(1)}, f32[3,4,1024]{2,1,0:T(4,128)S(1)}, u32[]{:S(2)}, u32[]{:S(2)}) collective-permute-start(f32[3,4,1024]{2,1,0:T(4,128)S(1)} %pad_maximum_fusion.1.um.refs_3_), channel_id=1, source_target_pairs={{0,240},{16,0},{32,16},{48,32},{64,48},{80,64},{96,80},{112,96},{1... | collective-permute-start | bytes 147464 | tf_op jit(solution)/shard_map/ppermute | solution.py:604
  36.4 0.9 %collective-permute-done.7.un.refs_5_ = f32[3,4,1024]{2,1,0:T(4,128)S(1)} collective-permute-done((f32[3,4,1024]{2,1,0:T(4,128)S(1)}, f32[3,4,1024]{2,1,0:T(4,128)S(1)}, u32[]{:S(2)}, u32[]{:S(2)}) %collective-permute-start.7) | collective-permute-done | bytes 49184 | tf_op jit(solution)/shard_map/ppermute | solution.py:604
  37.2 0.3 collective-permute-done.6.us.refs_4_
  37.6 1.7 %near_times.4 = (f32[3,1024]{1,0:T(4,128)S(1)}, f32[3,1024]{1,0:T(4,128)S(1)}, f32[4,1024]{1,0:T(4,128)S(1)}) custom-call(s32[8,128]{1,0:T(8,128)S(1)} %get-tuple-element.51.lists, s32[2,704]{1,0:T(2,128)S(1)} %get-tuple-element.52.long, f32[3,3]{1,0:T(4,128)S(1)} %get-tuple-element.53.corr, bf16[104,128,256]{2,1,0:T(8,128)(2,1)S(1)} %get-tuple-element.54.cache, ...), custom_call_target="tpu_custom_call" | custom-call | flops 100000000 | bytes 1048576 | tf_op jit(solution)/shard_map/near_times/pallas_call | solution.py:742
  39.3 3.1 %collective-permute-start.9 = (f32[4,1024]{1,0:T(4,128)S(1)}, f32[4,1024]{1,0:T(4,128)S(1)}, u32[]{:S(2)}, u32[]{:S(2)}) collective-permute-start(f32[4,1024]{1,0:T(4,128)S(1)} %get-tuple-element.67.u), channel_id=1, source_target_pairs={{1,2},{2,1},{3,4},{4,3},{5,6},{6,5},{7,8},{8,7},{9,10},{10,9},{11,... | collective-permute-start | bytes 49160 | tf_op jit(solution)/shard_map/ppermute | solution.py:613
  42.4 1.3 %own_times.5.acc_own = f32[8,8,128]{2,1,0:T(8,128)S(1)} custom-call(s32[8,128]{1,0:T(8,128)S(1)} %get-tuple-element.46.pairs, bf16[44,128,256]{2,1,0:T(8,128)(2,1)S(1)} %get-tuple-element.47.cache, f32[4,1024]{1,0:T(4,128)S(1)} %get-tuple-element.67.u), custom_call_target="tpu_custom_call" | custom-call | flops 100000000 | bytes 1048576 | tf_op jit(solution)/shard_map/own_times/pallas_call | solution.py:713
  43.7 1.5 %collective-permute-done.9 = f32[4,1024]{1,0:T(4,128)S(1)} collective-permute-done((f32[4,1024]{1,0:T(4,128)S(1)}, f32[4,1024]{1,0:T(4,128)S(1)}, u32[]{:S(2)}, u32[]{:S(2)}) %collective-permute-start.9) | collective-permute-done | bytes 16416 | tf_op jit(solution)/shard_map/ppermute | solution.py:613
  45.3 4.4 %collective-permute-start.11 = (f32[3,4,1024]{2,1,0:T(4,128)S(1)}, f32[3,4,1024]{2,1,0:T(4,128)S(1)}, u32[]{:S(2)}, u32[]{:S(2)}) collective-permute-start(f32[3,4,1024]{2,1,0:T(4,128)S(1)} %pad_maximum_fusion.2.um.refs_6_), channel_id=1, source_target_pairs={{0,240},{16,0},{32,16},{48,32},{64,48},{80,64},{96,80},{112,96},{1... | collective-permute-start | bytes 147464 | tf_op jit(solution)/shard_map/ppermute | solution.py:604
  49.7 0.4 unsort.1.w
  50.1 0.6 collective-permute-done.11.un.refs_8_
  50.8 0.2 collective-permute-done.10.us.refs_7_
  50.9 1.6 %near_times.5.a2 = f32[3,1024]{1,0:T(4,128)S(1)} custom-call(s32[8,128]{1,0:T(8,128)S(1)} %get-tuple-element.51.lists, s32[2,704]{1,0:T(2,128)S(1)} %get-tuple-element.52.long, f32[3,3]{1,0:T(4,128)S(1)} %get-tuple-element.53.corr, bf16[104,128,256]{2,1,0:T(8,128)(2,1)S(1)} %get-tuple-element.54.cache, f32[64,8,128]{2,1,0:T(8,128)S(1)} %get-tuple-element.55.q_ref.q_near, ...), custom_call_target="tpu_custom_call" | custom-call | flops 100000000 | bytes 1048576 | tf_op jit(solution)/shard_map/near_times/pallas_call | solution.py:742
  52.6 0.1 pack.1.packed
  52.7 0.8 %gram.1 = f32[256,1,16]{2,1,0:T(1,128)} custom-call(f32[3,1024]{1,0:T(4,128)S(1)} %get-tuple-element.40.field.b0, f32[3,1024]{1,0:T(4,128)S(1)} %get-tuple-element.59.field.b1, f32[3,1024]{1,0:T(4,128)S(1)} %get-tuple-element.64.field.b2, f32[3,1024]{1,0:T(4,128)S(1)} %get-tuple-element.65.a0, f32[3,1024]{1,0:T(4,128)S(1)} %get-tuple-element.66.a1, ...), custom_call_target="tpu_custom_call" | custom-call | flops 1000000 | bytes 1048576 | tf_op jit(solution)/shard_map/gram/pallas_call | solution.py:759
  53.6 12.7 %all-to-all-start = ((f32[256,1,16]{2,1,0:T(1,128)}), f32[256,1,16]{2,1,0:T(1,128)S(1)}, u32[]{:S(2)}, u32[]{:S(2)}) async-start(f32[256,1,16]{2,1,0:T(1,128)} %gram.1), calls=%async_computation | async-start | bytes 262144 | tf_op jit(solution)/shard_map/all_to_all | solution.py:763
  66.2 6.0 %grid.1.g = f32[3,3,512]{2,1,0:T(4,128)S(1)} custom-call(s32[8,128]{1,0:T(8,128)S(1)} %get-tuple-element.51.lists, s32[2,704]{1,0:T(2,128)S(1)} %get-tuple-element.52.long, f32[3,3]{1,0:T(4,128)S(1)} %get-tuple-element.53.corr, f32[8,8]{1,0:T(8,128)S(1)} %get-tuple-element.41.frame, f32[72,16,128]{2,1,0:T(8,128)S(1)} %pack.1.packed, ...), custom_call_target="tpu_custom_call" | custom-call | flops 1000000000 | bytes 1048576 | tf_op jit(solution)/shard_map/grid/pallas_call | solution.py:764
  72.2 7.0 %all-to-all-done.parts = f32[256,1,16]{2,1,0:T(1,128)S(1)} async-done(((f32[256,1,16]{2,1,0:T(1,128)}), f32[256,1,16]{2,1,0:T(1,128)S(1)}, u32[]{:S(2)}, u32[]{:S(2)}) %all-to-all-start) | async-done | bytes 16416 | tf_op jit(solution)/shard_map/all_to_all | solution.py:763
  79.3 0.8 %final.1 = (f32[3,1,1024]{2,1,0:T(1,128)}, f32[3,1,512]{2,1,0:T(1,128)}) custom-call(f32[256,1,16]{2,1,0:T(1,128)S(1)} %all-to-all-done.parts, f32[3,1024]{1,0:T(4,128)S(1)} %get-tuple-element.72.innov, f32[2,3,1024]{2,1,0:T(4,128)S(1)} %unsort.1.w, f32[3,3,512]{2,1,0:T(4,128)S(1)} %grid.1.g), custom_call_target="tpu_custom_call" | custom-call | flops 1000000 | bytes 1048576 | tf_op jit(solution)/shard_map/final/pallas_call | solution.py:777
  (11 shorter events, 0.1 us)
Async XLA Ops:
  4.3 8.5 %collective-permute-start.1 = (f32[8,1024]{1,0:T(8,128)S(1)}, f32[8,1024]{1,0:T(8,128)S(1)}, u32[]{:S(2)}, u32[]{:S(2)}) collective-permute-start(f32[8,1024]{1,0:T(8,128)S(1)} %get-tuple-element.43.hb.u), channel_id=1, source_target_pairs={{1,2},{2,1},{3,4},{4,3},{5,6},{6,5},{7,8},{8,7},{9,10},{10,9},{11,... | collective-permute-start | bytes 98312 | tf_op jit(solution)/shard_map/ppermute | solution.py:613
  10.2 3.1 %collective-permute-start = (f32[8,1024]{1,0:T(8,128)S(1)}, f32[8,1024]{1,0:T(8,128)S(1)}, u32[]{:S(2)}, u32[]{:S(2)}) collective-permute-start(f32[8,1024]{1,0:T(8,128)S(1)} %get-tuple-element.43.hb.u), channel_id=1, source_target_pairs={{0,1},{1,0},{2,3},{3,2},{4,5},{5,4},{6,7},{7,6},{8,9},{9,8},{10,11... | collective-permute-start | bytes 98312 | tf_op jit(solution)/shard_map/ppermute | solution.py:613
  13.2 6.1 %collective-permute-start.3 = (f32[3,8,1024]{2,1,0:T(8,128)S(1)}, f32[3,8,1024]{2,1,0:T(8,128)S(1)}, u32[]{:S(2)}, u32[]{:S(2)}) collective-permute-start(f32[3,8,1024]{2,1,0:T(8,128)S(1)} %pad_maximum_fusion.mid.um.refs_0_), channel_id=1, source_target_pairs={{0,240},{16,0},{32,16},{48,32},{64,48},{80,64},{96,80},{112,96},{1... | collective-permute-start | bytes 294920 | tf_op jit(solution)/shard_map/ppermute | solution.py:604
  15.1 4.7 %collective-permute-start.2 = (f32[3,8,1024]{2,1,0:T(8,128)S(1)}, f32[3,8,1024]{2,1,0:T(8,128)S(1)}, u32[]{:S(2)}, u32[]{:S(2)}) collective-permute-start(f32[3,8,1024]{2,1,0:T(8,128)S(1)} %pad_maximum_fusion.mid.um.refs_0_), channel_id=1, source_target_pairs={{0,16},{16,32},{32,48},{48,64},{64,80},{80,96},{96,112},{112,128},... | collective-permute-start | bytes 294920 | tf_op jit(solution)/shard_map/ppermute | solution.py:604
  25.6 6.0 %collective-permute-start.5 = (f32[4,1024]{1,0:T(4,128)S(1)}, f32[4,1024]{1,0:T(4,128)S(1)}, u32[]{:S(2)}, u32[]{:S(2)}) collective-permute-start(f32[4,1024]{1,0:T(4,128)S(1)} %get-tuple-element.60.u), channel_id=1, source_target_pairs={{1,2},{2,1},{3,4},{4,3},{5,6},{6,5},{7,8},{8,7},{9,10},{10,9},{11,... | collective-permute-start | bytes 49160 | tf_op jit(solution)/shard_map/ppermute | solution.py:613
  28.7 2.9 %collective-permute-start.4 = (f32[4,1024]{1,0:T(4,128)S(1)}, f32[4,1024]{1,0:T(4,128)S(1)}, u32[]{:S(2)}, u32[]{:S(2)}) collective-permute-start(f32[4,1024]{1,0:T(4,128)S(1)} %get-tuple-element.60.u), channel_id=1, source_target_pairs={{0,1},{1,0},{2,3},{3,2},{4,5},{5,4},{6,7},{7,6},{8,9},{9,8},{10,11... | collective-permute-start | bytes 49160 | tf_op jit(solution)/shard_map/ppermute | solution.py:613
  31.6 5.6 %collective-permute-start.7 = (f32[3,4,1024]{2,1,0:T(4,128)S(1)}, f32[3,4,1024]{2,1,0:T(4,128)S(1)}, u32[]{:S(2)}, u32[]{:S(2)}) collective-permute-start(f32[3,4,1024]{2,1,0:T(4,128)S(1)} %pad_maximum_fusion.1.um.refs_3_), channel_id=1, source_target_pairs={{0,240},{16,0},{32,16},{48,32},{64,48},{80,64},{96,80},{112,96},{1... | collective-permute-start | bytes 147464 | tf_op jit(solution)/shard_map/ppermute | solution.py:604
  36.4 1.2 %collective-permute-start.6 = (f32[3,4,1024]{2,1,0:T(4,128)S(1)}, f32[3,4,1024]{2,1,0:T(4,128)S(1)}, u32[]{:S(2)}, u32[]{:S(2)}) collective-permute-start(f32[3,4,1024]{2,1,0:T(4,128)S(1)} %pad_maximum_fusion.1.um.refs_3_), channel_id=1, source_target_pairs={{0,16},{16,32},{32,48},{48,64},{64,80},{80,96},{96,112},{112,128},... | collective-permute-start | bytes 147464 | tf_op jit(solution)/shard_map/ppermute | solution.py:604
  39.3 6.0 %collective-permute-start.9 = (f32[4,1024]{1,0:T(4,128)S(1)}, f32[4,1024]{1,0:T(4,128)S(1)}, u32[]{:S(2)}, u32[]{:S(2)}) collective-permute-start(f32[4,1024]{1,0:T(4,128)S(1)} %get-tuple-element.67.u), channel_id=1, source_target_pairs={{1,2},{2,1},{3,4},{4,3},{5,6},{6,5},{7,8},{8,7},{9,10},{10,9},{11,... | collective-permute-start | bytes 49160 | tf_op jit(solution)/shard_map/ppermute | solution.py:613
  42.4 2.9 %collective-permute-start.8 = (f32[4,1024]{1,0:T(4,128)S(1)}, f32[4,1024]{1,0:T(4,128)S(1)}, u32[]{:S(2)}, u32[]{:S(2)}) collective-permute-start(f32[4,1024]{1,0:T(4,128)S(1)} %get-tuple-element.67.u), channel_id=1, source_target_pairs={{0,1},{1,0},{2,3},{3,2},{4,5},{5,4},{6,7},{7,6},{8,9},{9,8},{10,11... | collective-permute-start | bytes 49160 | tf_op jit(solution)/shard_map/ppermute | solution.py:613
  45.3 5.5 %collective-permute-start.11 = (f32[3,4,1024]{2,1,0:T(4,128)S(1)}, f32[3,4,1024]{2,1,0:T(4,128)S(1)}, u32[]{:S(2)}, u32[]{:S(2)}) collective-permute-start(f32[3,4,1024]{2,1,0:T(4,128)S(1)} %pad_maximum_fusion.2.um.refs_6_), channel_id=1, source_target_pairs={{0,240},{16,0},{32,16},{48,32},{64,48},{80,64},{96,80},{112,96},{1... | collective-permute-start | bytes 147464 | tf_op jit(solution)/shard_map/ppermute | solution.py:604
  49.7 1.2 %collective-permute-start.10 = (f32[3,4,1024]{2,1,0:T(4,128)S(1)}, f32[3,4,1024]{2,1,0:T(4,128)S(1)}, u32[]{:S(2)}, u32[]{:S(2)}) collective-permute-start(f32[3,4,1024]{2,1,0:T(4,128)S(1)} %pad_maximum_fusion.2.um.refs_6_), channel_id=1, source_target_pairs={{0,16},{16,32},{32,48},{48,64},{64,80},{80,96},{96,112},{112,128},... | collective-permute-start | bytes 147464 | tf_op jit(solution)/shard_map/ppermute | solution.py:604
  53.6 25.7 %all-to-all-start = ((f32[256,1,16]{2,1,0:T(1,128)}), f32[256,1,16]{2,1,0:T(1,128)S(1)}, u32[]{:S(2)}, u32[]{:S(2)}) async-start(f32[256,1,16]{2,1,0:T(1,128)} %gram.1), calls=%async_computation | async-start | bytes 262144 | tf_op jit(solution)/shard_map/all_to_all | solution.py:763

commit v4 on v3

--- a/solution.py
+++ b/solution.py
@@ -205,7 +205,7 @@
     return rows
 
 
-def two_lists(active, source, target, regions):
+def list_of(active, source, target, regions):
     height = active.shape[0]
 
     def exact(x, y, dims):
@@ -218,15 +218,13 @@
         return lax.broadcasted_iota(jnp.int32, shape, dim)
 
     act = ones(active)
-    i, j = iota((BLK, BLK), 0), iota((BLK, BLK), 1)
-    same = ones((i >> 6) == (j >> 6))
-    ahead = ones(((i >> 6) == (j >> 6)) & (i < j))
+    ahead = ones(iota((BLK, BLK), 0) < iota((BLK, BLK), 1))
     above = ones(iota((height, height), 1) < iota((height, height), 0))
-    place = exact(act, ahead, NN) + exact(exact(above, act, NN), same, NN)
-    counts = exact(exact(jnp.ones((8, height), F32), act, NN), same, NN)[0:1]
-    lane = iota(active.shape, 1)
-    slot = jnp.where(active & (place < BLK), place + jnp.where(lane < 64, 0.0, 1.0 * BLK), -1.0)
-    index = iota((2 * BLK, BLK), 0).astype(F32)
+    rows = jnp.sum(act, axis=1, keepdims=True)
+    place = exact(act, ahead, NN) + exact(above, jnp.broadcast_to(rows, act.shape), NN)
+    count = jnp.broadcast_to(jnp.sum(rows, axis=0, keepdims=True), (1, BLK))
+    slot = jnp.where(active & (place < BLK), place, -1.0)
+    index = iota((BLK, BLK), 0).astype(F32)
     picks = jnp.concatenate([ones(index == slot[r : r + 1]) for r in range(regions)], axis=1)
     names = [
         jnp.concatenate([x[r : r + 1].astype(F32) for r in range(regions)], axis=1)
@@ -235,9 +233,33 @@
     names = jnp.concatenate(names + [jnp.zeros((6, regions * BLK), F32)], axis=0)
     found = exact(names, picks, NT)
     entries = found[0:1] * 8.0 + found[1:2]
-    return jnp.concatenate(
-        [entries[:, 0:BLK], entries[:, BLK : 2 * BLK], counts, jnp.zeros((5, BLK), F32)], axis=0
-    ).astype(jnp.int32)
+    return jnp.concatenate([entries, count, jnp.zeros((6, BLK), F32)], axis=0).astype(jnp.int32)
+
+
+def near_active(tiles, where, frame, bounds):
+    turn = 2.0 * math.pi / lax.axis_size("lon") * frame[4:5, 6:7]
+    active = active_blocks(
+        source_bounds(tiles, [(a - 1) * turn for c, a in where], 16),
+        [bounds[k : k + 1, :] for k in range(4)],
+        lax.axis_size("lat"),
+    )
+    lane = lax.broadcasted_iota(jnp.int32, active.shape, 1)
+    region = lax.broadcasted_iota(jnp.int32, active.shape, 0)
+    return active, lane, (lane & 7) + 8 * region, (lane >> 3) & 7
+
+
+def long_list(active, source, target, regions, out, mask_v, mask_s, sem):
+    mask_v[...] = jnp.where(active, source * 8 + target + 1, 0)
+    copy = pltpu.make_async_copy(mask_v, mask_s, sem)
+    copy.start()
+    copy.wait()
+
+    def step(i, k):
+        entry = mask_s[i >> 7, i & 127]
+        out[0, k] = entry - 1
+        return k + jnp.where(entry > 0, 1, 0)
+
+    lax.fori_loop(0, BLK * regions, step, 0)
 
 
 def rho_of(tcol, sx, sy, sz):
@@ -262,10 +284,14 @@
 
 
 def set_columns(targets, tcol):
+    part = lax.broadcasted_iota(jnp.int32, (24, 3 * BLK), 0)
+    lane = lax.broadcasted_iota(jnp.int32, (24, 3 * BLK), 1)
+    pick = jnp.where((part & 7) == lane // BLK, 1.0, 0.0).astype(BF16)
     for t, tile in enumerate(targets):
-        turned = jnp.transpose(tile)
+        turned = jnp.transpose(jnp.concatenate(parts_of(tile), axis=0)).astype(BF16)
+        wide = lax.dot_general(turned, pick, NN, preferred_element_type=F32)
         for k in range(3):
-            tcol[t, k] = jnp.broadcast_to(turned[:, k : k + 1], (BLK, BLK))
+            tcol[t, k] = wide[:, k * BLK : (k + 1) * BLK]
 
 
 def fill_rows(q, tcol, t, out):
@@ -281,19 +307,6 @@
     fill_rows(q_ref[entry >> 3], tcol, entry & 7, out)
 
 
-def fill_cache(count, lists, q_ref, tcol, cache, first):
-    room = cache.shape[0] - UNROLL - first
-    kept = jnp.minimum(count, room)
-
-    def fill(p, _):
-        fill_pair(lists[0, p], q_ref, tcol, cache.at[first + p])
-        return 0
-
-    lax.fori_loop(0, kept, fill, 0)
-    for k in range(UNROLL):
-        cache[first + kept + k] = jnp.zeros(cache.shape[1:], BF16)
-
-
 def parts_of(tile):
     hi = tile.astype(BF16).astype(F32)
     rest = tile - hi
@@ -317,7 +330,23 @@
     return wide[0:4] + wide[4:8]
 
 
-def own_fill_kernel(frame, hb, bounds, q_out, tcol_out, lists_out, cache_out, lists_v, sem):
+def both_ways(lists, p, slot, cache, v_ref):
+    n, t = lists[0, p] >> 3, lists[0, p] & 7
+    rho = cache[slot]
+    ahead = lax.dot_general(v_ref[n], rho, NT, preferred_element_type=F32)
+    back = lax.dot_general(v_ref[t, :, 0:BLK], rho, NN, preferred_element_type=F32)
+    return t, add_parts(ahead), n, add_parts(back[:, 0:BLK] + back[:, BLK : 2 * BLK])
+
+
+def add_both(acc, found):
+    for t, ahead, n, back in found:
+        acc[t] += ahead
+        acc[n] += back
+
+
+def own_first_kernel(
+    frame, hb, bounds, q_out, tcol_out, lists_out, cache_out, acc, v_ref, lists_v, sem
+):
     tile = hb[...]
     tiles = blocks(to_frame(tile, 3, frame[...]))
     per = len(tiles)
@@ -326,98 +355,144 @@
     )
     lane = lax.broadcasted_iota(jnp.int32, active.shape, 1)
     source, target = lane & 7, (lane >> 3) & 7
-    lists_v[...] = two_lists(active & (lane < 64) & (target < source), source, target, 1)
+    lists_v[...] = list_of(active & (lane < 64) & (target < source), source, target, 1)
     copy = pltpu.make_async_copy(lists_v, lists_out, sem)
     copy.start()
+    set_values(tile[0:4], v_ref, 0)
     for b, part in enumerate(tiles):
         q_out[b] = part
     set_columns(tiles, tcol_out)
 
-    def diagonal(b, _):
+    def fill_own(b):
         fill_pair(b * 9, q_out, tcol_out, cache_out.at[b])
+
+    def multiply_own(b):
+        acc[b] = add_parts(lax.dot_general(v_ref[b], cache_out[b], NT, preferred_element_type=F32))
+
+    def step_own(b, _):
+        multiply_own(b - 1)
+        fill_own(b)
         return 0
 
-    lax.fori_loop(0, per, diagonal, 0)
+    fill_own(0)
+    lax.fori_loop(1, per, step_own, 0)
+    multiply_own(per - 1)
     copy.wait()
-    fill_cache(lists_out[2, 0], lists_out, q_out, tcol_out, cache_out, per)
-
-
-def own_times_kernel(pairs, cache, u, acc, v_ref):
+    count = lists_out[1, 0]
+    steps = jnp.maximum((count + 1) // 2, 1)
+
+    def fill(i):
+        for p in (2 * i, 2 * i + 1):
+            fill_pair(lists_out[0, p], q_out, tcol_out, cache_out.at[per + p])
+
+    def multiply(i):
+        add_both(acc, [both_ways(lists_out, p, per + p, cache_out, v_ref) for p in (2 * i, 2 * i + 1)])
+
+    def step(i, _):
+        multiply(i - 1)
+        fill(i)
+        return 0
+
+    fill(0)
+    lax.fori_loop(1, steps, step, 0)
+    for k in range(UNROLL):
+        cache_out[per + count + k] = jnp.zeros(cache_out.shape[1:], BF16)
+    multiply(steps - 1)
+
+
+def own_times_kernel(lists, cache, u, acc, v_ref):
     set_values(u[0:4, :], v_ref, 0)
     per = acc.shape[0]
     for b in range(per):
         acc[b] = add_parts(lax.dot_general(v_ref[b], cache[b], NT, preferred_element_type=F32))
-    count = pairs[2, 0]
+    half = UNROLL // 2
 
     def group(i, _):
-        outs = []
-        for k in range(UNROLL // 2):
-            p = i * (UNROLL // 2) + k
-            n, t = pairs[0, p] >> 3, pairs[0, p] & 7
-            rho = cache[per + p]
-            ahead = lax.dot_general(v_ref[n], rho, NT, preferred_element_type=F32)
-            back = lax.dot_general(v_ref[t, :, 0:BLK], rho, NN, preferred_element_type=F32)
-            outs.append((ahead, back[:, 0:BLK] + back[:, BLK : 2 * BLK]))
-        for k in range(UNROLL // 2):
-            p = i * (UNROLL // 2) + k
-            n, t = pairs[0, p] >> 3, pairs[0, p] & 7
-            acc[t] += add_parts(outs[k][0])
-            acc[n] += add_parts(outs[k][1])
+        places = [i * half + k for k in range(half)]
+        add_both(acc, [both_ways(lists, p, per + p, cache, v_ref) for p in places])
         return 0
 
-    half = UNROLL // 2
-    lax.fori_loop(0, (count + half - 1) // half, group, 0)
+    lax.fori_loop(0, (lists[1, 0] + half - 1) // half, group, 0)
 
 
 OTHERS = [(0, 0), (0, 2), (1, 0), (1, 1), (1, 2), (2, 0), (2, 1), (2, 2)]
 
 
-def near_fill_kernel(
-    frame, bounds, tcol, mid, south, north,
-    q_out, lists_out, long_out, cache_out, lists_v, mask_v, mask_s, sem, sem_long,
+def near_first_kernel(
+    frame, bounds, corr, tcol, mid, three, four, acc_own, dev, var, field,
+    q_out, lists_out, long_out, cache_out, img_out, nxt_out, u_out,
+    v_ref, acc, pair, lists_v, mask_v, mask_s, sem, sem_long,
 ):
-    halo = (mid, south, north)
+    halo = (mid, three, four)
     per = mid.shape[2] // BLK
-    turn = 2.0 * math.pi / lax.axis_size("lon") * frame[4:5, 6:7]
-    where = [(0, 1)] + OTHERS
-    regions = len(where)
-    tiles = [halo[c][a] for c, a in where]
-    active = active_blocks(
-        source_bounds(tiles, [(a - 1) * turn for c, a in where], 16),
-        [bounds[k : k + 1, :] for k in range(4)],
-        lax.axis_size("lat"),
-    )
-    lane = lax.broadcasted_iota(jnp.int32, active.shape, 1)
-    region = lax.broadcasted_iota(jnp.int32, active.shape, 0)
-    active = active & ((lane >= 64) | (region > 0))
-    source = (lane & 7) + 8 * jnp.where(lane < 64, region - 1, region)
-    target = (lane >> 3) & 7
-    lists_v[...] = two_lists(active, source, target, regions)
+    turned = frame[...]
+    tiles = [halo[c][a] for c, a in OTHERS]
+    regions = len(tiles)
+    active, lane, source, target = near_active(tiles, OTHERS, turned, bounds)
+    active = active & (lane < 64)
+    lists_v[...] = list_of(active, source, target, regions)
     copy = pltpu.make_async_copy(lists_v, lists_out, sem)
     copy.start()
-    turned = frame[...]
-    for r in range(1, regions):
+    for r in range(regions):
         for b, part in enumerate(blocks(to_frame(tiles[r], 3, turned))):
-            q_out[(r - 1) * per + b] = part
-    mask_v[...] = jnp.where(active, source * 8 + target + 1, 0)
+            q_out[r * per + b] = part
+        set_values(tiles[r][0:4], v_ref, r * per)
+    acc[...] = acc_own[...]
     copy.wait()
-    count, count_cells = lists_out[2, 0], lists_out[2, 64]
-
-    @pl.when((count > KEPT) | (count_cells > KEPT))
+    count = lists_out[1, 0]
+
+    @pl.when(count > KEPT)
     def _():
-        again = pltpu.make_async_copy(mask_v, mask_s, sem_long)
-        again.start()
-        again.wait()
-        for half in range(2):
-
-            def step(i, k, half=half):
-                entry = mask_s[i >> 6, 64 * half + (i & 63)]
-                long_out[half, k] = entry - 1
-                return k + jnp.where(entry > 0, 1, 0)
-
-            lax.fori_loop(0, 64 * regions, step, 0)
-
-    fill_cache(count, lists_out, q_out, tcol, cache_out, 0)
+        long_list(active, source, target, regions, long_out, mask_v, mask_s, sem_long)
+
+    kept = jnp.minimum(count, cache_out.shape[0] - UNROLL)
+    steps = jnp.maximum((kept + 1) // 2, 1)
+
+    def fill(i):
+        for p in (2 * i, 2 * i + 1):
+            fill_pair(lists_out[0, p], q_out, tcol, cache_out.at[p])
+
+    def multiply(i):
+        found = []
+        for p in (2 * i, 2 * i + 1):
+            n = lists_out[0, p] >> 3
+            found.append(lax.dot_general(v_ref[n], cache_out[p], NT, preferred_element_type=F32))
+        for k in range(2):
+            acc[lists_out[0, 2 * i + k] & 7] += add_parts(found[k])
+
+    def step(i, _):
+        multiply(i - 1)
+        fill(i)
+        return 0
+
+    fill(0)
+    lax.fori_loop(1, steps, step, 0)
+    for k in range(UNROLL):
+        cache_out[kept + k] = jnp.zeros(cache_out.shape[1:], BF16)
+    multiply(steps - 1)
+    extra_pairs(kept, count, long_out, q_out, tcol, v_ref, acc, pair)
+    field = field[...]
+    dev = dev[...]
+    image = dev * mix(corr, total_of(acc)) + var[...] * field
+    give_next(image, field, dev, img_out, nxt_out, u_out)
+
+
+def cells_list_kernel(
+    frame, bounds, mid, three, four, lists_out, long_out, lists_v, mask_v, mask_s, sem, sem_long
+):
+    halo = (mid, three, four)
+    where = [(0, 1)] + OTHERS
+    tiles = [halo[c][a] for c, a in where]
+    active, lane, source, target = near_active(tiles, where, frame[...], bounds)
+    active = active & (lane >= 64)
+    lists_v[...] = list_of(active, source, target, len(where))
+    copy = pltpu.make_async_copy(lists_v, lists_out, sem)
+    copy.start()
+    copy.wait()
+
+    @pl.when(lists_out[1, 0] > KEPT)
+    def _():
+        long_list(active, source, target, len(where), long_out, mask_v, mask_s, sem_long)
 
 
 def mix(corr, total):
@@ -428,16 +503,35 @@
     return out
 
 
+def extra_pairs(kept, count, long, q_ref, tcol, v_ref, acc, pair):
+    def extra(p, _):
+        entry = long[0, p]
+        fill_pair(entry, q_ref, tcol, pair)
+        out = lax.dot_general(v_ref[entry >> 3], pair[...], NT, preferred_element_type=F32)
+        acc[entry & 7] += add_parts(out)
+        return 0
+
+    lax.fori_loop(kept, count, extra, 0)
+
+
+def give_next(image, field, dev, img_out, nxt_out, u_out):
+    nxt = image - SHIFT * field
+    img_out[...] = image
+    nxt_out[...] = nxt
+    u_out[...] = jnp.concatenate([dev * nxt, jnp.zeros((1, nxt.shape[1]), F32)], axis=0)
+
+
 def near_times_kernel(
     last, lists, long, corr, cache, q_ref, tcol, acc_own, um, us, un, dev, var, field, *refs
 ):
-    outs, (v_ref, acc, pair) = refs[:-3], refs[-3:]
+    refs, (v_ref, acc, pair) = refs[:-3], refs[-3:]
+    outs = refs[-1:] if last else refs
     halo = (um, us, un)
     per = acc.shape[0]
     for k, (c, a) in enumerate(OTHERS):
         set_values(halo[c][a, 0:4, :], v_ref, k * per)
     acc[...] = acc_own[...]
-    count = lists[2, 0]
+    count = lists[1, 0]
     kept = jnp.minimum(count, cache.shape[0] - UNROLL)
 
     def group(i, _):
@@ -452,29 +546,22 @@
 
     lax.fori_loop(0, (kept + UNROLL - 1) // UNROLL, group, 0)
 
-    def extra(p, _):
-        entry = long[0, p]
-        fill_pair(entry, q_ref, tcol, pair)
-        out = lax.dot_general(v_ref[entry >> 3], pair[...], NT, preferred_element_type=F32)
-        acc[entry & 7] += add_parts(out)
-        return 0
-
-    lax.fori_loop(kept, count, extra, 0)
+    extra_pairs(kept, count, long, q_ref, tcol, v_ref, acc, pair)
     field = field[...]
     dev = dev[...]
     image = dev * mix(corr, total_of(acc)) + var[...] * field
-    outs[0][...] = image
-    if not last:
-        nxt = image - SHIFT * field
-        outs[1][...] = nxt
-        outs[2][...] = jnp.concatenate([dev * nxt, jnp.zeros((1, nxt.shape[1]), F32)], axis=0)
-
-
-def gram_kernel(b0, b1, b2, a0, a1, a2, out):
+    if last:
+        b0, b1, a0, a1 = [ref[...] for ref in refs[:4]]
+        sums_out(b0, b1, field, a0, a1, image, outs[0])
+    else:
+        give_next(image, field, dev, *outs)
+
+
+def sums_out(b0, b1, b2, a0, a1, a2, out):
     pairs = [(b0, a0), (b0, a1), (b0, a2), (b1, a1), (b1, a2), (b2, a2), (b0, b0), (b1, b0), (b2, b0)]
     rows = []
     for x, y in pairs:
-        prod = blocks(x[...] * y[...])
+        prod = blocks(x * y)
         while len(prod) > 1:
             prod = [prod[k] + prod[k + 1] for k in range(0, len(prod), 2)]
         rows.append(jnp.sum(prod[0], axis=0, keepdims=True))
@@ -519,7 +606,7 @@
     point = jnp.where(row == 2, sinlat, point)
     set_columns(blocks(to_frame(point, 0, frame[...])), tcol)
     acc[...] = jnp.zeros(acc.shape, F32)
-    count = lists[2, 64]
+    count = lists[1, 0]
     short = jnp.minimum(count, KEPT)
 
     def one(entry, weight, out):
@@ -535,15 +622,15 @@
         for k in range(GROUP):
             p = i * GROUP + k
             weight = jnp.where(p < short, 1.0, 0.0).astype(F32)
-            found.append(one(lists[1, p], weight, rho.at[k]))
+            found.append(one(lists[0, p], weight, rho.at[k]))
         for k in range(GROUP):
-            acc[lists[1, i * GROUP + k] & 7] += found[k]
+            acc[lists[0, i * GROUP + k] & 7] += found[k]
         return 0
 
     lax.fori_loop(0, (short + GROUP - 1) // GROUP, group, 0)
 
     def extra(p, _):
-        entry = long[1, p]
+        entry = long[0, p]
         acc[entry & 7] += one(entry, 1.0, rho.at[0])
         return 0
 
@@ -599,17 +686,11 @@
         copy.wait()
 
 
-def ring(x, axis, step):
-    count = lax.axis_size(axis)
-    return lax.ppermute(x, axis, [(i, (i + step) % count) for i in range(count)])
-
-
-def swap(x, axis, first, wrap):
+def swap(x, axis, first):
     count = lax.axis_size(axis)
     pairs = []
     for i in range(first, count, 2):
-        if i + 1 < count or wrap:
-            pairs += [(i, (i + 1) % count), ((i + 1) % count, i)]
+        pairs += [(i, (i + 1) % count), ((i + 1) % count, i)]
     return lax.ppermute(x, axis, pairs)
 
 
@@ -683,30 +764,31 @@
     )
 
     def exchange(block, beside, after):
-        one, two = swap(block, "lon", 0, True), swap(block, "lon", 1, True)
+        one, two = swap(block, "lon", 0), swap(block, "lon", 1)
         first = beside()
         mid = tie(jnp.stack([one, block, two]), first)
-        three, four = ring(mid, "lat", 1), ring(mid, "lat", -1)
+        three, four = swap(mid, "lat", 0), swap(mid, "lat", 1)
         second = after(first)
         three, four, second = lax.optimization_barrier((three, four, second))
         return (mid, three, four), first, second
 
     off = per * (per - 1) // 2
 
-    def own_fill():
+    def own_first():
         return call(
-            own_fill_kernel,
-            "own_fill",
+            own_first_kernel,
+            "own_first",
             [VM] * 3,
             [
                 arr(per, 8, BLK),
                 arr(per, 3, BLK, BLK),
                 arr(8, BLK, dtype=jnp.int32),
                 arr(per + off + UNROLL, BLK, 2 * BLK, dtype=BF16),
+                arr(per, 8, BLK),
             ],
-            [LISTS, pltpu.SemaphoreType.DMA],
+            [pltpu.VMEM((per, 16, 2 * BLK), BF16), LISTS, pltpu.SemaphoreType.DMA],
             10**9,
-            [VM, VM, SM, VM],
+            [VM, VM, SM, VM, VM],
         )(frame, hb, bounds)
 
     def own_times(filled, u):
@@ -717,48 +799,65 @@
             [arr(per, 8, BLK)],
             [pltpu.VMEM((per, 16, 2 * BLK), BF16)],
             10**8,
-        )(*filled[2:], u)[0]
-
-    near0, filled, acc = exchange(hb, own_fill, lambda filled: own_times(filled, hb))
+        )(*filled[2:4], u)[0]
+
+    near0, filled, _ = exchange(hb, own_first, lambda filled: filled[4])
     q_own, tcol = filled[:2]
     full = 8 * per * per
-    q_near, lists, long, cache_near = call(
-        near_fill_kernel,
-        "near_fill",
-        [VM] * 6,
+    long_scratch = [LISTS, pltpu.VMEM((16, BLK), jnp.int32), pltpu.SMEM((16, BLK), jnp.int32)]
+    long_scratch += [pltpu.SemaphoreType.DMA] * 2
+    near_scratch = [
+        pltpu.VMEM((8 * per, 16, 2 * BLK), BF16),
+        pltpu.VMEM((per, 8, BLK), F32),
+        PAIR,
+    ]
+    next_outs = [three, three, arr(4, slots)]
+    q_near, lists, long, cache_near, a0, b1, u1 = call(
+        near_first_kernel,
+        "near_first",
+        [VM] * 11,
         [
             arr(8 * per, 8, BLK),
             arr(8, BLK, dtype=jnp.int32),
-            arr(2, 9 * per * per + BLK, dtype=jnp.int32),
+            arr(1, 10 * BLK, dtype=jnp.int32),
             arr(min(full, KEPT) + UNROLL, BLK, 2 * BLK, dtype=BF16),
-        ],
-        [LISTS, pltpu.VMEM((16, BLK), jnp.int32), pltpu.SMEM((16, BLK), jnp.int32)]
-        + [pltpu.SemaphoreType.DMA] * 2,
+        ]
+        + next_outs,
+        near_scratch + long_scratch,
         10**9,
-        [VM, SM, SM, VM],
-    )(frame, bounds, tcol, *near0)
-
-    def near_times(halo, acc, field, last=False):
+        [VM, SM, SM, VM, VM, VM, VM],
+    )(frame, bounds, corr, tcol, *near0, filled[4], dev, var, b0)
+
+    def near_times(halo, acc, field, *earlier):
+        last = len(earlier) > 0
+        outs = [arr(bands * sectors, 1, 16)] if last else next_outs
         return call(
             functools.partial(near_times_kernel, last),
             "near_times",
-            [SM] * 2 + [VM] * 11,
-            [three] if last else [three, three, arr(4, slots)],
-            [pltpu.VMEM((8 * per, 16, 2 * BLK), BF16), pltpu.VMEM((per, 8, BLK), F32), PAIR],
+            [SM] * 2 + [VM] * (11 + len(earlier)),
+            outs,
+            near_scratch,
             10**8,
-        )(lists, long, corr, cache_near, q_near, tcol, acc, *halo, dev, var, field)
-
-    a0, b1, u1 = near_times(near0, acc, b0)
-    near1, acc, _ = exchange(u1, lambda: own_times(filled, u1), lambda acc: acc)
+        )(lists, long, corr, cache_near, q_near, tcol, acc, *halo, dev, var, field, *earlier)
+
+    def list_cells(_):
+        return call(
+            cells_list_kernel,
+            "cells_list",
+            [VM] * 5,
+            [arr(8, BLK, dtype=jnp.int32), arr(1, 10 * BLK, dtype=jnp.int32)],
+            long_scratch,
+            10**8,
+            [SM, SM],
+        )(frame, bounds, *near0)
+
+    near1, acc, cells_lists = exchange(u1, lambda: own_times(filled, u1), list_cells)
     a1, b2, u2 = near_times(near1, acc, b1)
     near2, acc, _ = exchange(u2, lambda: own_times(filled, u2), lambda acc: acc)
-    (a2,) = near_times(near2, acc, b2, last=True)
+    (copies,) = near_times(near2, acc, b2, b0, b1, a0, a1)
     (packed,) = call(
         pack_kernel, "pack", [VM] * 11, [arr(9 * per, 16, BLK)], [], 10**7
     )(q_own, q_near, *near0, *near1, *near2)
-    (copies,) = call(gram_kernel, "gram", [VM] * 6, [arr(bands * sectors, 1, 16)], [], 10**6)(
-        b0, b1, b2, a0, a1, a2
-    )
     copies, packed = lax.optimization_barrier((copies, packed))
     parts = lax.all_to_all(copies, ("lat", "lon"), 0, 0, tiled=True)
     (parts_g,) = call(
@@ -772,7 +871,7 @@
             pltpu.VMEM((cells // BLK, 16, BLK), F32),
         ],
         10**9,
-    )(lists, long, corr, frame, packed, bgg)
+    )(*cells_lists, corr, frame, packed, bgg)
     (parts_w,) = call(unsort_kernel, "unsort", [VM] * 3, [arr(2, 3, slots)], [], 10**8)(rank, b1, b2)
     weights, increment = call(
         final_kernel,

time: 81 us -> 78.2 us (0.965)
  waiting for transfers between devices: 14 us -> 12.7 us
  Pallas kernels: 27 us -> 26 us
    ppermute x6 -> x0, starting transfers between devices: 13 us -> none  [ring(): lax.ppermute(x, axis, [(i, (i + step) % count) for i in range(count)])]
    ppermute x6 -> x12, starting transfers between devices: 12.1 us -> 24.6 us  [swap(): return lax.ppermute(x, axis, pairs)]
    ppermute x6 -> x0, waiting for transfers between devices: 3.4 us -> none  [ring(): lax.ppermute(x, axis, [(i, (i + step) % count) for i in range(count)])]
    ppermute x6 -> x12, waiting for transfers between devices: 3.53 us -> 5.49 us  [swap(): return lax.ppermute(x, axis, pairs)]
    pallas_call x3 -> x2, Pallas kernels: 3.89 us -> 2.59 us  [own_times(): call(own_times_kernel, 'own_times', [SM] + [VM] * 2, [arr(per, 8, BLK)],...]
    pallas_call x3, Pallas kernels: 7.73 us -> 8.95 us  [the longest x1 4.03 us: per_device(): call(near_first_kernel, 'near_first', [VM] * 11, [arr(8 * per, 8, BLK), a...]
    pallas_call x3 -> x2, Pallas kernels: 4.95 us -> 4.13 us  [near_times(): call(functools.partial(near_times_kernel, last), 'near_times', [SM] * 2 +...]
  transfers between devices with their start and end apart: 13 -> 13, of which waited for: 10 -> 5; matrix products, arithmetic and copies ran while one was open for 0% -> 0% of each run, Pallas kernels for 16% -> 18%
where the time goes in v4:
time: 78.2 us; the launch traced here: 78 us
  starting transfers between devices  38 us (49%)
  Pallas kernels  26 us (33%)
  waiting for transfers between devices  12.7 us (16%)
  between operations  1.42 us (2%)
    ppermute x12, starting transfers between devices, swap(): return lax.ppermute(x, axis, pairs)  24.6 us
    all_to_all x1, starting transfers between devices, per_device(): parts = lax.all_to_all(copies, ('lat', 'lon'), 0, 0, tiled=True)  13.4 us
    all_to_all x1, waiting for transfers between devices, per_device(): parts = lax.all_to_all(copies, ('lat', 'lon'), 0, 0, tiled=True)  7.18 us
    pallas_call x1, Pallas kernels, per_device(): call(grid_kernel, 'grid', [SM] * 2 + [VM] * 4, [arr(3, 3, cells)], [pltpu...  5.86 us
    ppermute x12, waiting for transfers between devices, swap(): return lax.ppermute(x, axis, pairs)  5.49 us
    pallas_call x2, Pallas kernels, near_times(): call(functools.partial(near_times_kernel, last), 'near_times', [SM] * 2 +...  4.13 us
    pallas_call x1, Pallas kernels, per_device(): call(near_first_kernel, 'near_first', [VM] * 11, [arr(8 * per, 8, BLK), a...  4.03 us
    pallas_call x1, Pallas kernels, per_device(): call(sort_kernel, 'sort', [SM] + [HB] * 7, [arr(8, slots), three, three,...  3.05 us
  transfers between devices with their start and end apart: 13, of which 5 were waited for; matrix products, arithmetic and copies ran while one was open for 0% of the time, Pallas kernels for 18%

profile of v4, /device:TPU:1, one launch (start us, length us, event | category | flops | bytes accessed | tf_op | source)
XLA Modules:
  0.0 78.0 jit_solution(18038971710698966361)
XLA Ops:
  1.3 3.0 %sort.1 = (f32[8,1024]{1,0:T(8,128)S(1)}, f32[3,1024]{1,0:T(4,128)S(1)}, f32[3,1024]{1,0:T(4,128)S(1)}, f32[3,1024]{1,0:T(4,128)S(1)}, f32[1,1024]{1,0:T(1,128)S...) custom-call(s32[1,1]{1,0:T(1,128)S(6)} %copy.12.count, ...), custom_call_target="tpu_custom_call" | custom-call | flops 100000000 | bytes 1048576 | tf_op jit(solution)/shard_map/sort/pallas_call | solution.py:753
  4.3 5.8 %collective-permute-start.1 = (f32[8,1024]{1,0:T(8,128)S(1)}, f32[8,1024]{1,0:T(8,128)S(1)}, u32[]{:S(2)}, u32[]{:S(2)}) collective-permute-start(f32[8,1024]{1,0:T(8,128)S(1)} %get-tuple-element.47.hb), channel_id=1, source_target_pairs={{1,2},{2,1},{3,4},{4,3},{5,6},{6,5},{7,8},{8,7},{9,10},{10,9},{11,... | collective-permute-start | bytes 98312 | tf_op jit(solution)/shard_map/ppermute | solution.py:694
  10.2 0.0 collective-permute-start
  10.2 3.0 %own_first.1 = (f32[8,8,128]{2,1,0:T(8,128)S(1)}, f32[8,3,128,128]{3,2,1,0:T(8,128)S(1)}, s32[8,128]{1,0:T(8,128)S(1)}, bf16[44,128,256]{2,1,0:T(8,128)(2,1)S(1)}, f32[8,8,128]{2,1,0:T(8,128)S(1)}) custom-call(f32[8,8]{1,0:T(8,128)S(1)} %get-tuple-element.44.frame, f32[8,1024]{1,0:T(8,128)S(1)} %get-tuple-element.47.hb, f32[8,128]{1,0:T(8,128)S(1)} %get-tuple-element.45.bounds), custom_call_target="tpu_custom_call" | custom-call | flops 1000000000 | bytes 1048576 | tf_op jit(solution)/shard_map/own_first/pallas_call | solution.py:778
  13.2 0.0 collective-permute-done
  13.3 3.4 %collective-permute-start.3 = (f32[3,8,1024]{2,1,0:T(8,128)S(1)}, f32[3,8,1024]{2,1,0:T(8,128)S(1)}, u32[]{:S(2)}, u32[]{:S(2)}) collective-permute-start(f32[3,8,1024]{2,1,0:T(8,128)S(1)} %pad_maximum_fusion.mid.refs_0_), channel_id=1, source_target_pairs={{16,32},{32,16},{48,64},{64,48},{80,96},{96,80},{112,128},{128,112... | collective-permute-start | bytes 294920 | tf_op jit(solution)/shard_map/ppermute | solution.py:694
  16.7 2.7 %collective-permute-start.2 = (f32[3,8,1024]{2,1,0:T(8,128)S(1)}, f32[3,8,1024]{2,1,0:T(8,128)S(1)}, u32[]{:S(2)}, u32[]{:S(2)}) collective-permute-start(f32[3,8,1024]{2,1,0:T(8,128)S(1)} %pad_maximum_fusion.mid.refs_0_), channel_id=1, source_target_pairs={{0,16},{16,0},{32,48},{48,32},{64,80},{80,64},{96,112},{112,96},{1... | collective-permute-start | bytes 294920 | tf_op jit(solution)/shard_map/ppermute | solution.py:694
  19.3 0.9 %collective-permute-done.2.three.refs_1_ = f32[3,8,1024]{2,1,0:T(8,128)S(1)} collective-permute-done((f32[3,8,1024]{2,1,0:T(8,128)S(1)}, f32[3,8,1024]{2,1,0:T(8,128)S(1)}, u32[]{:S(2)}, u32[]{:S(2)}) %collective-permute-start.2) | collective-permute-done | bytes 98336 | tf_op jit(solution)/shard_map/ppermute | solution.py:694
  20.3 4.0 %near_first.1 = (f32[64,8,128]{2,1,0:T(8,128)S(1)}, s32[8,128]{1,0:T(8,128)S(1)}, s32[1,1280]{1,0:T(1,128)S(1)}, bf16[104,128,256]{2,1,0:T(8,128)(2,1)S(1)}, f32...) custom-call(f32[8,8]{1,0:T(8,128)S(1)} %get-tuple-element.44.frame, ...), custom_call_target="tpu_custom_call" | custom-call | flops 1000000000 | bytes 1048576 | tf_op jit(solution)/shard_map/near_first/pallas_call | solution.py:815
  24.3 2.8 %collective-permute-start.5 = (f32[4,1024]{1,0:T(4,128)S(1)}, f32[4,1024]{1,0:T(4,128)S(1)}, u32[]{:S(2)}, u32[]{:S(2)}) collective-permute-start(f32[4,1024]{1,0:T(4,128)S(1)} %get-tuple-element.63.u), channel_id=1, source_target_pairs={{1,2},{2,1},{3,4},{4,3},{5,6},{6,5},{7,8},{8,7},{9,10},{10,9},{11,... | collective-permute-start | bytes 49160 | tf_op jit(solution)/shard_map/ppermute | solution.py:694
  27.1 1.3 %own_times.2.acc_own = f32[8,8,128]{2,1,0:T(8,128)S(1)} custom-call(s32[8,128]{1,0:T(8,128)S(1)} %get-tuple-element.50.lists, bf16[44,128,256]{2,1,0:T(8,128)(2,1)S(1)} %get-tuple-element.51.cache, f32[4,1024]{1,0:T(4,128)S(1)} %get-tuple-element.63.u), custom_call_target="tpu_custom_call" | custom-call | flops 100000000 | bytes 1048576 | tf_op jit(solution)/shard_map/own_times/pallas_call | solution.py:795
  28.4 1.9 %collective-permute-done.5 = f32[4,1024]{1,0:T(4,128)S(1)} collective-permute-done((f32[4,1024]{1,0:T(4,128)S(1)}, f32[4,1024]{1,0:T(4,128)S(1)}, u32[]{:S(2)}, u32[]{:S(2)}) %collective-permute-start.5) | collective-permute-done | bytes 16416 | tf_op jit(solution)/shard_map/ppermute | solution.py:694
  30.3 0.0 collective-permute-done.4
  30.3 1.4 %collective-permute-start.7 = (f32[3,4,1024]{2,1,0:T(4,128)S(1)}, f32[3,4,1024]{2,1,0:T(4,128)S(1)}, u32[]{:S(2)}, u32[]{:S(2)}) collective-permute-start(f32[3,4,1024]{2,1,0:T(4,128)S(1)} %pad_maximum_fusion.1.um.refs_3_), channel_id=1, source_target_pairs={{16,32},{32,16},{48,64},{64,48},{80,96},{96,80},{112,128},{128,112... | collective-permute-start | bytes 147464 | tf_op jit(solution)/shard_map/ppermute | solution.py:694
  31.7 2.2 %collective-permute-start.6 = (f32[3,4,1024]{2,1,0:T(4,128)S(1)}, f32[3,4,1024]{2,1,0:T(4,128)S(1)}, u32[]{:S(2)}, u32[]{:S(2)}) collective-permute-start(f32[3,4,1024]{2,1,0:T(4,128)S(1)} %pad_maximum_fusion.1.um.refs_3_), channel_id=1, source_target_pairs={{0,16},{16,0},{32,48},{48,32},{64,80},{80,64},{96,112},{112,96},{1... | collective-permute-start | bytes 147464 | tf_op jit(solution)/shard_map/ppermute | solution.py:694
  33.9 1.9 %cells_list.1 = (s32[8,128]{1,0:T(8,128)S(1)}, s32[1,1280]{1,0:T(1,128)S(1)}) custom-call(f32[8,8]{1,0:T(8,128)S(1)} %get-tuple-element.44.frame, f32[8,128]{1,0:T(8,128)S(1)} %get-tuple-element.45.bounds, f32[3,8,1024]{2,1,0:T(8,128)S(1)} %pad_maximum_fusion.mid.refs_0_, f32[3,8,1024]{2,1,0:T(8,128)S(1)} %collective-permute-done.2.three.refs_1_, ...), custom_call_target="tpu_custom_call" | custom-call | flops 100000000 | bytes 1048576 | tf_op jit(solution)/shard_map/cells_list/pallas_call | solution.py:844
  35.8 0.0 collective-permute-done.7.un.refs_5_
  35.8 1.7 %near_times.2 = (f32[3,1024]{1,0:T(4,128)S(1)}, f32[3,1024]{1,0:T(4,128)S(1)}, f32[4,1024]{1,0:T(4,128)S(1)}) custom-call(s32[8,128]{1,0:T(8,128)S(1)} %get-tuple-element.59.lists, s32[1,1280]{1,0:T(1,128)S(1)} %get-tuple-element.60.long, f32[3,3]{1,0:T(4,128)S(1)} %get-tuple-element.46.corr, bf16[104,128,256]{2,1,0:T(8,128)(2,1)S(1)} %get-tuple-element.61.cache, ...), custom_call_target="tpu_custom_call" | custom-call | flops 100000000 | bytes 1048576 | tf_op jit(solution)/shard_map/near_times/pallas_call | solution.py:834
  37.5 3.4 %collective-permute-start.9 = (f32[4,1024]{1,0:T(4,128)S(1)}, f32[4,1024]{1,0:T(4,128)S(1)}, u32[]{:S(2)}, u32[]{:S(2)}) collective-permute-start(f32[4,1024]{1,0:T(4,128)S(1)} %get-tuple-element.70.u), channel_id=1, source_target_pairs={{1,2},{2,1},{3,4},{4,3},{5,6},{6,5},{7,8},{8,7},{9,10},{10,9},{11,... | collective-permute-start | bytes 49160 | tf_op jit(solution)/shard_map/ppermute | solution.py:694
  40.9 1.3 %own_times.3.acc_own = f32[8,8,128]{2,1,0:T(8,128)S(1)} custom-call(s32[8,128]{1,0:T(8,128)S(1)} %get-tuple-element.50.lists, bf16[44,128,256]{2,1,0:T(8,128)(2,1)S(1)} %get-tuple-element.51.cache, f32[4,1024]{1,0:T(4,128)S(1)} %get-tuple-element.70.u), custom_call_target="tpu_custom_call" | custom-call | flops 100000000 | bytes 1048576 | tf_op jit(solution)/shard_map/own_times/pallas_call | solution.py:795
  42.2 1.3 %collective-permute-done.9 = f32[4,1024]{1,0:T(4,128)S(1)} collective-permute-done((f32[4,1024]{1,0:T(4,128)S(1)}, f32[4,1024]{1,0:T(4,128)S(1)}, u32[]{:S(2)}, u32[]{:S(2)}) %collective-permute-start.9) | collective-permute-done | bytes 16416 | tf_op jit(solution)/shard_map/ppermute | solution.py:694
  43.5 0.0 collective-permute-done.8
  43.5 2.9 %collective-permute-start.11 = (f32[3,4,1024]{2,1,0:T(4,128)S(1)}, f32[3,4,1024]{2,1,0:T(4,128)S(1)}, u32[]{:S(2)}, u32[]{:S(2)}) collective-permute-start(f32[3,4,1024]{2,1,0:T(4,128)S(1)} %pad_maximum_fusion.2.um.refs_6_), channel_id=1, source_target_pairs={{16,32},{32,16},{48,64},{64,48},{80,96},{96,80},{112,128},{128,112... | collective-permute-start | bytes 147464 | tf_op jit(solution)/shard_map/ppermute | solution.py:694
  46.4 0.0 collective-permute-start.10
  46.4 0.4 unsort.1.w
  46.9 1.3 %collective-permute-done.11.un.refs_8_ = f32[3,4,1024]{2,1,0:T(4,128)S(1)} collective-permute-done((f32[3,4,1024]{2,1,0:T(4,128)S(1)}, f32[3,4,1024]{2,1,0:T(4,128)S(1)}, u32[]{:S(2)}, u32[]{:S(2)}) %collective-permute-start.11) | collective-permute-done | bytes 49184 | tf_op jit(solution)/shard_map/ppermute | solution.py:694
  48.2 0.1 pack.1.packed
  48.3 2.5 %near_times.3 = f32[256,1,16]{2,1,0:T(1,128)} custom-call(s32[8,128]{1,0:T(8,128)S(1)} %get-tuple-element.59.lists, s32[1,1280]{1,0:T(1,128)S(1)} %get-tuple-element.60.long, f32[3,3]{1,0:T(4,128)S(1)} %get-tuple-element.46.corr, bf16[104,128,256]{2,1,0:T(8,128)(2,1)S(1)} %get-tuple-element.61.cache, f32[64,8,128]{2,1,0:T(8,128)S(1)} %get-tuple-element.62.q_ref.q_near, ...), custom_call_target="tpu_custom_call" | custom-call | flops 100000000 | bytes 1048576 | tf_op jit(solution)/shard_map/near_times/pallas_call | solution.py:834
  50.8 13.4 %all-to-all-start = ((f32[256,1,16]{2,1,0:T(1,128)}), f32[256,1,16]{2,1,0:T(1,128)S(1)}, u32[]{:S(2)}, u32[]{:S(2)}) async-start(f32[256,1,16]{2,1,0:T(1,128)} %near_times.3), calls=%async_computation | async-start | bytes 262144 | tf_op jit(solution)/shard_map/all_to_all | solution.py:862
  64.2 5.9 %grid.1.g = f32[3,3,512]{2,1,0:T(4,128)S(1)} custom-call(s32[8,128]{1,0:T(8,128)S(1)} %get-tuple-element.80.lists, s32[1,1280]{1,0:T(1,128)S(1)} %get-tuple-element.81.long, f32[3,3]{1,0:T(4,128)S(1)} %get-tuple-element.46.corr, f32[8,8]{1,0:T(8,128)S(1)} %get-tuple-element.44.frame, f32[72,16,128]{2,1,0:T(8,128)S(1)} %pack.1.packed, ...), custom_call_target="tpu_custom_call" | custom-call | flops 1000000000 | bytes 1048576 | tf_op jit(solution)/shard_map/grid/pallas_call | solution.py:863
  70.0 7.2 %all-to-all-done.parts = f32[256,1,16]{2,1,0:T(1,128)S(1)} async-done(((f32[256,1,16]{2,1,0:T(1,128)}), f32[256,1,16]{2,1,0:T(1,128)S(1)}, u32[]{:S(2)}, u32[]{:S(2)}) %all-to-all-start) | async-done | bytes 16416 | tf_op jit(solution)/shard_map/all_to_all | solution.py:862
  77.2 0.8 %final.1 = (f32[3,1,1024]{2,1,0:T(1,128)}, f32[3,1,512]{2,1,0:T(1,128)}) custom-call(f32[256,1,16]{2,1,0:T(1,128)S(1)} %all-to-all-done.parts, f32[3,1024]{1,0:T(4,128)S(1)} %get-tuple-element.78.innov, f32[2,3,1024]{2,1,0:T(4,128)S(1)} %unsort.1.w, f32[3,3,512]{2,1,0:T(4,128)S(1)} %grid.1.g), custom_call_target="tpu_custom_call" | custom-call | flops 1000000 | bytes 1048576 | tf_op jit(solution)/shard_map/final/pallas_call | solution.py:876
  (9 shorter events, 0.0 us)
Async XLA Ops:
  4.3 8.9 %collective-permute-start.1 = (f32[8,1024]{1,0:T(8,128)S(1)}, f32[8,1024]{1,0:T(8,128)S(1)}, u32[]{:S(2)}, u32[]{:S(2)}) collective-permute-start(f32[8,1024]{1,0:T(8,128)S(1)} %get-tuple-element.47.hb), channel_id=1, source_target_pairs={{1,2},{2,1},{3,4},{4,3},{5,6},{6,5},{7,8},{8,7},{9,10},{10,9},{11,... | collective-permute-start | bytes 98312 | tf_op jit(solution)/shard_map/ppermute | solution.py:694
  10.2 3.1 %collective-permute-start = (f32[8,1024]{1,0:T(8,128)S(1)}, f32[8,1024]{1,0:T(8,128)S(1)}, u32[]{:S(2)}, u32[]{:S(2)}) collective-permute-start(f32[8,1024]{1,0:T(8,128)S(1)} %get-tuple-element.47.hb), channel_id=1, source_target_pairs={{0,1},{1,0},{2,3},{3,2},{4,5},{5,4},{6,7},{7,6},{8,9},{9,8},{10,11... | collective-permute-start | bytes 98312 | tf_op jit(solution)/shard_map/ppermute | solution.py:694
  13.3 6.1 %collective-permute-start.3 = (f32[3,8,1024]{2,1,0:T(8,128)S(1)}, f32[3,8,1024]{2,1,0:T(8,128)S(1)}, u32[]{:S(2)}, u32[]{:S(2)}) collective-permute-start(f32[3,8,1024]{2,1,0:T(8,128)S(1)} %pad_maximum_fusion.mid.refs_0_), channel_id=1, source_target_pairs={{16,32},{32,16},{48,64},{64,48},{80,96},{96,80},{112,128},{128,112... | collective-permute-start | bytes 294920 | tf_op jit(solution)/shard_map/ppermute | solution.py:694
  16.7 3.6 %collective-permute-start.2 = (f32[3,8,1024]{2,1,0:T(8,128)S(1)}, f32[3,8,1024]{2,1,0:T(8,128)S(1)}, u32[]{:S(2)}, u32[]{:S(2)}) collective-permute-start(f32[3,8,1024]{2,1,0:T(8,128)S(1)} %pad_maximum_fusion.mid.refs_0_), channel_id=1, source_target_pairs={{0,16},{16,0},{32,48},{48,32},{64,80},{80,64},{96,112},{112,96},{1... | collective-permute-start | bytes 294920 | tf_op jit(solution)/shard_map/ppermute | solution.py:694
  24.3 6.0 %collective-permute-start.5 = (f32[4,1024]{1,0:T(4,128)S(1)}, f32[4,1024]{1,0:T(4,128)S(1)}, u32[]{:S(2)}, u32[]{:S(2)}) collective-permute-start(f32[4,1024]{1,0:T(4,128)S(1)} %get-tuple-element.63.u), channel_id=1, source_target_pairs={{1,2},{2,1},{3,4},{4,3},{5,6},{6,5},{7,8},{8,7},{9,10},{10,9},{11,... | collective-permute-start | bytes 49160 | tf_op jit(solution)/shard_map/ppermute | solution.py:694
  27.1 3.2 %collective-permute-start.4 = (f32[4,1024]{1,0:T(4,128)S(1)}, f32[4,1024]{1,0:T(4,128)S(1)}, u32[]{:S(2)}, u32[]{:S(2)}) collective-permute-start(f32[4,1024]{1,0:T(4,128)S(1)} %get-tuple-element.63.u), channel_id=1, source_target_pairs={{0,1},{1,0},{2,3},{3,2},{4,5},{5,4},{6,7},{7,6},{8,9},{9,8},{10,11... | collective-permute-start | bytes 49160 | tf_op jit(solution)/shard_map/ppermute | solution.py:694
  30.3 5.5 %collective-permute-start.7 = (f32[3,4,1024]{2,1,0:T(4,128)S(1)}, f32[3,4,1024]{2,1,0:T(4,128)S(1)}, u32[]{:S(2)}, u32[]{:S(2)}) collective-permute-start(f32[3,4,1024]{2,1,0:T(4,128)S(1)} %pad_maximum_fusion.1.um.refs_3_), channel_id=1, source_target_pairs={{16,32},{32,16},{48,64},{64,48},{80,96},{96,80},{112,128},{128,112... | collective-permute-start | bytes 147464 | tf_op jit(solution)/shard_map/ppermute | solution.py:694
  31.7 4.1 %collective-permute-start.6 = (f32[3,4,1024]{2,1,0:T(4,128)S(1)}, f32[3,4,1024]{2,1,0:T(4,128)S(1)}, u32[]{:S(2)}, u32[]{:S(2)}) collective-permute-start(f32[3,4,1024]{2,1,0:T(4,128)S(1)} %pad_maximum_fusion.1.um.refs_3_), channel_id=1, source_target_pairs={{0,16},{16,0},{32,48},{48,32},{64,80},{80,64},{96,112},{112,96},{1... | collective-permute-start | bytes 147464 | tf_op jit(solution)/shard_map/ppermute | solution.py:694
  37.5 6.0 %collective-permute-start.9 = (f32[4,1024]{1,0:T(4,128)S(1)}, f32[4,1024]{1,0:T(4,128)S(1)}, u32[]{:S(2)}, u32[]{:S(2)}) collective-permute-start(f32[4,1024]{1,0:T(4,128)S(1)} %get-tuple-element.70.u), channel_id=1, source_target_pairs={{1,2},{2,1},{3,4},{4,3},{5,6},{6,5},{7,8},{8,7},{9,10},{10,9},{11,... | collective-permute-start | bytes 49160 | tf_op jit(solution)/shard_map/ppermute | solution.py:694
  40.9 2.6 %collective-permute-start.8 = (f32[4,1024]{1,0:T(4,128)S(1)}, f32[4,1024]{1,0:T(4,128)S(1)}, u32[]{:S(2)}, u32[]{:S(2)}) collective-permute-start(f32[4,1024]{1,0:T(4,128)S(1)} %get-tuple-element.70.u), channel_id=1, source_target_pairs={{0,1},{1,0},{2,3},{3,2},{4,5},{5,4},{6,7},{7,6},{8,9},{9,8},{10,11... | collective-permute-start | bytes 49160 | tf_op jit(solution)/shard_map/ppermute | solution.py:694
  43.5 4.7 %collective-permute-start.11 = (f32[3,4,1024]{2,1,0:T(4,128)S(1)}, f32[3,4,1024]{2,1,0:T(4,128)S(1)}, u32[]{:S(2)}, u32[]{:S(2)}) collective-permute-start(f32[3,4,1024]{2,1,0:T(4,128)S(1)} %pad_maximum_fusion.2.um.refs_6_), channel_id=1, source_target_pairs={{16,32},{32,16},{48,64},{64,48},{80,96},{96,80},{112,128},{128,112... | collective-permute-start | bytes 147464 | tf_op jit(solution)/shard_map/ppermute | solution.py:694
  46.4 1.8 %collective-permute-start.10 = (f32[3,4,1024]{2,1,0:T(4,128)S(1)}, f32[3,4,1024]{2,1,0:T(4,128)S(1)}, u32[]{:S(2)}, u32[]{:S(2)}) collective-permute-start(f32[3,4,1024]{2,1,0:T(4,128)S(1)} %pad_maximum_fusion.2.um.refs_6_), channel_id=1, source_target_pairs={{0,16},{16,0},{32,48},{48,32},{64,80},{80,64},{96,112},{112,96},{1... | collective-permute-start | bytes 147464 | tf_op jit(solution)/shard_map/ppermute | solution.py:694
  50.8 26.4 %all-to-all-start = ((f32[256,1,16]{2,1,0:T(1,128)}), f32[256,1,16]{2,1,0:T(1,128)S(1)}, u32[]{:S(2)}, u32[]{:S(2)}) async-start(f32[256,1,16]{2,1,0:T(1,128)} %near_times.3), calls=%async_computation | async-start | bytes 262144 | tf_op jit(solution)/shard_map/all_to_all | solution.py:862

commit v5 on v4

--- a/solution.py
+++ b/solution.py
@@ -23,6 +23,7 @@
 ROWS = 32
 GROUP = 4
 KEPT = 96
+EARLY = 14
 CELLS = 512
 
 
@@ -344,8 +345,32 @@
         acc[n] += back
 
 
+def own_pairs(lists, first, count, slot, q, tcol, cache, v_ref, acc):
+    steps = jnp.maximum((count + 1) // 2, 1)
+
+    def fill(i):
+        for p in (2 * i, 2 * i + 1):
+            fill_pair(lists[0, first + p], q, tcol, cache.at[slot + p])
+
+    def multiply(i):
+        add_both(
+            acc, [both_ways(lists, first + p, slot + p, cache, v_ref) for p in (2 * i, 2 * i + 1)]
+        )
+
+    def step(i, _):
+        multiply(i - 1)
+        fill(i)
+        return 0
+
+    fill(0)
+    lax.fori_loop(1, steps, step, 0)
+    for k in range(UNROLL):
+        cache[slot + count + k] = jnp.zeros(cache.shape[1:], BF16)
+    multiply(steps - 1)
+
+
 def own_first_kernel(
-    frame, hb, bounds, q_out, tcol_out, lists_out, cache_out, acc, v_ref, lists_v, sem
+    frame, hb, bounds, q_out, tcol_out, lists_out, cache_out, v_ref, acc, lists_v, sem
 ):
     tile = hb[...]
     tiles = blocks(to_frame(tile, 3, frame[...]))
@@ -378,41 +403,34 @@
     lax.fori_loop(1, per, step_own, 0)
     multiply_own(per - 1)
     copy.wait()
-    count = lists_out[1, 0]
-    steps = jnp.maximum((count + 1) // 2, 1)
-
-    def fill(i):
-        for p in (2 * i, 2 * i + 1):
-            fill_pair(lists_out[0, p], q_out, tcol_out, cache_out.at[per + p])
-
-    def multiply(i):
-        add_both(acc, [both_ways(lists_out, p, per + p, cache_out, v_ref) for p in (2 * i, 2 * i + 1)])
-
-    def step(i, _):
-        multiply(i - 1)
-        fill(i)
-        return 0
-
-    fill(0)
-    lax.fori_loop(1, steps, step, 0)
-    for k in range(UNROLL):
-        cache_out[per + count + k] = jnp.zeros(cache_out.shape[1:], BF16)
-    multiply(steps - 1)
-
-
-def own_times_kernel(lists, cache, u, acc, v_ref):
+    count = jnp.minimum(lists_out[1, 0], EARLY)
+    own_pairs(lists_out, 0, count, per, q_out, tcol_out, cache_out, v_ref, acc)
+
+
+def own_second_kernel(lists, q, tcol, v_ref, acc_in, cache_out, acc):
+    acc[...] = acc_in[...]
+    count = jnp.maximum(lists[1, 0] - EARLY, 0)
+    own_pairs(lists, EARLY, count, 0, q, tcol, cache_out, v_ref, acc)
+
+
+def own_times_kernel(lists, cache, cache_late, u, acc, v_ref):
     set_values(u[0:4, :], v_ref, 0)
     per = acc.shape[0]
     for b in range(per):
         acc[b] = add_parts(lax.dot_general(v_ref[b], cache[b], NT, preferred_element_type=F32))
     half = UNROLL // 2
 
-    def group(i, _):
-        places = [i * half + k for k in range(half)]
-        add_both(acc, [both_ways(lists, p, per + p, cache, v_ref) for p in places])
-        return 0
-
-    lax.fori_loop(0, (lists[1, 0] + half - 1) // half, group, 0)
+    def apply(ref, first, count, slot):
+        def group(i, _):
+            places = [i * half + k for k in range(half)]
+            add_both(acc, [both_ways(lists, first + p, slot + p, ref, v_ref) for p in places])
+            return 0
+
+        lax.fori_loop(0, (count + half - 1) // half, group, 0)
+
+    count = lists[1, 0]
+    apply(cache, 0, jnp.minimum(count, EARLY), per)
+    apply(cache_late, EARLY, jnp.maximum(count - EARLY, 0), 0)
 
 
 OTHERS = [(0, 0), (0, 2), (1, 0), (1, 1), (1, 2), (2, 0), (2, 1), (2, 2)]
@@ -783,25 +801,36 @@
                 arr(per, 8, BLK),
                 arr(per, 3, BLK, BLK),
                 arr(8, BLK, dtype=jnp.int32),
-                arr(per + off + UNROLL, BLK, 2 * BLK, dtype=BF16),
+                arr(per + EARLY + UNROLL, BLK, 2 * BLK, dtype=BF16),
+                arr(per, 16, 2 * BLK, dtype=BF16),
                 arr(per, 8, BLK),
             ],
-            [pltpu.VMEM((per, 16, 2 * BLK), BF16), LISTS, pltpu.SemaphoreType.DMA],
+            [LISTS, pltpu.SemaphoreType.DMA],
             10**9,
-            [VM, VM, SM, VM, VM],
+            [VM, VM, SM, VM, VM, VM],
         )(frame, hb, bounds)
 
-    def own_times(filled, u):
+    def own_second(filled):
+        return call(
+            own_second_kernel,
+            "own_second",
+            [SM] + [VM] * 4,
+            [arr(off - EARLY + UNROLL, BLK, 2 * BLK, dtype=BF16), arr(per, 8, BLK)],
+            [],
+            10**9,
+        )(filled[2], filled[0], filled[1], filled[4], filled[5])
+
+    def own_times(u):
         return call(
             own_times_kernel,
             "own_times",
-            [SM] + [VM] * 2,
+            [SM] + [VM] * 3,
             [arr(per, 8, BLK)],
             [pltpu.VMEM((per, 16, 2 * BLK), BF16)],
             10**8,
-        )(*filled[2:4], u)[0]
-
-    near0, filled, _ = exchange(hb, own_first, lambda filled: filled[4])
+        )(*filled[2:4], late[0], u)[0]
+
+    near0, filled, late = exchange(hb, own_first, own_second)
     q_own, tcol = filled[:2]
     full = 8 * per * per
     long_scratch = [LISTS, pltpu.VMEM((16, BLK), jnp.int32), pltpu.SMEM((16, BLK), jnp.int32)]
@@ -826,7 +855,7 @@
         near_scratch + long_scratch,
         10**9,
         [VM, SM, SM, VM, VM, VM, VM],
-    )(frame, bounds, corr, tcol, *near0, filled[4], dev, var, b0)
+    )(frame, bounds, corr, tcol, *near0, late[1], dev, var, b0)
 
     def near_times(halo, acc, field, *earlier):
         last = len(earlier) > 0
@@ -851,9 +880,9 @@
             [SM, SM],
         )(frame, bounds, *near0)
 
-    near1, acc, cells_lists = exchange(u1, lambda: own_times(filled, u1), list_cells)
+    near1, acc, cells_lists = exchange(u1, lambda: own_times(u1), list_cells)
     a1, b2, u2 = near_times(near1, acc, b1)
-    near2, acc, _ = exchange(u2, lambda: own_times(filled, u2), lambda acc: acc)
+    near2, acc, _ = exchange(u2, lambda: own_times(u2), lambda acc: acc)
     (copies,) = near_times(near2, acc, b2, b0, b1, a0, a1)
     (packed,) = call(
         pack_kernel, "pack", [VM] * 11, [arr(9 * per, 16, BLK)], [], 10**7

time: 78.2 us -> 78.7 us (level)
  starting transfers between devices: 38 us -> 39.5 us
  waiting for transfers between devices: 12.7 us -> 11.3 us
    ppermute x12, waiting for transfers between devices: 5.49 us -> 3.61 us  [swap(): return lax.ppermute(x, axis, pairs)]
    all_to_all x1, starting transfers between devices: 13.4 us -> 14.8 us  [per_device(): parts = lax.all_to_all(copies, ('lat', 'lon'), 0, 0, tiled=True)]
    pallas_call x2 -> x3, Pallas kernels: 2.59 us -> 3.59 us  [the longest x2 2.61 us: own_times(): call(own_times_kernel, 'own_times', [SM] + [VM] * 3, [arr(per, 8, BLK)],...]
where the time goes in v5:
time: 78.7 us; the launch traced here: 78.6 us
  starting transfers between devices  39.5 us (50%)
  Pallas kernels  26.1 us (33%)
  waiting for transfers between devices  11.3 us (14%)
  between operations  1.59 us (2%)
    ppermute x12, starting transfers between devices, swap(): return lax.ppermute(x, axis, pairs)  24.7 us
    all_to_all x1, starting transfers between devices, per_device(): parts = lax.all_to_all(copies, ('lat', 'lon'), 0, 0, tiled=True)  14.8 us
    all_to_all x1, waiting for transfers between devices, per_device(): parts = lax.all_to_all(copies, ('lat', 'lon'), 0, 0, tiled=True)  7.72 us
    pallas_call x1, Pallas kernels, per_device(): call(grid_kernel, 'grid', [SM] * 2 + [VM] * 4, [arr(3, 3, cells)], [pltpu...  5.34 us
    pallas_call x2, Pallas kernels, near_times(): call(functools.partial(near_times_kernel, last), 'near_times', [SM] * 2 +...  4.13 us
    pallas_call x1, Pallas kernels, per_device(): call(near_first_kernel, 'near_first', [VM] * 11, [arr(8 * per, 8, BLK), a...  3.7 us
    ppermute x12, waiting for transfers between devices, swap(): return lax.ppermute(x, axis, pairs)  3.61 us
    pallas_call x1, Pallas kernels, per_device(): call(sort_kernel, 'sort', [SM] + [HB] * 7, [arr(8, slots), three, three,...  3.05 us
  transfers between devices with their start and end apart: 13, of which 5 were waited for; matrix products, arithmetic and copies ran while one was open for 0% of the time, Pallas kernels for 18%

profile of v5, /device:TPU:1, one launch (start us, length us, event | category | flops | bytes accessed | tf_op | source)
XLA Modules:
  0.0 78.6 jit_solution(15699407559298874578)
XLA Ops:
  1.3 3.0 %sort.1 = (f32[8,1024]{1,0:T(8,128)S(1)}, f32[3,1024]{1,0:T(4,128)S(1)}, f32[3,1024]{1,0:T(4,128)S(1)}, f32[3,1024]{1,0:T(4,128)S(1)}, f32[1,1024]{1,0:T(1,128)S...) custom-call(s32[1,1]{1,0:T(1,128)S(6)} %copy.12.count, ...), custom_call_target="tpu_custom_call" | custom-call | flops 100000000 | bytes 1048576 | tf_op jit(solution)/shard_map/sort/pallas_call | solution.py:771
  4.3 5.8 %collective-permute-start.1 = (f32[8,1024]{1,0:T(8,128)S(1)}, f32[8,1024]{1,0:T(8,128)S(1)}, u32[]{:S(2)}, u32[]{:S(2)}) collective-permute-start(f32[8,1024]{1,0:T(8,128)S(1)} %get-tuple-element.52.hb), channel_id=1, source_target_pairs={{1,2},{2,1},{3,4},{4,3},{5,6},{6,5},{7,8},{8,7},{9,10},{10,9},{11,... | collective-permute-start | bytes 98312 | tf_op jit(solution)/shard_map/ppermute | solution.py:712
  10.2 3.0 %own_first.1 = (f32[8,8,128]{2,1,0:T(8,128)S(1)}, f32[8,3,128,128]{3,2,1,0:T(8,128)S(1)}, s32[8,128]{1,0:T(8,128)S(1)}, bf16[30,128,256]{2,1,0:T(8,128)(2,1)S(1)...) custom-call(f32[8,8]{1,0:T(8,128)S(1)} %get-tuple-element.49.frame, f32[8,1024]{1,0:T(8,128)S(1)} %get-tuple-element.52.hb, ...), custom_call_target="tpu_custom_call" | custom-call | flops 1000000000 | bytes 1048576 | tf_op jit(solution)/shard_map/own_first/pallas_call | solution.py:796
  13.2 0.0 collective-permute-done
  13.3 3.4 %collective-permute-start.3 = (f32[3,8,1024]{2,1,0:T(8,128)S(1)}, f32[3,8,1024]{2,1,0:T(8,128)S(1)}, u32[]{:S(2)}, u32[]{:S(2)}) collective-permute-start(f32[3,8,1024]{2,1,0:T(8,128)S(1)} %pad_maximum_fusion.mid.refs_0_), channel_id=1, source_target_pairs={{16,32},{32,16},{48,64},{64,48},{80,96},{96,80},{112,128},{128,112... | collective-permute-start | bytes 294920 | tf_op jit(solution)/shard_map/ppermute | solution.py:712
  16.7 2.7 %collective-permute-start.2 = (f32[3,8,1024]{2,1,0:T(8,128)S(1)}, f32[3,8,1024]{2,1,0:T(8,128)S(1)}, u32[]{:S(2)}, u32[]{:S(2)}) collective-permute-start(f32[3,8,1024]{2,1,0:T(8,128)S(1)} %pad_maximum_fusion.mid.refs_0_), channel_id=1, source_target_pairs={{0,16},{16,0},{32,48},{48,32},{64,80},{80,64},{96,112},{112,96},{1... | collective-permute-start | bytes 294920 | tf_op jit(solution)/shard_map/ppermute | solution.py:712
  19.3 1.0 %own_second.1 = (bf16[22,128,256]{2,1,0:T(8,128)(2,1)S(1)}, f32[8,8,128]{2,1,0:T(8,128)S(1)}) custom-call(s32[8,128]{1,0:T(8,128)S(1)} %get-tuple-element.55.lists, f32[8,8,128]{2,1,0:T(8,128)S(1)} %get-tuple-element.54.q.q_own, f32[8,3,128,128]{3,2,1,0:T(8,128)S(1)} %get-tuple-element.53.tcol, bf16[8,16,256]{2,1,0:T(8,128)(2,1)S(1)} %get-tuple-element.57.v_ref, ...), custom_call_target="tpu_custom_call" | custom-call | flops 1000000000 | bytes 1048576 | tf_op jit(solution)/shard_map/own_second/pallas_call | solution.py:814
  20.3 0.0 collective-permute-done.3.four.refs_2_
  20.3 0.0 collective-permute-done.2.three.refs_1_
  20.3 3.7 %near_first.1 = (f32[64,8,128]{2,1,0:T(8,128)S(1)}, s32[8,128]{1,0:T(8,128)S(1)}, s32[1,1280]{1,0:T(1,128)S(1)}, bf16[104,128,256]{2,1,0:T(8,128)(2,1)S(1)}, f32...) custom-call(f32[8,8]{1,0:T(8,128)S(1)} %get-tuple-element.49.frame, ...), custom_call_target="tpu_custom_call" | custom-call | flops 1000000000 | bytes 1048576 | tf_op jit(solution)/shard_map/near_first/pallas_call | solution.py:844
  24.0 3.4 %collective-permute-start.5 = (f32[4,1024]{1,0:T(4,128)S(1)}, f32[4,1024]{1,0:T(4,128)S(1)}, u32[]{:S(2)}, u32[]{:S(2)}) collective-permute-start(f32[4,1024]{1,0:T(4,128)S(1)} %get-tuple-element.73.u), channel_id=1, source_target_pairs={{1,2},{2,1},{3,4},{4,3},{5,6},{6,5},{7,8},{8,7},{9,10},{10,9},{11,... | collective-permute-start | bytes 49160 | tf_op jit(solution)/shard_map/ppermute | solution.py:712
  27.5 0.1 collective-permute-start.4
  27.5 1.3 %own_times.2.acc_own = f32[8,8,128]{2,1,0:T(8,128)S(1)} custom-call(s32[8,128]{1,0:T(8,128)S(1)} %get-tuple-element.55.lists, bf16[30,128,256]{2,1,0:T(8,128)(2,1)S(1)} %get-tuple-element.56.cache, bf16[22,128,256]{2,1,0:T(8,128)(2,1)S(1)} %get-tuple-element.72.cache_late, f32[4,1024]{1,0:T(4,128)S(1)} %get-tuple-element.73.u), custom_call_target="tpu_custom_call" | custom-call | flops 100000000 | bytes 1048576 | tf_op jit(solution)/shard_map/own_times/pallas_call | solution.py:824
  28.9 1.2 %collective-permute-done.5 = f32[4,1024]{1,0:T(4,128)S(1)} collective-permute-done((f32[4,1024]{1,0:T(4,128)S(1)}, f32[4,1024]{1,0:T(4,128)S(1)}, u32[]{:S(2)}, u32[]{:S(2)}) %collective-permute-start.5) | collective-permute-done | bytes 16416 | tf_op jit(solution)/shard_map/ppermute | solution.py:712
  30.0 0.3 collective-permute-done.4
  30.4 2.0 %collective-permute-start.7 = (f32[3,4,1024]{2,1,0:T(4,128)S(1)}, f32[3,4,1024]{2,1,0:T(4,128)S(1)}, u32[]{:S(2)}, u32[]{:S(2)}) collective-permute-start(f32[3,4,1024]{2,1,0:T(4,128)S(1)} %pad_maximum_fusion.1.um.refs_3_), channel_id=1, source_target_pairs={{16,32},{32,16},{48,64},{64,48},{80,96},{96,80},{112,128},{128,112... | collective-permute-start | bytes 147464 | tf_op jit(solution)/shard_map/ppermute | solution.py:712
  32.3 1.6 %collective-permute-start.6 = (f32[3,4,1024]{2,1,0:T(4,128)S(1)}, f32[3,4,1024]{2,1,0:T(4,128)S(1)}, u32[]{:S(2)}, u32[]{:S(2)}) collective-permute-start(f32[3,4,1024]{2,1,0:T(4,128)S(1)} %pad_maximum_fusion.1.um.refs_3_), channel_id=1, source_target_pairs={{0,16},{16,0},{32,48},{48,32},{64,80},{80,64},{96,112},{112,96},{1... | collective-permute-start | bytes 147464 | tf_op jit(solution)/shard_map/ppermute | solution.py:712
  33.9 1.9 %cells_list.1 = (s32[8,128]{1,0:T(8,128)S(1)}, s32[1,1280]{1,0:T(1,128)S(1)}) custom-call(f32[8,8]{1,0:T(8,128)S(1)} %get-tuple-element.49.frame, f32[8,128]{1,0:T(8,128)S(1)} %get-tuple-element.50.bounds, f32[3,8,1024]{2,1,0:T(8,128)S(1)} %pad_maximum_fusion.mid.refs_0_, f32[3,8,1024]{2,1,0:T(8,128)S(1)} %collective-permute-done.2.three.refs_1_, ...), custom_call_target="tpu_custom_call" | custom-call | flops 100000000 | bytes 1048576 | tf_op jit(solution)/shard_map/cells_list/pallas_call | solution.py:873
  35.8 1.7 %near_times.2 = (f32[3,1024]{1,0:T(4,128)S(1)}, f32[3,1024]{1,0:T(4,128)S(1)}, f32[4,1024]{1,0:T(4,128)S(1)}) custom-call(s32[8,128]{1,0:T(8,128)S(1)} %get-tuple-element.68.lists, s32[1,1280]{1,0:T(1,128)S(1)} %get-tuple-element.69.long, f32[3,3]{1,0:T(4,128)S(1)} %get-tuple-element.51.corr, bf16[104,128,256]{2,1,0:T(8,128)(2,1)S(1)} %get-tuple-element.70.cache, ...), custom_call_target="tpu_custom_call" | custom-call | flops 100000000 | bytes 1048576 | tf_op jit(solution)/shard_map/near_times/pallas_call | solution.py:863
  37.5 3.1 %collective-permute-start.9 = (f32[4,1024]{1,0:T(4,128)S(1)}, f32[4,1024]{1,0:T(4,128)S(1)}, u32[]{:S(2)}, u32[]{:S(2)}) collective-permute-start(f32[4,1024]{1,0:T(4,128)S(1)} %get-tuple-element.80.u), channel_id=1, source_target_pairs={{1,2},{2,1},{3,4},{4,3},{5,6},{6,5},{7,8},{8,7},{9,10},{10,9},{11,... | collective-permute-start | bytes 49160 | tf_op jit(solution)/shard_map/ppermute | solution.py:712
  40.6 1.3 %own_times.3.acc_own = f32[8,8,128]{2,1,0:T(8,128)S(1)} custom-call(s32[8,128]{1,0:T(8,128)S(1)} %get-tuple-element.55.lists, bf16[30,128,256]{2,1,0:T(8,128)(2,1)S(1)} %get-tuple-element.56.cache, bf16[22,128,256]{2,1,0:T(8,128)(2,1)S(1)} %get-tuple-element.72.cache_late, f32[4,1024]{1,0:T(4,128)S(1)} %get-tuple-element.80.u), custom_call_target="tpu_custom_call" | custom-call | flops 100000000 | bytes 1048576 | tf_op jit(solution)/shard_map/own_times/pallas_call | solution.py:824
  41.9 1.6 %collective-permute-done.9 = f32[4,1024]{1,0:T(4,128)S(1)} collective-permute-done((f32[4,1024]{1,0:T(4,128)S(1)}, f32[4,1024]{1,0:T(4,128)S(1)}, u32[]{:S(2)}, u32[]{:S(2)}) %collective-permute-start.9) | collective-permute-done | bytes 16416 | tf_op jit(solution)/shard_map/ppermute | solution.py:712
  43.5 1.7 %collective-permute-start.11 = (f32[3,4,1024]{2,1,0:T(4,128)S(1)}, f32[3,4,1024]{2,1,0:T(4,128)S(1)}, u32[]{:S(2)}, u32[]{:S(2)}) collective-permute-start(f32[3,4,1024]{2,1,0:T(4,128)S(1)} %pad_maximum_fusion.2.um.refs_6_), channel_id=1, source_target_pairs={{16,32},{32,16},{48,64},{64,48},{80,96},{96,80},{112,128},{128,112... | collective-permute-start | bytes 147464 | tf_op jit(solution)/shard_map/ppermute | solution.py:712
  45.2 0.9 %collective-permute-start.10 = (f32[3,4,1024]{2,1,0:T(4,128)S(1)}, f32[3,4,1024]{2,1,0:T(4,128)S(1)}, u32[]{:S(2)}, u32[]{:S(2)}) collective-permute-start(f32[3,4,1024]{2,1,0:T(4,128)S(1)} %pad_maximum_fusion.2.um.refs_6_), channel_id=1, source_target_pairs={{0,16},{16,0},{32,48},{48,32},{64,80},{80,64},{96,112},{112,96},{1... | collective-permute-start | bytes 147464 | tf_op jit(solution)/shard_map/ppermute | solution.py:712
  46.1 0.4 unsort.1.w
  46.6 0.5 collective-permute-done.11.un.refs_8_
  47.1 0.1 pack.1.packed
  47.2 2.5 %near_times.3 = f32[256,1,16]{2,1,0:T(1,128)} custom-call(s32[8,128]{1,0:T(8,128)S(1)} %get-tuple-element.68.lists, s32[1,1280]{1,0:T(1,128)S(1)} %get-tuple-element.69.long, f32[3,3]{1,0:T(4,128)S(1)} %get-tuple-element.51.corr, bf16[104,128,256]{2,1,0:T(8,128)(2,1)S(1)} %get-tuple-element.70.cache, f32[64,8,128]{2,1,0:T(8,128)S(1)} %get-tuple-element.71.q_ref.q_near, ...), custom_call_target="tpu_custom_call" | custom-call | flops 100000000 | bytes 1048576 | tf_op jit(solution)/shard_map/near_times/pallas_call | solution.py:863
  49.7 14.8 %all-to-all-start = ((f32[256,1,16]{2,1,0:T(1,128)}), f32[256,1,16]{2,1,0:T(1,128)S(1)}, u32[]{:S(2)}, u32[]{:S(2)}) async-start(f32[256,1,16]{2,1,0:T(1,128)} %near_times.3), calls=%async_computation | async-start | bytes 262144 | tf_op jit(solution)/shard_map/all_to_all | solution.py:891
  64.5 5.3 %grid.1.g = f32[3,3,512]{2,1,0:T(4,128)S(1)} custom-call(s32[8,128]{1,0:T(8,128)S(1)} %get-tuple-element.90.lists, s32[1,1280]{1,0:T(1,128)S(1)} %get-tuple-element.91.long, f32[3,3]{1,0:T(4,128)S(1)} %get-tuple-element.51.corr, f32[8,8]{1,0:T(8,128)S(1)} %get-tuple-element.49.frame, f32[72,16,128]{2,1,0:T(8,128)S(1)} %pack.1.packed, ...), custom_call_target="tpu_custom_call" | custom-call | flops 1000000000 | bytes 1048576 | tf_op jit(solution)/shard_map/grid/pallas_call | solution.py:892
  69.9 7.7 %all-to-all-done.parts = f32[256,1,16]{2,1,0:T(1,128)S(1)} async-done(((f32[256,1,16]{2,1,0:T(1,128)}), f32[256,1,16]{2,1,0:T(1,128)S(1)}, u32[]{:S(2)}, u32[]{:S(2)}) %all-to-all-start) | async-done | bytes 16416 | tf_op jit(solution)/shard_map/all_to_all | solution.py:891
  77.6 0.8 %final.1 = (f32[3,1,1024]{2,1,0:T(1,128)}, f32[3,1,512]{2,1,0:T(1,128)}) custom-call(f32[256,1,16]{2,1,0:T(1,128)S(1)} %all-to-all-done.parts, f32[3,1024]{1,0:T(4,128)S(1)} %get-tuple-element.88.innov, f32[2,3,1024]{2,1,0:T(4,128)S(1)} %unsort.1.w, f32[3,3,512]{2,1,0:T(4,128)S(1)} %grid.1.g), custom_call_target="tpu_custom_call" | custom-call | flops 1000000 | bytes 1048576 | tf_op jit(solution)/shard_map/final/pallas_call | solution.py:905
  (10 shorter events, 0.1 us)
Async XLA Ops:
  4.3 8.9 %collective-permute-start.1 = (f32[8,1024]{1,0:T(8,128)S(1)}, f32[8,1024]{1,0:T(8,128)S(1)}, u32[]{:S(2)}, u32[]{:S(2)}) collective-permute-start(f32[8,1024]{1,0:T(8,128)S(1)} %get-tuple-element.52.hb), channel_id=1, source_target_pairs={{1,2},{2,1},{3,4},{4,3},{5,6},{6,5},{7,8},{8,7},{9,10},{10,9},{11,... | collective-permute-start | bytes 98312 | tf_op jit(solution)/shard_map/ppermute | solution.py:712
  10.2 3.1 %collective-permute-start = (f32[8,1024]{1,0:T(8,128)S(1)}, f32[8,1024]{1,0:T(8,128)S(1)}, u32[]{:S(2)}, u32[]{:S(2)}) collective-permute-start(f32[8,1024]{1,0:T(8,128)S(1)} %get-tuple-element.52.hb), channel_id=1, source_target_pairs={{0,1},{1,0},{2,3},{3,2},{4,5},{5,4},{6,7},{7,6},{8,9},{9,8},{10,11... | collective-permute-start | bytes 98312 | tf_op jit(solution)/shard_map/ppermute | solution.py:712
  13.3 7.0 %collective-permute-start.3 = (f32[3,8,1024]{2,1,0:T(8,128)S(1)}, f32[3,8,1024]{2,1,0:T(8,128)S(1)}, u32[]{:S(2)}, u32[]{:S(2)}) collective-permute-start(f32[3,8,1024]{2,1,0:T(8,128)S(1)} %pad_maximum_fusion.mid.refs_0_), channel_id=1, source_target_pairs={{16,32},{32,16},{48,64},{64,48},{80,96},{96,80},{112,128},{128,112... | collective-permute-start | bytes 294920 | tf_op jit(solution)/shard_map/ppermute | solution.py:712
  16.7 3.6 %collective-permute-start.2 = (f32[3,8,1024]{2,1,0:T(8,128)S(1)}, f32[3,8,1024]{2,1,0:T(8,128)S(1)}, u32[]{:S(2)}, u32[]{:S(2)}) collective-permute-start(f32[3,8,1024]{2,1,0:T(8,128)S(1)} %pad_maximum_fusion.mid.refs_0_), channel_id=1, source_target_pairs={{0,16},{16,0},{32,48},{48,32},{64,80},{80,64},{96,112},{112,96},{1... | collective-permute-start | bytes 294920 | tf_op jit(solution)/shard_map/ppermute | solution.py:712
  24.0 6.0 %collective-permute-start.5 = (f32[4,1024]{1,0:T(4,128)S(1)}, f32[4,1024]{1,0:T(4,128)S(1)}, u32[]{:S(2)}, u32[]{:S(2)}) collective-permute-start(f32[4,1024]{1,0:T(4,128)S(1)} %get-tuple-element.73.u), channel_id=1, source_target_pairs={{1,2},{2,1},{3,4},{4,3},{5,6},{6,5},{7,8},{8,7},{9,10},{10,9},{11,... | collective-permute-start | bytes 49160 | tf_op jit(solution)/shard_map/ppermute | solution.py:712
  27.5 2.9 %collective-permute-start.4 = (f32[4,1024]{1,0:T(4,128)S(1)}, f32[4,1024]{1,0:T(4,128)S(1)}, u32[]{:S(2)}, u32[]{:S(2)}) collective-permute-start(f32[4,1024]{1,0:T(4,128)S(1)} %get-tuple-element.73.u), channel_id=1, source_target_pairs={{0,1},{1,0},{2,3},{3,2},{4,5},{5,4},{6,7},{7,6},{8,9},{9,8},{10,11... | collective-permute-start | bytes 49160 | tf_op jit(solution)/shard_map/ppermute | solution.py:712
  30.4 5.4 %collective-permute-start.7 = (f32[3,4,1024]{2,1,0:T(4,128)S(1)}, f32[3,4,1024]{2,1,0:T(4,128)S(1)}, u32[]{:S(2)}, u32[]{:S(2)}) collective-permute-start(f32[3,4,1024]{2,1,0:T(4,128)S(1)} %pad_maximum_fusion.1.um.refs_3_), channel_id=1, source_target_pairs={{16,32},{32,16},{48,64},{64,48},{80,96},{96,80},{112,128},{128,112... | collective-permute-start | bytes 147464 | tf_op jit(solution)/shard_map/ppermute | solution.py:712
  32.3 3.5 %collective-permute-start.6 = (f32[3,4,1024]{2,1,0:T(4,128)S(1)}, f32[3,4,1024]{2,1,0:T(4,128)S(1)}, u32[]{:S(2)}, u32[]{:S(2)}) collective-permute-start(f32[3,4,1024]{2,1,0:T(4,128)S(1)} %pad_maximum_fusion.1.um.refs_3_), channel_id=1, source_target_pairs={{0,16},{16,0},{32,48},{48,32},{64,80},{80,64},{96,112},{112,96},{1... | collective-permute-start | bytes 147464 | tf_op jit(solution)/shard_map/ppermute | solution.py:712
  37.5 6.0 %collective-permute-start.9 = (f32[4,1024]{1,0:T(4,128)S(1)}, f32[4,1024]{1,0:T(4,128)S(1)}, u32[]{:S(2)}, u32[]{:S(2)}) collective-permute-start(f32[4,1024]{1,0:T(4,128)S(1)} %get-tuple-element.80.u), channel_id=1, source_target_pairs={{1,2},{2,1},{3,4},{4,3},{5,6},{6,5},{7,8},{8,7},{9,10},{10,9},{11,... | collective-permute-start | bytes 49160 | tf_op jit(solution)/shard_map/ppermute | solution.py:712
  40.6 2.9 %collective-permute-start.8 = (f32[4,1024]{1,0:T(4,128)S(1)}, f32[4,1024]{1,0:T(4,128)S(1)}, u32[]{:S(2)}, u32[]{:S(2)}) collective-permute-start(f32[4,1024]{1,0:T(4,128)S(1)} %get-tuple-element.80.u), channel_id=1, source_target_pairs={{0,1},{1,0},{2,3},{3,2},{4,5},{5,4},{6,7},{7,6},{8,9},{9,8},{10,11... | collective-permute-start | bytes 49160 | tf_op jit(solution)/shard_map/ppermute | solution.py:712
  43.5 3.6 %collective-permute-start.11 = (f32[3,4,1024]{2,1,0:T(4,128)S(1)}, f32[3,4,1024]{2,1,0:T(4,128)S(1)}, u32[]{:S(2)}, u32[]{:S(2)}) collective-permute-start(f32[3,4,1024]{2,1,0:T(4,128)S(1)} %pad_maximum_fusion.2.um.refs_6_), channel_id=1, source_target_pairs={{16,32},{32,16},{48,64},{64,48},{80,96},{96,80},{112,128},{128,112... | collective-permute-start | bytes 147464 | tf_op jit(solution)/shard_map/ppermute | solution.py:712
  45.2 1.9 %collective-permute-start.10 = (f32[3,4,1024]{2,1,0:T(4,128)S(1)}, f32[3,4,1024]{2,1,0:T(4,128)S(1)}, u32[]{:S(2)}, u32[]{:S(2)}) collective-permute-start(f32[3,4,1024]{2,1,0:T(4,128)S(1)} %pad_maximum_fusion.2.um.refs_6_), channel_id=1, source_target_pairs={{0,16},{16,0},{32,48},{48,32},{64,80},{80,64},{96,112},{112,96},{1... | collective-permute-start | bytes 147464 | tf_op jit(solution)/shard_map/ppermute | solution.py:712
  49.7 27.9 %all-to-all-start = ((f32[256,1,16]{2,1,0:T(1,128)}), f32[256,1,16]{2,1,0:T(1,128)S(1)}, u32[]{:S(2)}, u32[]{:S(2)}) async-start(f32[256,1,16]{2,1,0:T(1,128)} %near_times.3), calls=%async_computation | async-start | bytes 262144 | tf_op jit(solution)/shard_map/all_to_all | solution.py:891

commit v6 on v5

--- a/solution.py
+++ b/solution.py
@@ -19,7 +19,7 @@
 F32 = jnp.float32
 BF16 = jnp.bfloat16
 VLIM = 8 * 1024 * 1024
-UNROLL = 8
+UNROLL = 16
 ROWS = 32
 GROUP = 4
 KEPT = 96
@@ -249,8 +249,11 @@
     return active, lane, (lane & 7) + 8 * region, (lane >> 3) & 7
 
 
-def long_list(active, source, target, regions, out, mask_v, mask_s, sem):
-    mask_v[...] = jnp.where(active, source * 8 + target + 1, 0)
+def entries_of(active, source, target):
+    return jnp.where(active, source * 8 + target + 1, 0)
+
+
+def long_list(mask_v, regions, out, mask_s, sem):
     copy = pltpu.make_async_copy(mask_v, mask_s, sem)
     copy.start()
     copy.wait()
@@ -461,7 +464,8 @@
 
     @pl.when(count > KEPT)
     def _():
-        long_list(active, source, target, regions, long_out, mask_v, mask_s, sem_long)
+        mask_v[...] = entries_of(active, source, target)
+        long_list(mask_v, regions, long_out, mask_s, sem_long)
 
     kept = jnp.minimum(count, cache_out.shape[0] - UNROLL)
     steps = jnp.maximum((kept + 1) // 2, 1)
@@ -495,22 +499,14 @@
     give_next(image, field, dev, img_out, nxt_out, u_out)
 
 
-def cells_list_kernel(
-    frame, bounds, mid, three, four, lists_out, long_out, lists_v, mask_v, mask_s, sem, sem_long
-):
+def cells_list_kernel(frame, bounds, mid, three, four, lists_out, mask_out):
     halo = (mid, three, four)
     where = [(0, 1)] + OTHERS
     tiles = [halo[c][a] for c, a in where]
     active, lane, source, target = near_active(tiles, where, frame[...], bounds)
     active = active & (lane >= 64)
-    lists_v[...] = list_of(active, source, target, len(where))
-    copy = pltpu.make_async_copy(lists_v, lists_out, sem)
-    copy.start()
-    copy.wait()
-
-    @pl.when(lists_out[1, 0] > KEPT)
-    def _():
-        long_list(active, source, target, len(where), long_out, mask_v, mask_s, sem_long)
+    lists_out[...] = list_of(active, source, target, len(where))
+    mask_out[...] = entries_of(active, source, target)
 
 
 def mix(corr, total):
@@ -608,7 +604,12 @@
         out[n, 12:16, :] = jnp.zeros((4, BLK), F32)
 
 
-def grid_kernel(lists, long, corr, frame, packed, bgg, g_out, tcol, rho, acc):
+def grid_kernel(
+    lists_v, mask_v, corr, frame, packed, bgg, g_out,
+    tcol, rho, acc, lists, long, mask_s, sem, sem_long,
+):
+    copy = pltpu.make_async_copy(lists_v, lists, sem)
+    copy.start()
     cells = g_out.shape[2]
     columns = cells // GRID_ROWS
     bands, sectors = lax.axis_size("lat"), lax.axis_size("lon")
@@ -624,8 +625,14 @@
     point = jnp.where(row == 2, sinlat, point)
     set_columns(blocks(to_frame(point, 0, frame[...])), tcol)
     acc[...] = jnp.zeros(acc.shape, F32)
+    copy.wait()
     count = lists[1, 0]
     short = jnp.minimum(count, KEPT)
+
+    @pl.when(count > KEPT)
+    def _():
+        long_list(mask_v, 1 + len(OTHERS), long, mask_s, sem_long)
+
 
     def one(entry, weight, out):
         near = packed[entry >> 3]
@@ -874,10 +881,9 @@
             cells_list_kernel,
             "cells_list",
             [VM] * 5,
-            [arr(8, BLK, dtype=jnp.int32), arr(1, 10 * BLK, dtype=jnp.int32)],
-            long_scratch,
+            [arr(8, BLK, dtype=jnp.int32), arr(16, BLK, dtype=jnp.int32)],
+            [],
             10**8,
-            [SM, SM],
         )(frame, bounds, *near0)
 
     near1, acc, cells_lists = exchange(u1, lambda: own_times(u1), list_cells)
@@ -892,13 +898,17 @@
     (parts_g,) = call(
         grid_kernel,
         "grid",
-        [SM] * 2 + [VM] * 4,
+        [VM] * 6,
         [arr(3, 3, cells)],
         [
             pltpu.VMEM((cells // BLK, 3, BLK, BLK), F32),
             pltpu.VMEM((GROUP, BLK, 2 * BLK), BF16),
             pltpu.VMEM((cells // BLK, 16, BLK), F32),
-        ],
+            pltpu.SMEM((8, BLK), jnp.int32),
+            pltpu.SMEM((1, 10 * BLK), jnp.int32),
+            pltpu.SMEM((16, BLK), jnp.int32),
+        ]
+        + [pltpu.SemaphoreType.DMA] * 2,
         10**9,
     )(*cells_lists, corr, frame, packed, bgg)
     (parts_w,) = call(unsort_kernel, "unsort", [VM] * 3, [arr(2, 3, slots)], [], 10**8)(rank, b1, b2)

time: 78.7 us -> 78.8 us (level)
  starting transfers between devices: 39.5 us -> 32.3 us
  Pallas kernels: 26.1 us -> 31.5 us
  waiting for transfers between devices: 11.3 us -> 13 us
    ppermute x12, starting transfers between devices: 24.7 us -> 19.1 us  [swap(): return lax.ppermute(x, axis, pairs)]
    ppermute x12, waiting for transfers between devices: 3.61 us -> 6.76 us  [swap(): return lax.ppermute(x, axis, pairs)]
    pallas_call x2, Pallas kernels: 2.61 us -> 4.38 us  [own_times(): call(own_times_kernel, 'own_times', [SM] + [VM] * 3, [arr(per, 8, BLK)],...]
    all_to_all x1, starting transfers between devices: 14.8 us -> 13.2 us  [per_device(): parts = lax.all_to_all(copies, ('lat', 'lon'), 0, 0, tiled=True)]
    all_to_all x1, waiting for transfers between devices: 7.72 us -> 6.19 us  [per_device(): parts = lax.all_to_all(copies, ('lat', 'lon'), 0, 0, tiled=True)]
    pallas_call x1, Pallas kernels: 5.34 us -> 6.87 us  [per_device(): call(grid_kernel, 'grid', [VM] * 6, [arr(3, 3, cells)], [pltpu.VMEM((cell...]
    pallas_call x1, Pallas kernels: 1.89 us -> 0.47 us  [list_cells(): call(cells_list_kernel, 'cells_list', [VM] * 5, [arr(8, BLK, dtype=jnp.in...]
    pallas_call x1, Pallas kernels: 3.7 us -> 4.89 us  [per_device(): call(near_first_kernel, 'near_first', [VM] * 11, [arr(8 * per, 8, BLK), a...]
  transfers between devices with their start and end apart: 13 -> 13, of which waited for: 5 -> 5; matrix products, arithmetic and copies ran while one was open for 0% -> 0% of each run, Pallas kernels for 18% -> 22%
where the time goes in v6:
time: 78.8 us; the launch traced here: 78.3 us
  starting transfers between devices  32.3 us (41%)
  Pallas kernels  31.5 us (40%)
  waiting for transfers between devices  13 us (16%)
  between operations  1.57 us (2%)
    ppermute x12, starting transfers between devices, swap(): return lax.ppermute(x, axis, pairs)  19.1 us
    all_to_all x1, starting transfers between devices, per_device(): parts = lax.all_to_all(copies, ('lat', 'lon'), 0, 0, tiled=True)  13.2 us
    pallas_call x1, Pallas kernels, per_device(): call(grid_kernel, 'grid', [VM] * 6, [arr(3, 3, cells)], [pltpu.VMEM((cell...  6.87 us
    ppermute x12, waiting for transfers between devices, swap(): return lax.ppermute(x, axis, pairs)  6.76 us
    all_to_all x1, waiting for transfers between devices, per_device(): parts = lax.all_to_all(copies, ('lat', 'lon'), 0, 0, tiled=True)  6.19 us
    pallas_call x2, Pallas kernels, near_times(): call(functools.partial(near_times_kernel, last), 'near_times', [SM] * 2 +...  4.99 us
    pallas_call x1, Pallas kernels, per_device(): call(near_first_kernel, 'near_first', [VM] * 11, [arr(8 * per, 8, BLK), a...  4.89 us
    pallas_call x2, Pallas kernels, own_times(): call(own_times_kernel, 'own_times', [SM] + [VM] * 3, [arr(per, 8, BLK)],...  4.38 us
  transfers between devices with their start and end apart: 13, of which 5 were waited for; matrix products, arithmetic and copies ran while one was open for 0% of the time, Pallas kernels for 22%

profile of v6, /device:TPU:1, one launch (start us, length us, event | category | flops | bytes accessed | tf_op | source)
XLA Modules:
  0.0 78.3 jit_solution(16584033694880013756)
XLA Ops:
  1.3 3.0 %sort.1 = (f32[8,1024]{1,0:T(8,128)S(1)}, f32[3,1024]{1,0:T(4,128)S(1)}, f32[3,1024]{1,0:T(4,128)S(1)}, f32[3,1024]{1,0:T(4,128)S(1)}, f32[1,1024]{1,0:T(1,128)S...) custom-call(s32[1,1]{1,0:T(1,128)S(6)} %copy.12.count, ...), custom_call_target="tpu_custom_call" | custom-call | flops 100000000 | bytes 1048576 | tf_op jit(solution)/shard_map/sort/pallas_call | solution.py:778
  4.3 5.8 %collective-permute-start.1 = (f32[8,1024]{1,0:T(8,128)S(1)}, f32[8,1024]{1,0:T(8,128)S(1)}, u32[]{:S(2)}, u32[]{:S(2)}) collective-permute-start(f32[8,1024]{1,0:T(8,128)S(1)} %get-tuple-element.52.hb), channel_id=1, source_target_pairs={{1,2},{2,1},{3,4},{4,3},{5,6},{6,5},{7,8},{8,7},{9,10},{10,9},{11,... | collective-permute-start | bytes 98312 | tf_op jit(solution)/shard_map/ppermute | solution.py:719
  10.2 3.7 %own_first.1 = (f32[8,8,128]{2,1,0:T(8,128)S(1)}, f32[8,3,128,128]{3,2,1,0:T(8,128)S(1)}, s32[8,128]{1,0:T(8,128)S(1)}, bf16[38,128,256]{2,1,0:T(8,128)(2,1)S(1)...) custom-call(f32[8,8]{1,0:T(8,128)S(1)} %get-tuple-element.49.frame, f32[8,1024]{1,0:T(8,128)S(1)} %get-tuple-element.52.hb, ...), custom_call_target="tpu_custom_call" | custom-call | flops 1000000000 | bytes 1048576 | tf_op jit(solution)/shard_map/own_first/pallas_call | solution.py:803
  13.9 0.0 collective-permute-done
  14.0 2.7 %collective-permute-start.3 = (f32[3,8,1024]{2,1,0:T(8,128)S(1)}, f32[3,8,1024]{2,1,0:T(8,128)S(1)}, u32[]{:S(2)}, u32[]{:S(2)}) collective-permute-start(f32[3,8,1024]{2,1,0:T(8,128)S(1)} %pad_maximum_fusion.mid.refs_0_), channel_id=1, source_target_pairs={{16,32},{32,16},{48,64},{64,48},{80,96},{96,80},{112,128},{128,112... | collective-permute-start | bytes 294920 | tf_op jit(solution)/shard_map/ppermute | solution.py:719
  16.7 2.7 %collective-permute-start.2 = (f32[3,8,1024]{2,1,0:T(8,128)S(1)}, f32[3,8,1024]{2,1,0:T(8,128)S(1)}, u32[]{:S(2)}, u32[]{:S(2)}) collective-permute-start(f32[3,8,1024]{2,1,0:T(8,128)S(1)} %pad_maximum_fusion.mid.refs_0_), channel_id=1, source_target_pairs={{0,16},{16,0},{32,48},{48,32},{64,80},{80,64},{96,112},{112,96},{1... | collective-permute-start | bytes 294920 | tf_op jit(solution)/shard_map/ppermute | solution.py:719
  19.3 1.7 %own_second.1 = (bf16[30,128,256]{2,1,0:T(8,128)(2,1)S(1)}, f32[8,8,128]{2,1,0:T(8,128)S(1)}) custom-call(s32[8,128]{1,0:T(8,128)S(1)} %get-tuple-element.55.lists, f32[8,8,128]{2,1,0:T(8,128)S(1)} %get-tuple-element.54.q.q_own, f32[8,3,128,128]{3,2,1,0:T(8,128)S(1)} %get-tuple-element.53.tcol, bf16[8,16,256]{2,1,0:T(8,128)(2,1)S(1)} %get-tuple-element.57.v_ref, ...), custom_call_target="tpu_custom_call" | custom-call | flops 1000000000 | bytes 1048576 | tf_op jit(solution)/shard_map/own_second/pallas_call | solution.py:821
  21.0 0.0 collective-permute-done.3.four.refs_2_
  21.0 0.0 collective-permute-done.2.three.refs_1_
  21.1 4.9 %near_first.1 = (f32[64,8,128]{2,1,0:T(8,128)S(1)}, s32[8,128]{1,0:T(8,128)S(1)}, s32[1,1280]{1,0:T(1,128)S(1)}, bf16[112,128,256]{2,1,0:T(8,128)(2,1)S(1)}, f32...) custom-call(f32[8,8]{1,0:T(8,128)S(1)} %get-tuple-element.49.frame, ...), custom_call_target="tpu_custom_call" | custom-call | flops 1000000000 | bytes 1048576 | tf_op jit(solution)/shard_map/near_first/pallas_call | solution.py:851
  26.0 1.3 %collective-permute-start.5 = (f32[4,1024]{1,0:T(4,128)S(1)}, f32[4,1024]{1,0:T(4,128)S(1)}, u32[]{:S(2)}, u32[]{:S(2)}) collective-permute-start(f32[4,1024]{1,0:T(4,128)S(1)} %get-tuple-element.73.u), channel_id=1, source_target_pairs={{1,2},{2,1},{3,4},{4,3},{5,6},{6,5},{7,8},{8,7},{9,10},{10,9},{11,... | collective-permute-start | bytes 49160 | tf_op jit(solution)/shard_map/ppermute | solution.py:719
  27.2 0.0 collective-permute-start.4
  27.2 2.2 %own_times.2.acc_own = f32[8,8,128]{2,1,0:T(8,128)S(1)} custom-call(s32[8,128]{1,0:T(8,128)S(1)} %get-tuple-element.55.lists, bf16[38,128,256]{2,1,0:T(8,128)(2,1)S(1)} %get-tuple-element.56.cache, bf16[30,128,256]{2,1,0:T(8,128)(2,1)S(1)} %get-tuple-element.72.cache_late, f32[4,1024]{1,0:T(4,128)S(1)} %get-tuple-element.73.u), custom_call_target="tpu_custom_call" | custom-call | flops 100000000 | bytes 1048576 | tf_op jit(solution)/shard_map/own_times/pallas_call | solution.py:831
  29.4 2.6 %collective-permute-done.5 = f32[4,1024]{1,0:T(4,128)S(1)} collective-permute-done((f32[4,1024]{1,0:T(4,128)S(1)}, f32[4,1024]{1,0:T(4,128)S(1)}, u32[]{:S(2)}, u32[]{:S(2)}) %collective-permute-start.5) | collective-permute-done | bytes 16416 | tf_op jit(solution)/shard_map/ppermute | solution.py:719
  32.0 1.4 %collective-permute-start.7 = (f32[3,4,1024]{2,1,0:T(4,128)S(1)}, f32[3,4,1024]{2,1,0:T(4,128)S(1)}, u32[]{:S(2)}, u32[]{:S(2)}) collective-permute-start(f32[3,4,1024]{2,1,0:T(4,128)S(1)} %pad_maximum_fusion.1.um.refs_3_), channel_id=1, source_target_pairs={{16,32},{32,16},{48,64},{64,48},{80,96},{96,80},{112,128},{128,112... | collective-permute-start | bytes 147464 | tf_op jit(solution)/shard_map/ppermute | solution.py:719
  33.4 0.6 collective-permute-start.6
  33.9 0.5 cells_list.1
  34.4 1.2 %collective-permute-done.7.un.refs_5_ = f32[3,4,1024]{2,1,0:T(4,128)S(1)} collective-permute-done((f32[3,4,1024]{2,1,0:T(4,128)S(1)}, f32[3,4,1024]{2,1,0:T(4,128)S(1)}, u32[]{:S(2)}, u32[]{:S(2)}) %collective-permute-start.7) | collective-permute-done | bytes 49184 | tf_op jit(solution)/shard_map/ppermute | solution.py:719
  35.6 2.1 %near_times.2 = (f32[3,1024]{1,0:T(4,128)S(1)}, f32[3,1024]{1,0:T(4,128)S(1)}, f32[4,1024]{1,0:T(4,128)S(1)}) custom-call(s32[8,128]{1,0:T(8,128)S(1)} %get-tuple-element.68.lists, s32[1,1280]{1,0:T(1,128)S(1)} %get-tuple-element.69.long, f32[3,3]{1,0:T(4,128)S(1)} %get-tuple-element.51.corr, bf16[112,128,256]{2,1,0:T(8,128)(2,1)S(1)} %get-tuple-element.70.cache, ...), custom_call_target="tpu_custom_call" | custom-call | flops 100000000 | bytes 1048576 | tf_op jit(solution)/shard_map/near_times/pallas_call | solution.py:870
  37.7 1.9 %collective-permute-start.9 = (f32[4,1024]{1,0:T(4,128)S(1)}, f32[4,1024]{1,0:T(4,128)S(1)}, u32[]{:S(2)}, u32[]{:S(2)}) collective-permute-start(f32[4,1024]{1,0:T(4,128)S(1)} %get-tuple-element.80.u), channel_id=1, source_target_pairs={{1,2},{2,1},{3,4},{4,3},{5,6},{6,5},{7,8},{8,7},{9,10},{10,9},{11,... | collective-permute-start | bytes 49160 | tf_op jit(solution)/shard_map/ppermute | solution.py:719
  39.6 2.2 %own_times.3.acc_own = f32[8,8,128]{2,1,0:T(8,128)S(1)} custom-call(s32[8,128]{1,0:T(8,128)S(1)} %get-tuple-element.55.lists, bf16[38,128,256]{2,1,0:T(8,128)(2,1)S(1)} %get-tuple-element.56.cache, bf16[30,128,256]{2,1,0:T(8,128)(2,1)S(1)} %get-tuple-element.72.cache_late, f32[4,1024]{1,0:T(4,128)S(1)} %get-tuple-element.80.u), custom_call_target="tpu_custom_call" | custom-call | flops 100000000 | bytes 1048576 | tf_op jit(solution)/shard_map/own_times/pallas_call | solution.py:831
  41.8 1.9 %collective-permute-done.9 = f32[4,1024]{1,0:T(4,128)S(1)} collective-permute-done((f32[4,1024]{1,0:T(4,128)S(1)}, f32[4,1024]{1,0:T(4,128)S(1)}, u32[]{:S(2)}, u32[]{:S(2)}) %collective-permute-start.9) | collective-permute-done | bytes 16416 | tf_op jit(solution)/shard_map/ppermute | solution.py:719
  43.7 2.5 %collective-permute-start.11 = (f32[3,4,1024]{2,1,0:T(4,128)S(1)}, f32[3,4,1024]{2,1,0:T(4,128)S(1)}, u32[]{:S(2)}, u32[]{:S(2)}) collective-permute-start(f32[3,4,1024]{2,1,0:T(4,128)S(1)} %pad_maximum_fusion.2.um.refs_6_), channel_id=1, source_target_pairs={{16,32},{32,16},{48,64},{64,48},{80,96},{96,80},{112,128},{128,112... | collective-permute-start | bytes 147464 | tf_op jit(solution)/shard_map/ppermute | solution.py:719
  46.2 0.2 collective-permute-start.10
  46.4 0.4 unsort.1.w
  46.9 1.1 %collective-permute-done.11.un.refs_8_ = f32[3,4,1024]{2,1,0:T(4,128)S(1)} collective-permute-done((f32[3,4,1024]{2,1,0:T(4,128)S(1)}, f32[3,4,1024]{2,1,0:T(4,128)S(1)}, u32[]{:S(2)}, u32[]{:S(2)}) %collective-permute-start.11) | collective-permute-done | bytes 49184 | tf_op jit(solution)/shard_map/ppermute | solution.py:719
  48.0 0.1 pack.1.packed
  48.1 2.9 %near_times.3 = f32[256,1,16]{2,1,0:T(1,128)} custom-call(s32[8,128]{1,0:T(8,128)S(1)} %get-tuple-element.68.lists, s32[1,1280]{1,0:T(1,128)S(1)} %get-tuple-element.69.long, f32[3,3]{1,0:T(4,128)S(1)} %get-tuple-element.51.corr, bf16[112,128,256]{2,1,0:T(8,128)(2,1)S(1)} %get-tuple-element.70.cache, f32[64,8,128]{2,1,0:T(8,128)S(1)} %get-tuple-element.71.q_ref.q_near, ...), custom_call_target="tpu_custom_call" | custom-call | flops 100000000 | bytes 1048576 | tf_op jit(solution)/shard_map/near_times/pallas_call | solution.py:870
  51.0 13.2 %all-to-all-start = ((f32[256,1,16]{2,1,0:T(1,128)}), f32[256,1,16]{2,1,0:T(1,128)S(1)}, u32[]{:S(2)}, u32[]{:S(2)}) async-start(f32[256,1,16]{2,1,0:T(1,128)} %near_times.3), calls=%async_computation | async-start | bytes 262144 | tf_op jit(solution)/shard_map/all_to_all | solution.py:897
  64.3 6.9 %grid.1.g = f32[3,3,512]{2,1,0:T(4,128)S(1)} custom-call(s32[8,128]{1,0:T(8,128)S(1)} %get-tuple-element.90.lists_v, s32[16,128]{1,0:T(8,128)S(1)} %get-tuple-element.91.mask_v, f32[3,3]{1,0:T(4,128)S(1)} %get-tuple-element.51.corr, f32[8,8]{1,0:T(8,128)S(1)} %get-tuple-element.49.frame, f32[72,16,128]{2,1,0:T(8,128)S(1)} %pack.1.packed, ...), custom_call_target="tpu_custom_call" | custom-call | flops 1000000000 | bytes 1048576 | tf_op jit(solution)/shard_map/grid/pallas_call | solution.py:898
  71.1 6.2 %all-to-all-done.parts = f32[256,1,16]{2,1,0:T(1,128)S(1)} async-done(((f32[256,1,16]{2,1,0:T(1,128)}), f32[256,1,16]{2,1,0:T(1,128)S(1)}, u32[]{:S(2)}, u32[]{:S(2)}) %all-to-all-start) | async-done | bytes 16416 | tf_op jit(solution)/shard_map/all_to_all | solution.py:897
  77.3 0.8 %final.1 = (f32[3,1,1024]{2,1,0:T(1,128)}, f32[3,1,512]{2,1,0:T(1,128)}) custom-call(f32[256,1,16]{2,1,0:T(1,128)S(1)} %all-to-all-done.parts, f32[3,1024]{1,0:T(4,128)S(1)} %get-tuple-element.88.innov, f32[2,3,1024]{2,1,0:T(4,128)S(1)} %unsort.1.w, f32[3,3,512]{2,1,0:T(4,128)S(1)} %grid.1.g), custom_call_target="tpu_custom_call" | custom-call | flops 1000000 | bytes 1048576 | tf_op jit(solution)/shard_map/final/pallas_call | solution.py:915
  (10 shorter events, 0.1 us)
Async XLA Ops:
  4.3 9.6 %collective-permute-start.1 = (f32[8,1024]{1,0:T(8,128)S(1)}, f32[8,1024]{1,0:T(8,128)S(1)}, u32[]{:S(2)}, u32[]{:S(2)}) collective-permute-start(f32[8,1024]{1,0:T(8,128)S(1)} %get-tuple-element.52.hb), channel_id=1, source_target_pairs={{1,2},{2,1},{3,4},{4,3},{5,6},{6,5},{7,8},{8,7},{9,10},{10,9},{11,... | collective-permute-start | bytes 98312 | tf_op jit(solution)/shard_map/ppermute | solution.py:719
  10.2 3.8 %collective-permute-start = (f32[8,1024]{1,0:T(8,128)S(1)}, f32[8,1024]{1,0:T(8,128)S(1)}, u32[]{:S(2)}, u32[]{:S(2)}) collective-permute-start(f32[8,1024]{1,0:T(8,128)S(1)} %get-tuple-element.52.hb), channel_id=1, source_target_pairs={{0,1},{1,0},{2,3},{3,2},{4,5},{5,4},{6,7},{7,6},{8,9},{9,8},{10,11... | collective-permute-start | bytes 98312 | tf_op jit(solution)/shard_map/ppermute | solution.py:719
  14.0 7.1 %collective-permute-start.3 = (f32[3,8,1024]{2,1,0:T(8,128)S(1)}, f32[3,8,1024]{2,1,0:T(8,128)S(1)}, u32[]{:S(2)}, u32[]{:S(2)}) collective-permute-start(f32[3,8,1024]{2,1,0:T(8,128)S(1)} %pad_maximum_fusion.mid.refs_0_), channel_id=1, source_target_pairs={{16,32},{32,16},{48,64},{64,48},{80,96},{96,80},{112,128},{128,112... | collective-permute-start | bytes 294920 | tf_op jit(solution)/shard_map/ppermute | solution.py:719
  16.7 4.4 %collective-permute-start.2 = (f32[3,8,1024]{2,1,0:T(8,128)S(1)}, f32[3,8,1024]{2,1,0:T(8,128)S(1)}, u32[]{:S(2)}, u32[]{:S(2)}) collective-permute-start(f32[3,8,1024]{2,1,0:T(8,128)S(1)} %pad_maximum_fusion.mid.refs_0_), channel_id=1, source_target_pairs={{0,16},{16,0},{32,48},{48,32},{64,80},{80,64},{96,112},{112,96},{1... | collective-permute-start | bytes 294920 | tf_op jit(solution)/shard_map/ppermute | solution.py:719
  26.0 6.0 %collective-permute-start.5 = (f32[4,1024]{1,0:T(4,128)S(1)}, f32[4,1024]{1,0:T(4,128)S(1)}, u32[]{:S(2)}, u32[]{:S(2)}) collective-permute-start(f32[4,1024]{1,0:T(4,128)S(1)} %get-tuple-element.73.u), channel_id=1, source_target_pairs={{1,2},{2,1},{3,4},{4,3},{5,6},{6,5},{7,8},{8,7},{9,10},{10,9},{11,... | collective-permute-start | bytes 49160 | tf_op jit(solution)/shard_map/ppermute | solution.py:719
  27.2 4.8 %collective-permute-start.4 = (f32[4,1024]{1,0:T(4,128)S(1)}, f32[4,1024]{1,0:T(4,128)S(1)}, u32[]{:S(2)}, u32[]{:S(2)}) collective-permute-start(f32[4,1024]{1,0:T(4,128)S(1)} %get-tuple-element.73.u), channel_id=1, source_target_pairs={{0,1},{1,0},{2,3},{3,2},{4,5},{5,4},{6,7},{7,6},{8,9},{9,8},{10,11... | collective-permute-start | bytes 49160 | tf_op jit(solution)/shard_map/ppermute | solution.py:719
  32.0 3.6 %collective-permute-start.7 = (f32[3,4,1024]{2,1,0:T(4,128)S(1)}, f32[3,4,1024]{2,1,0:T(4,128)S(1)}, u32[]{:S(2)}, u32[]{:S(2)}) collective-permute-start(f32[3,4,1024]{2,1,0:T(4,128)S(1)} %pad_maximum_fusion.1.um.refs_3_), channel_id=1, source_target_pairs={{16,32},{32,16},{48,64},{64,48},{80,96},{96,80},{112,128},{128,112... | collective-permute-start | bytes 147464 | tf_op jit(solution)/shard_map/ppermute | solution.py:719
  33.4 2.2 %collective-permute-start.6 = (f32[3,4,1024]{2,1,0:T(4,128)S(1)}, f32[3,4,1024]{2,1,0:T(4,128)S(1)}, u32[]{:S(2)}, u32[]{:S(2)}) collective-permute-start(f32[3,4,1024]{2,1,0:T(4,128)S(1)} %pad_maximum_fusion.1.um.refs_3_), channel_id=1, source_target_pairs={{0,16},{16,0},{32,48},{48,32},{64,80},{80,64},{96,112},{112,96},{1... | collective-permute-start | bytes 147464 | tf_op jit(solution)/shard_map/ppermute | solution.py:719
  37.7 6.0 %collective-permute-start.9 = (f32[4,1024]{1,0:T(4,128)S(1)}, f32[4,1024]{1,0:T(4,128)S(1)}, u32[]{:S(2)}, u32[]{:S(2)}) collective-permute-start(f32[4,1024]{1,0:T(4,128)S(1)} %get-tuple-element.80.u), channel_id=1, source_target_pairs={{1,2},{2,1},{3,4},{4,3},{5,6},{6,5},{7,8},{8,7},{9,10},{10,9},{11,... | collective-permute-start | bytes 49160 | tf_op jit(solution)/shard_map/ppermute | solution.py:719
  39.6 4.1 %collective-permute-start.8 = (f32[4,1024]{1,0:T(4,128)S(1)}, f32[4,1024]{1,0:T(4,128)S(1)}, u32[]{:S(2)}, u32[]{:S(2)}) collective-permute-start(f32[4,1024]{1,0:T(4,128)S(1)} %get-tuple-element.80.u), channel_id=1, source_target_pairs={{0,1},{1,0},{2,3},{3,2},{4,5},{5,4},{6,7},{7,6},{8,9},{9,8},{10,11... | collective-permute-start | bytes 49160 | tf_op jit(solution)/shard_map/ppermute | solution.py:719
  43.7 4.3 %collective-permute-start.11 = (f32[3,4,1024]{2,1,0:T(4,128)S(1)}, f32[3,4,1024]{2,1,0:T(4,128)S(1)}, u32[]{:S(2)}, u32[]{:S(2)}) collective-permute-start(f32[3,4,1024]{2,1,0:T(4,128)S(1)} %pad_maximum_fusion.2.um.refs_6_), channel_id=1, source_target_pairs={{16,32},{32,16},{48,64},{64,48},{80,96},{96,80},{112,128},{128,112... | collective-permute-start | bytes 147464 | tf_op jit(solution)/shard_map/ppermute | solution.py:719
  46.2 1.8 %collective-permute-start.10 = (f32[3,4,1024]{2,1,0:T(4,128)S(1)}, f32[3,4,1024]{2,1,0:T(4,128)S(1)}, u32[]{:S(2)}, u32[]{:S(2)}) collective-permute-start(f32[3,4,1024]{2,1,0:T(4,128)S(1)} %pad_maximum_fusion.2.um.refs_6_), channel_id=1, source_target_pairs={{0,16},{16,0},{32,48},{48,32},{64,80},{80,64},{96,112},{112,96},{1... | collective-permute-start | bytes 147464 | tf_op jit(solution)/shard_map/ppermute | solution.py:719
  51.0 26.3 %all-to-all-start = ((f32[256,1,16]{2,1,0:T(1,128)}), f32[256,1,16]{2,1,0:T(1,128)S(1)}, u32[]{:S(2)}, u32[]{:S(2)}) async-start(f32[256,1,16]{2,1,0:T(1,128)} %near_times.3), calls=%async_computation | async-start | bytes 262144 | tf_op jit(solution)/shard_map/all_to_all | solution.py:897

commit v7 on v6

--- a/solution.py
+++ b/solution.py
@@ -413,7 +413,10 @@
 def own_second_kernel(lists, q, tcol, v_ref, acc_in, cache_out, acc):
     acc[...] = acc_in[...]
     count = jnp.maximum(lists[1, 0] - EARLY, 0)
-    own_pairs(lists, EARLY, count, 0, q, tcol, cache_out, v_ref, acc)
+
+    @pl.when(count > 0)
+    def _():
+        own_pairs(lists, EARLY, count, 0, q, tcol, cache_out, v_ref, acc)
 
 
 def own_times_kernel(lists, cache, cache_late, u, acc, v_ref):

time: 78.8 us -> 79 us (level)
  starting transfers between devices: 32.3 us -> 38.4 us
  waiting for transfers between devices: 13 us -> 8.46 us
  Pallas kernels: 31.5 us -> 30.1 us
    ppermute x12, starting transfers between devices: 19.1 us -> 24.1 us  [swap(): return lax.ppermute(x, axis, pairs)]
    ppermute x12, waiting for transfers between devices: 6.76 us -> 2.26 us  [swap(): return lax.ppermute(x, axis, pairs)]
    all_to_all x1, starting transfers between devices: 13.2 us -> 14.3 us  [per_device(): parts = lax.all_to_all(copies, ('lat', 'lon'), 0, 0, tiled=True)]
    pallas_call x2, Pallas kernels: 4.99 us -> 4.17 us  [near_times(): call(functools.partial(near_times_kernel, last), 'near_times', [SM] * 2 +...]
  transfers between devices with their start and end apart: 13 -> 13, of which waited for: 5 -> 6; matrix products, arithmetic and copies ran while one was open for 0% -> 0% of each run, Pallas kernels for 22% -> 22%
where the time goes in v7:
time: 79 us; the launch traced here: 78.6 us
  starting transfers between devices  38.4 us (49%)
  Pallas kernels  30.1 us (38%)
  waiting for transfers between devices  8.46 us (11%)
  between operations  1.58 us (2%)
    ppermute x12, starting transfers between devices, swap(): return lax.ppermute(x, axis, pairs)  24.1 us
    all_to_all x1, starting transfers between devices, per_device(): parts = lax.all_to_all(copies, ('lat', 'lon'), 0, 0, tiled=True)  14.3 us
    pallas_call x1, Pallas kernels, per_device(): call(grid_kernel, 'grid', [VM] * 6, [arr(3, 3, cells)], [pltpu.VMEM((cell...  6.87 us
    all_to_all x1, waiting for transfers between devices, per_device(): parts = lax.all_to_all(copies, ('lat', 'lon'), 0, 0, tiled=True)  6.19 us
    pallas_call x1, Pallas kernels, per_device(): call(near_first_kernel, 'near_first', [VM] * 11, [arr(8 * per, 8, BLK), a...  4.39 us
    pallas_call x2, Pallas kernels, own_times(): call(own_times_kernel, 'own_times', [SM] + [VM] * 3, [arr(per, 8, BLK)],...  4.38 us
    pallas_call x2, Pallas kernels, near_times(): call(functools.partial(near_times_kernel, last), 'near_times', [SM] * 2 +...  4.17 us
    pallas_call x1, Pallas kernels, own_first(): call(own_first_kernel, 'own_first', [VM] * 3, [arr(per, 8, BLK), arr(per,...  3.75 us
  transfers between devices with their start and end apart: 13, of which 6 were waited for; matrix products, arithmetic and copies ran while one was open for 0% of the time, Pallas kernels for 22%

profile of v7, /device:TPU:1, one launch (start us, length us, event | category | flops | bytes accessed | tf_op | source)
XLA Modules:
  0.0 78.6 jit_solution(5627249214026883131)
XLA Ops:
  1.3 3.0 %sort.1 = (f32[8,1024]{1,0:T(8,128)S(1)}, f32[3,1024]{1,0:T(4,128)S(1)}, f32[3,1024]{1,0:T(4,128)S(1)}, f32[3,1024]{1,0:T(4,128)S(1)}, f32[1,1024]{1,0:T(1,128)S...) custom-call(s32[1,1]{1,0:T(1,128)S(6)} %copy.12.count, ...), custom_call_target="tpu_custom_call" | custom-call | flops 100000000 | bytes 1048576 | tf_op jit(solution)/shard_map/sort/pallas_call | solution.py:781
  4.3 5.8 %collective-permute-start.1 = (f32[8,1024]{1,0:T(8,128)S(1)}, f32[8,1024]{1,0:T(8,128)S(1)}, u32[]{:S(2)}, u32[]{:S(2)}) collective-permute-start(f32[8,1024]{1,0:T(8,128)S(1)} %get-tuple-element.52.hb), channel_id=1, source_target_pairs={{1,2},{2,1},{3,4},{4,3},{5,6},{6,5},{7,8},{8,7},{9,10},{10,9},{11,... | collective-permute-start | bytes 98312 | tf_op jit(solution)/shard_map/ppermute | solution.py:722
  10.2 0.0 collective-permute-start
  10.2 3.7 %own_first.1 = (f32[8,8,128]{2,1,0:T(8,128)S(1)}, f32[8,3,128,128]{3,2,1,0:T(8,128)S(1)}, s32[8,128]{1,0:T(8,128)S(1)}, bf16[38,128,256]{2,1,0:T(8,128)(2,1)S(1)...) custom-call(f32[8,8]{1,0:T(8,128)S(1)} %get-tuple-element.49.frame, f32[8,1024]{1,0:T(8,128)S(1)} %get-tuple-element.52.hb, ...), custom_call_target="tpu_custom_call" | custom-call | flops 1000000000 | bytes 1048576 | tf_op jit(solution)/shard_map/own_first/pallas_call | solution.py:806
  13.9 0.0 collective-permute-done.1
  14.0 2.7 %collective-permute-start.3 = (f32[3,8,1024]{2,1,0:T(8,128)S(1)}, f32[3,8,1024]{2,1,0:T(8,128)S(1)}, u32[]{:S(2)}, u32[]{:S(2)}) collective-permute-start(f32[3,8,1024]{2,1,0:T(8,128)S(1)} %pad_maximum_fusion.mid.refs_0_), channel_id=1, source_target_pairs={{16,32},{32,16},{48,64},{64,48},{80,96},{96,80},{112,128},{128,112... | collective-permute-start | bytes 294920 | tf_op jit(solution)/shard_map/ppermute | solution.py:722
  16.7 2.7 %collective-permute-start.2 = (f32[3,8,1024]{2,1,0:T(8,128)S(1)}, f32[3,8,1024]{2,1,0:T(8,128)S(1)}, u32[]{:S(2)}, u32[]{:S(2)}) collective-permute-start(f32[3,8,1024]{2,1,0:T(8,128)S(1)} %pad_maximum_fusion.mid.refs_0_), channel_id=1, source_target_pairs={{0,16},{16,0},{32,48},{48,32},{64,80},{80,64},{96,112},{112,96},{1... | collective-permute-start | bytes 294920 | tf_op jit(solution)/shard_map/ppermute | solution.py:722
  19.3 1.7 %own_second.1 = (bf16[30,128,256]{2,1,0:T(8,128)(2,1)S(1)}, f32[8,8,128]{2,1,0:T(8,128)S(1)}) custom-call(s32[8,128]{1,0:T(8,128)S(1)} %get-tuple-element.55.lists, f32[8,8,128]{2,1,0:T(8,128)S(1)} %get-tuple-element.54.q.q_own, f32[8,3,128,128]{3,2,1,0:T(8,128)S(1)} %get-tuple-element.53.tcol, bf16[8,16,256]{2,1,0:T(8,128)(2,1)S(1)} %get-tuple-element.57.v_ref, ...), custom_call_target="tpu_custom_call" | custom-call | flops 1000000000 | bytes 1048576 | tf_op jit(solution)/shard_map/own_second/pallas_call | solution.py:824
  21.0 0.0 collective-permute-done.3.four.refs_2_
  21.1 4.4 %near_first.1 = (f32[64,8,128]{2,1,0:T(8,128)S(1)}, s32[8,128]{1,0:T(8,128)S(1)}, s32[1,1280]{1,0:T(1,128)S(1)}, bf16[112,128,256]{2,1,0:T(8,128)(2,1)S(1)}, f32...) custom-call(f32[8,8]{1,0:T(8,128)S(1)} %get-tuple-element.49.frame, ...), custom_call_target="tpu_custom_call" | custom-call | flops 1000000000 | bytes 1048576 | tf_op jit(solution)/shard_map/near_first/pallas_call | solution.py:854
  25.5 3.1 %collective-permute-start.5 = (f32[4,1024]{1,0:T(4,128)S(1)}, f32[4,1024]{1,0:T(4,128)S(1)}, u32[]{:S(2)}, u32[]{:S(2)}) collective-permute-start(f32[4,1024]{1,0:T(4,128)S(1)} %get-tuple-element.73.u), channel_id=1, source_target_pairs={{1,2},{2,1},{3,4},{4,3},{5,6},{6,5},{7,8},{8,7},{9,10},{10,9},{11,... | collective-permute-start | bytes 49160 | tf_op jit(solution)/shard_map/ppermute | solution.py:722
  28.6 2.2 %own_times.2.acc_own = f32[8,8,128]{2,1,0:T(8,128)S(1)} custom-call(s32[8,128]{1,0:T(8,128)S(1)} %get-tuple-element.55.lists, bf16[38,128,256]{2,1,0:T(8,128)(2,1)S(1)} %get-tuple-element.56.cache, bf16[30,128,256]{2,1,0:T(8,128)(2,1)S(1)} %get-tuple-element.72.cache_late, f32[4,1024]{1,0:T(4,128)S(1)} %get-tuple-element.73.u), custom_call_target="tpu_custom_call" | custom-call | flops 100000000 | bytes 1048576 | tf_op jit(solution)/shard_map/own_times/pallas_call | solution.py:834
  30.7 0.7 collective-permute-done.5
  31.5 0.6 collective-permute-start.7
  32.0 2.2 %collective-permute-start.6 = (f32[3,4,1024]{2,1,0:T(4,128)S(1)}, f32[3,4,1024]{2,1,0:T(4,128)S(1)}, u32[]{:S(2)}, u32[]{:S(2)}) collective-permute-start(f32[3,4,1024]{2,1,0:T(4,128)S(1)} %pad_maximum_fusion.1.um.refs_3_), channel_id=1, source_target_pairs={{0,16},{16,0},{32,48},{48,32},{64,80},{80,64},{96,112},{112,96},{1... | collective-permute-start | bytes 147464 | tf_op jit(solution)/shard_map/ppermute | solution.py:722
  34.3 0.5 cells_list.1
  34.7 0.3 collective-permute-done.7.un.refs_5_
  35.1 0.1 collective-permute-done.6.us.refs_4_
  35.1 1.7 %near_times.2 = (f32[3,1024]{1,0:T(4,128)S(1)}, f32[3,1024]{1,0:T(4,128)S(1)}, f32[4,1024]{1,0:T(4,128)S(1)}) custom-call(s32[8,128]{1,0:T(8,128)S(1)} %get-tuple-element.68.lists, s32[1,1280]{1,0:T(1,128)S(1)} %get-tuple-element.69.long, f32[3,3]{1,0:T(4,128)S(1)} %get-tuple-element.51.corr, bf16[112,128,256]{2,1,0:T(8,128)(2,1)S(1)} %get-tuple-element.70.cache, ...), custom_call_target="tpu_custom_call" | custom-call | flops 100000000 | bytes 1048576 | tf_op jit(solution)/shard_map/near_times/pallas_call | solution.py:873
  36.8 3.1 %collective-permute-start.9 = (f32[4,1024]{1,0:T(4,128)S(1)}, f32[4,1024]{1,0:T(4,128)S(1)}, u32[]{:S(2)}, u32[]{:S(2)}) collective-permute-start(f32[4,1024]{1,0:T(4,128)S(1)} %get-tuple-element.80.u), channel_id=1, source_target_pairs={{1,2},{2,1},{3,4},{4,3},{5,6},{6,5},{7,8},{8,7},{9,10},{10,9},{11,... | collective-permute-start | bytes 49160 | tf_op jit(solution)/shard_map/ppermute | solution.py:722
  39.9 2.2 %own_times.3.acc_own = f32[8,8,128]{2,1,0:T(8,128)S(1)} custom-call(s32[8,128]{1,0:T(8,128)S(1)} %get-tuple-element.55.lists, bf16[38,128,256]{2,1,0:T(8,128)(2,1)S(1)} %get-tuple-element.56.cache, bf16[30,128,256]{2,1,0:T(8,128)(2,1)S(1)} %get-tuple-element.72.cache_late, f32[4,1024]{1,0:T(4,128)S(1)} %get-tuple-element.80.u), custom_call_target="tpu_custom_call" | custom-call | flops 100000000 | bytes 1048576 | tf_op jit(solution)/shard_map/own_times/pallas_call | solution.py:834
  42.1 0.7 collective-permute-done.9
  42.8 1.7 %collective-permute-start.11 = (f32[3,4,1024]{2,1,0:T(4,128)S(1)}, f32[3,4,1024]{2,1,0:T(4,128)S(1)}, u32[]{:S(2)}, u32[]{:S(2)}) collective-permute-start(f32[3,4,1024]{2,1,0:T(4,128)S(1)} %pad_maximum_fusion.2.um.refs_6_), channel_id=1, source_target_pairs={{16,32},{32,16},{48,64},{64,48},{80,96},{96,80},{112,128},{128,112... | collective-permute-start | bytes 147464 | tf_op jit(solution)/shard_map/ppermute | solution.py:722
  44.5 2.3 %collective-permute-start.10 = (f32[3,4,1024]{2,1,0:T(4,128)S(1)}, f32[3,4,1024]{2,1,0:T(4,128)S(1)}, u32[]{:S(2)}, u32[]{:S(2)}) collective-permute-start(f32[3,4,1024]{2,1,0:T(4,128)S(1)} %pad_maximum_fusion.2.um.refs_6_), channel_id=1, source_target_pairs={{0,16},{16,0},{32,48},{48,32},{64,80},{80,64},{96,112},{112,96},{1... | collective-permute-start | bytes 147464 | tf_op jit(solution)/shard_map/ppermute | solution.py:722
  46.8 0.4 unsort.1.w
  47.2 0.4 collective-permute-done.10.us.refs_7_
  47.7 0.1 pack.1.packed
  47.8 2.5 %near_times.3 = f32[256,1,16]{2,1,0:T(1,128)} custom-call(s32[8,128]{1,0:T(8,128)S(1)} %get-tuple-element.68.lists, s32[1,1280]{1,0:T(1,128)S(1)} %get-tuple-element.69.long, f32[3,3]{1,0:T(4,128)S(1)} %get-tuple-element.51.corr, bf16[112,128,256]{2,1,0:T(8,128)(2,1)S(1)} %get-tuple-element.70.cache, f32[64,8,128]{2,1,0:T(8,128)S(1)} %get-tuple-element.71.q_ref.q_near, ...), custom_call_target="tpu_custom_call" | custom-call | flops 100000000 | bytes 1048576 | tf_op jit(solution)/shard_map/near_times/pallas_call | solution.py:873
  50.3 14.3 %all-to-all-start = ((f32[256,1,16]{2,1,0:T(1,128)}), f32[256,1,16]{2,1,0:T(1,128)S(1)}, u32[]{:S(2)}, u32[]{:S(2)}) async-start(f32[256,1,16]{2,1,0:T(1,128)} %near_times.3), calls=%async_computation | async-start | bytes 262144 | tf_op jit(solution)/shard_map/all_to_all | solution.py:900
  64.6 6.9 %grid.1.g = f32[3,3,512]{2,1,0:T(4,128)S(1)} custom-call(s32[8,128]{1,0:T(8,128)S(1)} %get-tuple-element.90.lists_v, s32[16,128]{1,0:T(8,128)S(1)} %get-tuple-element.91.mask_v, f32[3,3]{1,0:T(4,128)S(1)} %get-tuple-element.51.corr, f32[8,8]{1,0:T(8,128)S(1)} %get-tuple-element.49.frame, f32[72,16,128]{2,1,0:T(8,128)S(1)} %pack.1.packed, ...), custom_call_target="tpu_custom_call" | custom-call | flops 1000000000 | bytes 1048576 | tf_op jit(solution)/shard_map/grid/pallas_call | solution.py:901
  71.5 6.2 %all-to-all-done.parts = f32[256,1,16]{2,1,0:T(1,128)S(1)} async-done(((f32[256,1,16]{2,1,0:T(1,128)}), f32[256,1,16]{2,1,0:T(1,128)S(1)}, u32[]{:S(2)}, u32[]{:S(2)}) %all-to-all-start) | async-done | bytes 16416 | tf_op jit(solution)/shard_map/all_to_all | solution.py:900
  77.7 0.8 %final.1 = (f32[3,1,1024]{2,1,0:T(1,128)}, f32[3,1,512]{2,1,0:T(1,128)}) custom-call(f32[256,1,16]{2,1,0:T(1,128)S(1)} %all-to-all-done.parts, f32[3,1024]{1,0:T(4,128)S(1)} %get-tuple-element.88.innov, f32[2,3,1024]{2,1,0:T(4,128)S(1)} %unsort.1.w, f32[3,3,512]{2,1,0:T(4,128)S(1)} %grid.1.g), custom_call_target="tpu_custom_call" | custom-call | flops 1000000 | bytes 1048576 | tf_op jit(solution)/shard_map/final/pallas_call | solution.py:918
  (10 shorter events, 0.1 us)
Async XLA Ops:
  4.3 9.6 %collective-permute-start.1 = (f32[8,1024]{1,0:T(8,128)S(1)}, f32[8,1024]{1,0:T(8,128)S(1)}, u32[]{:S(2)}, u32[]{:S(2)}) collective-permute-start(f32[8,1024]{1,0:T(8,128)S(1)} %get-tuple-element.52.hb), channel_id=1, source_target_pairs={{1,2},{2,1},{3,4},{4,3},{5,6},{6,5},{7,8},{8,7},{9,10},{10,9},{11,... | collective-permute-start | bytes 98312 | tf_op jit(solution)/shard_map/ppermute | solution.py:722
  10.2 3.8 %collective-permute-start = (f32[8,1024]{1,0:T(8,128)S(1)}, f32[8,1024]{1,0:T(8,128)S(1)}, u32[]{:S(2)}, u32[]{:S(2)}) collective-permute-start(f32[8,1024]{1,0:T(8,128)S(1)} %get-tuple-element.52.hb), channel_id=1, source_target_pairs={{0,1},{1,0},{2,3},{3,2},{4,5},{5,4},{6,7},{7,6},{8,9},{9,8},{10,11... | collective-permute-start | bytes 98312 | tf_op jit(solution)/shard_map/ppermute | solution.py:722
  14.0 7.1 %collective-permute-start.3 = (f32[3,8,1024]{2,1,0:T(8,128)S(1)}, f32[3,8,1024]{2,1,0:T(8,128)S(1)}, u32[]{:S(2)}, u32[]{:S(2)}) collective-permute-start(f32[3,8,1024]{2,1,0:T(8,128)S(1)} %pad_maximum_fusion.mid.refs_0_), channel_id=1, source_target_pairs={{16,32},{32,16},{48,64},{64,48},{80,96},{96,80},{112,128},{128,112... | collective-permute-start | bytes 294920 | tf_op jit(solution)/shard_map/ppermute | solution.py:722
  16.7 4.4 %collective-permute-start.2 = (f32[3,8,1024]{2,1,0:T(8,128)S(1)}, f32[3,8,1024]{2,1,0:T(8,128)S(1)}, u32[]{:S(2)}, u32[]{:S(2)}) collective-permute-start(f32[3,8,1024]{2,1,0:T(8,128)S(1)} %pad_maximum_fusion.mid.refs_0_), channel_id=1, source_target_pairs={{0,16},{16,0},{32,48},{48,32},{64,80},{80,64},{96,112},{112,96},{1... | collective-permute-start | bytes 294920 | tf_op jit(solution)/shard_map/ppermute | solution.py:722
  25.5 6.0 %collective-permute-start.5 = (f32[4,1024]{1,0:T(4,128)S(1)}, f32[4,1024]{1,0:T(4,128)S(1)}, u32[]{:S(2)}, u32[]{:S(2)}) collective-permute-start(f32[4,1024]{1,0:T(4,128)S(1)} %get-tuple-element.73.u), channel_id=1, source_target_pairs={{1,2},{2,1},{3,4},{4,3},{5,6},{6,5},{7,8},{8,7},{9,10},{10,9},{11,... | collective-permute-start | bytes 49160 | tf_op jit(solution)/shard_map/ppermute | solution.py:722
  28.6 2.9 %collective-permute-start.4 = (f32[4,1024]{1,0:T(4,128)S(1)}, f32[4,1024]{1,0:T(4,128)S(1)}, u32[]{:S(2)}, u32[]{:S(2)}) collective-permute-start(f32[4,1024]{1,0:T(4,128)S(1)} %get-tuple-element.73.u), channel_id=1, source_target_pairs={{0,1},{1,0},{2,3},{3,2},{4,5},{5,4},{6,7},{7,6},{8,9},{9,8},{10,11... | collective-permute-start | bytes 49160 | tf_op jit(solution)/shard_map/ppermute | solution.py:722
  31.5 3.6 %collective-permute-start.7 = (f32[3,4,1024]{2,1,0:T(4,128)S(1)}, f32[3,4,1024]{2,1,0:T(4,128)S(1)}, u32[]{:S(2)}, u32[]{:S(2)}) collective-permute-start(f32[3,4,1024]{2,1,0:T(4,128)S(1)} %pad_maximum_fusion.1.um.refs_3_), channel_id=1, source_target_pairs={{16,32},{32,16},{48,64},{64,48},{80,96},{96,80},{112,128},{128,112... | collective-permute-start | bytes 147464 | tf_op jit(solution)/shard_map/ppermute | solution.py:722
  32.0 3.1 %collective-permute-start.6 = (f32[3,4,1024]{2,1,0:T(4,128)S(1)}, f32[3,4,1024]{2,1,0:T(4,128)S(1)}, u32[]{:S(2)}, u32[]{:S(2)}) collective-permute-start(f32[3,4,1024]{2,1,0:T(4,128)S(1)} %pad_maximum_fusion.1.um.refs_3_), channel_id=1, source_target_pairs={{0,16},{16,0},{32,48},{48,32},{64,80},{80,64},{96,112},{112,96},{1... | collective-permute-start | bytes 147464 | tf_op jit(solution)/shard_map/ppermute | solution.py:722
  36.8 6.0 %collective-permute-start.9 = (f32[4,1024]{1,0:T(4,128)S(1)}, f32[4,1024]{1,0:T(4,128)S(1)}, u32[]{:S(2)}, u32[]{:S(2)}) collective-permute-start(f32[4,1024]{1,0:T(4,128)S(1)} %get-tuple-element.80.u), channel_id=1, source_target_pairs={{1,2},{2,1},{3,4},{4,3},{5,6},{6,5},{7,8},{8,7},{9,10},{10,9},{11,... | collective-permute-start | bytes 49160 | tf_op jit(solution)/shard_map/ppermute | solution.py:722
  39.9 2.9 %collective-permute-start.8 = (f32[4,1024]{1,0:T(4,128)S(1)}, f32[4,1024]{1,0:T(4,128)S(1)}, u32[]{:S(2)}, u32[]{:S(2)}) collective-permute-start(f32[4,1024]{1,0:T(4,128)S(1)} %get-tuple-element.80.u), channel_id=1, source_target_pairs={{0,1},{1,0},{2,3},{3,2},{4,5},{5,4},{6,7},{7,6},{8,9},{9,8},{10,11... | collective-permute-start | bytes 49160 | tf_op jit(solution)/shard_map/ppermute | solution.py:722
  42.8 4.4 %collective-permute-start.11 = (f32[3,4,1024]{2,1,0:T(4,128)S(1)}, f32[3,4,1024]{2,1,0:T(4,128)S(1)}, u32[]{:S(2)}, u32[]{:S(2)}) collective-permute-start(f32[3,4,1024]{2,1,0:T(4,128)S(1)} %pad_maximum_fusion.2.um.refs_6_), channel_id=1, source_target_pairs={{16,32},{32,16},{48,64},{64,48},{80,96},{96,80},{112,128},{128,112... | collective-permute-start | bytes 147464 | tf_op jit(solution)/shard_map/ppermute | solution.py:722
  44.5 3.2 %collective-permute-start.10 = (f32[3,4,1024]{2,1,0:T(4,128)S(1)}, f32[3,4,1024]{2,1,0:T(4,128)S(1)}, u32[]{:S(2)}, u32[]{:S(2)}) collective-permute-start(f32[3,4,1024]{2,1,0:T(4,128)S(1)} %pad_maximum_fusion.2.um.refs_6_), channel_id=1, source_target_pairs={{0,16},{16,0},{32,48},{48,32},{64,80},{80,64},{96,112},{112,96},{1... | collective-permute-start | bytes 147464 | tf_op jit(solution)/shard_map/ppermute | solution.py:722
  50.3 27.4 %all-to-all-start = ((f32[256,1,16]{2,1,0:T(1,128)}), f32[256,1,16]{2,1,0:T(1,128)S(1)}, u32[]{:S(2)}, u32[]{:S(2)}) async-start(f32[256,1,16]{2,1,0:T(1,128)} %near_times.3), calls=%async_computation | async-start | bytes 262144 | tf_op jit(solution)/shard_map/all_to_all | solution.py:900

commit v8 on v6

--- a/solution.py
+++ b/solution.py
@@ -23,7 +23,7 @@
 ROWS = 32
 GROUP = 4
 KEPT = 96
-EARLY = 14
+EARLY = 10
 CELLS = 512
 
 

time: 78.8 us -> 80 us (1.015)
  starting transfers between devices: 32.3 us -> 39.9 us
  Pallas kernels: 31.5 us -> 24.9 us
    ppermute x12, starting transfers between devices: 19.1 us -> 25.2 us  [swap(): return lax.ppermute(x, axis, pairs)]
    pallas_call x2, Pallas kernels: 4.38 us -> 2.37 us  [own_times(): call(own_times_kernel, 'own_times', [SM] + [VM] * 3, [arr(per, 8, BLK)],...]
    ppermute x12, waiting for transfers between devices: 6.76 us -> 4.8 us  [swap(): return lax.ppermute(x, axis, pairs)]
    all_to_all x1, waiting for transfers between devices: 6.19 us -> 7.74 us  [per_device(): parts = lax.all_to_all(copies, ('lat', 'lon'), 0, 0, tiled=True)]
    pallas_call x1, Pallas kernels: 6.87 us -> 5.33 us  [per_device(): call(grid_kernel, 'grid', [VM] * 6, [arr(3, 3, cells)], [pltpu.VMEM((cell...]
    all_to_all x1, starting transfers between devices: 13.2 us -> 14.7 us  [per_device(): parts = lax.all_to_all(copies, ('lat', 'lon'), 0, 0, tiled=True)]
    pallas_call x1, Pallas kernels: 4.89 us -> 4.06 us  [per_device(): call(near_first_kernel, 'near_first', [VM] * 11, [arr(8 * per, 8, BLK), a...]
    pallas_call x2, Pallas kernels: 4.99 us -> 4.18 us  [near_times(): call(functools.partial(near_times_kernel, last), 'near_times', [SM] * 2 +...]
  transfers between devices with their start and end apart: 13 -> 13, of which waited for: 5 -> 5; matrix products, arithmetic and copies ran while one was open for 0% -> 0% of each run, Pallas kernels for 22% -> 16%
where the time goes in v8:
time: 80 us; the launch traced here: 79 us
  starting transfers between devices  39.9 us (50%)
  Pallas kernels  24.9 us (31%)
  waiting for transfers between devices  12.5 us (16%)
  between operations  1.58 us (2%)
    ppermute x12, starting transfers between devices, swap(): return lax.ppermute(x, axis, pairs)  25.2 us
    all_to_all x1, starting transfers between devices, per_device(): parts = lax.all_to_all(copies, ('lat', 'lon'), 0, 0, tiled=True)  14.7 us
    all_to_all x1, waiting for transfers between devices, per_device(): parts = lax.all_to_all(copies, ('lat', 'lon'), 0, 0, tiled=True)  7.74 us
    pallas_call x1, Pallas kernels, per_device(): call(grid_kernel, 'grid', [VM] * 6, [arr(3, 3, cells)], [pltpu.VMEM((cell...  5.33 us
    ppermute x12, waiting for transfers between devices, swap(): return lax.ppermute(x, axis, pairs)  4.8 us
    pallas_call x2, Pallas kernels, near_times(): call(functools.partial(near_times_kernel, last), 'near_times', [SM] * 2 +...  4.18 us
    pallas_call x1, Pallas kernels, per_device(): call(near_first_kernel, 'near_first', [VM] * 11, [arr(8 * per, 8, BLK), a...  4.06 us
    pallas_call x1, Pallas kernels, per_device(): call(sort_kernel, 'sort', [SM] + [HB] * 7, [arr(8, slots), three, three,...  3.05 us
  transfers between devices with their start and end apart: 13, of which 5 were waited for; matrix products, arithmetic and copies ran while one was open for 0% of the time, Pallas kernels for 16%

profile of v8, /device:TPU:1, one launch (start us, length us, event | category | flops | bytes accessed | tf_op | source)
XLA Modules:
  0.0 79.0 jit_solution(148107811517038368)
XLA Ops:
  1.3 3.0 %sort.1 = (f32[8,1024]{1,0:T(8,128)S(1)}, f32[3,1024]{1,0:T(4,128)S(1)}, f32[3,1024]{1,0:T(4,128)S(1)}, f32[3,1024]{1,0:T(4,128)S(1)}, f32[1,1024]{1,0:T(1,128)S...) custom-call(s32[1,1]{1,0:T(1,128)S(6)} %copy.12.count, ...), custom_call_target="tpu_custom_call" | custom-call | flops 100000000 | bytes 1048576 | tf_op jit(solution)/shard_map/sort/pallas_call | solution.py:778
  4.3 5.8 %collective-permute-start.1 = (f32[8,1024]{1,0:T(8,128)S(1)}, f32[8,1024]{1,0:T(8,128)S(1)}, u32[]{:S(2)}, u32[]{:S(2)}) collective-permute-start(f32[8,1024]{1,0:T(8,128)S(1)} %get-tuple-element.52.hb), channel_id=1, source_target_pairs={{1,2},{2,1},{3,4},{4,3},{5,6},{6,5},{7,8},{8,7},{9,10},{10,9},{11,... | collective-permute-start | bytes 98312 | tf_op jit(solution)/shard_map/ppermute | solution.py:719
  10.2 0.0 collective-permute-start
  10.2 3.0 %own_first.1 = (f32[8,8,128]{2,1,0:T(8,128)S(1)}, f32[8,3,128,128]{3,2,1,0:T(8,128)S(1)}, s32[8,128]{1,0:T(8,128)S(1)}, bf16[34,128,256]{2,1,0:T(8,128)(2,1)S(1)...) custom-call(f32[8,8]{1,0:T(8,128)S(1)} %get-tuple-element.49.frame, f32[8,1024]{1,0:T(8,128)S(1)} %get-tuple-element.52.hb, ...), custom_call_target="tpu_custom_call" | custom-call | flops 1000000000 | bytes 1048576 | tf_op jit(solution)/shard_map/own_first/pallas_call | solution.py:803
  13.2 0.0 collective-permute-done.1
  13.2 0.0 collective-permute-done
  13.3 3.4 %collective-permute-start.3 = (f32[3,8,1024]{2,1,0:T(8,128)S(1)}, f32[3,8,1024]{2,1,0:T(8,128)S(1)}, u32[]{:S(2)}, u32[]{:S(2)}) collective-permute-start(f32[3,8,1024]{2,1,0:T(8,128)S(1)} %pad_maximum_fusion.mid.refs_0_), channel_id=1, source_target_pairs={{16,32},{32,16},{48,64},{64,48},{80,96},{96,80},{112,128},{128,112... | collective-permute-start | bytes 294920 | tf_op jit(solution)/shard_map/ppermute | solution.py:719
  16.7 2.7 %collective-permute-start.2 = (f32[3,8,1024]{2,1,0:T(8,128)S(1)}, f32[3,8,1024]{2,1,0:T(8,128)S(1)}, u32[]{:S(2)}, u32[]{:S(2)}) collective-permute-start(f32[3,8,1024]{2,1,0:T(8,128)S(1)} %pad_maximum_fusion.mid.refs_0_), channel_id=1, source_target_pairs={{0,16},{16,0},{32,48},{48,32},{64,80},{80,64},{96,112},{112,96},{1... | collective-permute-start | bytes 294920 | tf_op jit(solution)/shard_map/ppermute | solution.py:719
  19.3 1.0 %own_second.1 = (bf16[34,128,256]{2,1,0:T(8,128)(2,1)S(1)}, f32[8,8,128]{2,1,0:T(8,128)S(1)}) custom-call(s32[8,128]{1,0:T(8,128)S(1)} %get-tuple-element.55.lists, f32[8,8,128]{2,1,0:T(8,128)S(1)} %get-tuple-element.54.q.q_own, f32[8,3,128,128]{3,2,1,0:T(8,128)S(1)} %get-tuple-element.53.tcol, bf16[8,16,256]{2,1,0:T(8,128)(2,1)S(1)} %get-tuple-element.57.v_ref, ...), custom_call_target="tpu_custom_call" | custom-call | flops 1000000000 | bytes 1048576 | tf_op jit(solution)/shard_map/own_second/pallas_call | solution.py:821
  20.4 4.1 %near_first.1 = (f32[64,8,128]{2,1,0:T(8,128)S(1)}, s32[8,128]{1,0:T(8,128)S(1)}, s32[1,1280]{1,0:T(1,128)S(1)}, bf16[112,128,256]{2,1,0:T(8,128)(2,1)S(1)}, f32...) custom-call(f32[8,8]{1,0:T(8,128)S(1)} %get-tuple-element.49.frame, ...), custom_call_target="tpu_custom_call" | custom-call | flops 1000000000 | bytes 1048576 | tf_op jit(solution)/shard_map/near_first/pallas_call | solution.py:851
  24.4 2.8 %collective-permute-start.5 = (f32[4,1024]{1,0:T(4,128)S(1)}, f32[4,1024]{1,0:T(4,128)S(1)}, u32[]{:S(2)}, u32[]{:S(2)}) collective-permute-start(f32[4,1024]{1,0:T(4,128)S(1)} %get-tuple-element.73.u), channel_id=1, source_target_pairs={{1,2},{2,1},{3,4},{4,3},{5,6},{6,5},{7,8},{8,7},{9,10},{10,9},{11,... | collective-permute-start | bytes 49160 | tf_op jit(solution)/shard_map/ppermute | solution.py:719
  27.2 1.2 %own_times.2.acc_own = f32[8,8,128]{2,1,0:T(8,128)S(1)} custom-call(s32[8,128]{1,0:T(8,128)S(1)} %get-tuple-element.55.lists, bf16[34,128,256]{2,1,0:T(8,128)(2,1)S(1)} %get-tuple-element.56.cache, bf16[34,128,256]{2,1,0:T(8,128)(2,1)S(1)} %get-tuple-element.72.cache_late, f32[4,1024]{1,0:T(4,128)S(1)} %get-tuple-element.73.u), custom_call_target="tpu_custom_call" | custom-call | flops 100000000 | bytes 1048576 | tf_op jit(solution)/shard_map/own_times/pallas_call | solution.py:831
  28.4 2.0 %collective-permute-done.5 = f32[4,1024]{1,0:T(4,128)S(1)} collective-permute-done((f32[4,1024]{1,0:T(4,128)S(1)}, f32[4,1024]{1,0:T(4,128)S(1)}, u32[]{:S(2)}, u32[]{:S(2)}) %collective-permute-start.5) | collective-permute-done | bytes 16416 | tf_op jit(solution)/shard_map/ppermute | solution.py:719
  30.4 2.5 %collective-permute-start.7 = (f32[3,4,1024]{2,1,0:T(4,128)S(1)}, f32[3,4,1024]{2,1,0:T(4,128)S(1)}, u32[]{:S(2)}, u32[]{:S(2)}) collective-permute-start(f32[3,4,1024]{2,1,0:T(4,128)S(1)} %pad_maximum_fusion.1.um.refs_3_), channel_id=1, source_target_pairs={{16,32},{32,16},{48,64},{64,48},{80,96},{96,80},{112,128},{128,112... | collective-permute-start | bytes 147464 | tf_op jit(solution)/shard_map/ppermute | solution.py:719
  32.9 1.3 %collective-permute-start.6 = (f32[3,4,1024]{2,1,0:T(4,128)S(1)}, f32[3,4,1024]{2,1,0:T(4,128)S(1)}, u32[]{:S(2)}, u32[]{:S(2)}) collective-permute-start(f32[3,4,1024]{2,1,0:T(4,128)S(1)} %pad_maximum_fusion.1.um.refs_3_), channel_id=1, source_target_pairs={{0,16},{16,0},{32,48},{48,32},{64,80},{80,64},{96,112},{112,96},{1... | collective-permute-start | bytes 147464 | tf_op jit(solution)/shard_map/ppermute | solution.py:719
  34.2 0.5 cells_list.1
  34.7 0.0 collective-permute-done.7.un.refs_5_
  34.7 0.4 collective-permute-done.6.us.refs_4_
  35.1 1.7 %near_times.2 = (f32[3,1024]{1,0:T(4,128)S(1)}, f32[3,1024]{1,0:T(4,128)S(1)}, f32[4,1024]{1,0:T(4,128)S(1)}) custom-call(s32[8,128]{1,0:T(8,128)S(1)} %get-tuple-element.68.lists, s32[1,1280]{1,0:T(1,128)S(1)} %get-tuple-element.69.long, f32[3,3]{1,0:T(4,128)S(1)} %get-tuple-element.51.corr, bf16[112,128,256]{2,1,0:T(8,128)(2,1)S(1)} %get-tuple-element.70.cache, ...), custom_call_target="tpu_custom_call" | custom-call | flops 100000000 | bytes 1048576 | tf_op jit(solution)/shard_map/near_times/pallas_call | solution.py:870
  36.8 3.1 %collective-permute-start.9 = (f32[4,1024]{1,0:T(4,128)S(1)}, f32[4,1024]{1,0:T(4,128)S(1)}, u32[]{:S(2)}, u32[]{:S(2)}) collective-permute-start(f32[4,1024]{1,0:T(4,128)S(1)} %get-tuple-element.80.u), channel_id=1, source_target_pairs={{1,2},{2,1},{3,4},{4,3},{5,6},{6,5},{7,8},{8,7},{9,10},{10,9},{11,... | collective-permute-start | bytes 49160 | tf_op jit(solution)/shard_map/ppermute | solution.py:719
  39.9 1.2 %own_times.3.acc_own = f32[8,8,128]{2,1,0:T(8,128)S(1)} custom-call(s32[8,128]{1,0:T(8,128)S(1)} %get-tuple-element.55.lists, bf16[34,128,256]{2,1,0:T(8,128)(2,1)S(1)} %get-tuple-element.56.cache, bf16[34,128,256]{2,1,0:T(8,128)(2,1)S(1)} %get-tuple-element.72.cache_late, f32[4,1024]{1,0:T(4,128)S(1)} %get-tuple-element.80.u), custom_call_target="tpu_custom_call" | custom-call | flops 100000000 | bytes 1048576 | tf_op jit(solution)/shard_map/own_times/pallas_call | solution.py:831
  41.1 1.7 %collective-permute-done.9 = f32[4,1024]{1,0:T(4,128)S(1)} collective-permute-done((f32[4,1024]{1,0:T(4,128)S(1)}, f32[4,1024]{1,0:T(4,128)S(1)}, u32[]{:S(2)}, u32[]{:S(2)}) %collective-permute-start.9) | collective-permute-done | bytes 16416 | tf_op jit(solution)/shard_map/ppermute | solution.py:719
  42.8 3.0 %collective-permute-start.11 = (f32[3,4,1024]{2,1,0:T(4,128)S(1)}, f32[3,4,1024]{2,1,0:T(4,128)S(1)}, u32[]{:S(2)}, u32[]{:S(2)}) collective-permute-start(f32[3,4,1024]{2,1,0:T(4,128)S(1)} %pad_maximum_fusion.2.um.refs_6_), channel_id=1, source_target_pairs={{16,32},{32,16},{48,64},{64,48},{80,96},{96,80},{112,128},{128,112... | collective-permute-start | bytes 147464 | tf_op jit(solution)/shard_map/ppermute | solution.py:719
  45.8 0.7 collective-permute-start.10
  46.5 0.4 unsort.1.w
  46.9 0.7 collective-permute-done.11.un.refs_8_
  47.6 0.1 pack.1.packed
  47.7 2.5 %near_times.3 = f32[256,1,16]{2,1,0:T(1,128)} custom-call(s32[8,128]{1,0:T(8,128)S(1)} %get-tuple-element.68.lists, s32[1,1280]{1,0:T(1,128)S(1)} %get-tuple-element.69.long, f32[3,3]{1,0:T(4,128)S(1)} %get-tuple-element.51.corr, bf16[112,128,256]{2,1,0:T(8,128)(2,1)S(1)} %get-tuple-element.70.cache, f32[64,8,128]{2,1,0:T(8,128)S(1)} %get-tuple-element.71.q_ref.q_near, ...), custom_call_target="tpu_custom_call" | custom-call | flops 100000000 | bytes 1048576 | tf_op jit(solution)/shard_map/near_times/pallas_call | solution.py:870
  50.2 14.7 %all-to-all-start = ((f32[256,1,16]{2,1,0:T(1,128)}), f32[256,1,16]{2,1,0:T(1,128)S(1)}, u32[]{:S(2)}, u32[]{:S(2)}) async-start(f32[256,1,16]{2,1,0:T(1,128)} %near_times.3), calls=%async_computation | async-start | bytes 262144 | tf_op jit(solution)/shard_map/all_to_all | solution.py:897
  64.9 5.3 %grid.1.g = f32[3,3,512]{2,1,0:T(4,128)S(1)} custom-call(s32[8,128]{1,0:T(8,128)S(1)} %get-tuple-element.90.lists_v, s32[16,128]{1,0:T(8,128)S(1)} %get-tuple-element.91.mask_v, f32[3,3]{1,0:T(4,128)S(1)} %get-tuple-element.51.corr, f32[8,8]{1,0:T(8,128)S(1)} %get-tuple-element.49.frame, f32[72,16,128]{2,1,0:T(8,128)S(1)} %pack.1.packed, ...), custom_call_target="tpu_custom_call" | custom-call | flops 1000000000 | bytes 1048576 | tf_op jit(solution)/shard_map/grid/pallas_call | solution.py:898
  70.3 7.7 %all-to-all-done.parts = f32[256,1,16]{2,1,0:T(1,128)S(1)} async-done(((f32[256,1,16]{2,1,0:T(1,128)}), f32[256,1,16]{2,1,0:T(1,128)S(1)}, u32[]{:S(2)}, u32[]{:S(2)}) %all-to-all-start) | async-done | bytes 16416 | tf_op jit(solution)/shard_map/all_to_all | solution.py:897
  78.0 0.8 %final.1 = (f32[3,1,1024]{2,1,0:T(1,128)}, f32[3,1,512]{2,1,0:T(1,128)}) custom-call(f32[256,1,16]{2,1,0:T(1,128)S(1)} %all-to-all-done.parts, f32[3,1024]{1,0:T(4,128)S(1)} %get-tuple-element.88.innov, f32[2,3,1024]{2,1,0:T(4,128)S(1)} %unsort.1.w, f32[3,3,512]{2,1,0:T(4,128)S(1)} %grid.1.g), custom_call_target="tpu_custom_call" | custom-call | flops 1000000 | bytes 1048576 | tf_op jit(solution)/shard_map/final/pallas_call | solution.py:915
  (10 shorter events, 0.1 us)
Async XLA Ops:
  4.3 8.9 %collective-permute-start.1 = (f32[8,1024]{1,0:T(8,128)S(1)}, f32[8,1024]{1,0:T(8,128)S(1)}, u32[]{:S(2)}, u32[]{:S(2)}) collective-permute-start(f32[8,1024]{1,0:T(8,128)S(1)} %get-tuple-element.52.hb), channel_id=1, source_target_pairs={{1,2},{2,1},{3,4},{4,3},{5,6},{6,5},{7,8},{8,7},{9,10},{10,9},{11,... | collective-permute-start | bytes 98312 | tf_op jit(solution)/shard_map/ppermute | solution.py:719
  10.2 3.1 %collective-permute-start = (f32[8,1024]{1,0:T(8,128)S(1)}, f32[8,1024]{1,0:T(8,128)S(1)}, u32[]{:S(2)}, u32[]{:S(2)}) collective-permute-start(f32[8,1024]{1,0:T(8,128)S(1)} %get-tuple-element.52.hb), channel_id=1, source_target_pairs={{0,1},{1,0},{2,3},{3,2},{4,5},{5,4},{6,7},{7,6},{8,9},{9,8},{10,11... | collective-permute-start | bytes 98312 | tf_op jit(solution)/shard_map/ppermute | solution.py:719
  13.3 7.1 %collective-permute-start.3 = (f32[3,8,1024]{2,1,0:T(8,128)S(1)}, f32[3,8,1024]{2,1,0:T(8,128)S(1)}, u32[]{:S(2)}, u32[]{:S(2)}) collective-permute-start(f32[3,8,1024]{2,1,0:T(8,128)S(1)} %pad_maximum_fusion.mid.refs_0_), channel_id=1, source_target_pairs={{16,32},{32,16},{48,64},{64,48},{80,96},{96,80},{112,128},{128,112... | collective-permute-start | bytes 294920 | tf_op jit(solution)/shard_map/ppermute | solution.py:719
  16.7 3.7 %collective-permute-start.2 = (f32[3,8,1024]{2,1,0:T(8,128)S(1)}, f32[3,8,1024]{2,1,0:T(8,128)S(1)}, u32[]{:S(2)}, u32[]{:S(2)}) collective-permute-start(f32[3,8,1024]{2,1,0:T(8,128)S(1)} %pad_maximum_fusion.mid.refs_0_), channel_id=1, source_target_pairs={{0,16},{16,0},{32,48},{48,32},{64,80},{80,64},{96,112},{112,96},{1... | collective-permute-start | bytes 294920 | tf_op jit(solution)/shard_map/ppermute | solution.py:719
  24.4 6.0 %collective-permute-start.5 = (f32[4,1024]{1,0:T(4,128)S(1)}, f32[4,1024]{1,0:T(4,128)S(1)}, u32[]{:S(2)}, u32[]{:S(2)}) collective-permute-start(f32[4,1024]{1,0:T(4,128)S(1)} %get-tuple-element.73.u), channel_id=1, source_target_pairs={{1,2},{2,1},{3,4},{4,3},{5,6},{6,5},{7,8},{8,7},{9,10},{10,9},{11,... | collective-permute-start | bytes 49160 | tf_op jit(solution)/shard_map/ppermute | solution.py:719
  27.2 3.2 %collective-permute-start.4 = (f32[4,1024]{1,0:T(4,128)S(1)}, f32[4,1024]{1,0:T(4,128)S(1)}, u32[]{:S(2)}, u32[]{:S(2)}) collective-permute-start(f32[4,1024]{1,0:T(4,128)S(1)} %get-tuple-element.73.u), channel_id=1, source_target_pairs={{0,1},{1,0},{2,3},{3,2},{4,5},{5,4},{6,7},{7,6},{8,9},{9,8},{10,11... | collective-permute-start | bytes 49160 | tf_op jit(solution)/shard_map/ppermute | solution.py:719
  30.4 4.3 %collective-permute-start.7 = (f32[3,4,1024]{2,1,0:T(4,128)S(1)}, f32[3,4,1024]{2,1,0:T(4,128)S(1)}, u32[]{:S(2)}, u32[]{:S(2)}) collective-permute-start(f32[3,4,1024]{2,1,0:T(4,128)S(1)} %pad_maximum_fusion.1.um.refs_3_), channel_id=1, source_target_pairs={{16,32},{32,16},{48,64},{64,48},{80,96},{96,80},{112,128},{128,112... | collective-permute-start | bytes 147464 | tf_op jit(solution)/shard_map/ppermute | solution.py:719
  32.9 2.2 %collective-permute-start.6 = (f32[3,4,1024]{2,1,0:T(4,128)S(1)}, f32[3,4,1024]{2,1,0:T(4,128)S(1)}, u32[]{:S(2)}, u32[]{:S(2)}) collective-permute-start(f32[3,4,1024]{2,1,0:T(4,128)S(1)} %pad_maximum_fusion.1.um.refs_3_), channel_id=1, source_target_pairs={{0,16},{16,0},{32,48},{48,32},{64,80},{80,64},{96,112},{112,96},{1... | collective-permute-start | bytes 147464 | tf_op jit(solution)/shard_map/ppermute | solution.py:719
  36.8 6.0 %collective-permute-start.9 = (f32[4,1024]{1,0:T(4,128)S(1)}, f32[4,1024]{1,0:T(4,128)S(1)}, u32[]{:S(2)}, u32[]{:S(2)}) collective-permute-start(f32[4,1024]{1,0:T(4,128)S(1)} %get-tuple-element.80.u), channel_id=1, source_target_pairs={{1,2},{2,1},{3,4},{4,3},{5,6},{6,5},{7,8},{8,7},{9,10},{10,9},{11,... | collective-permute-start | bytes 49160 | tf_op jit(solution)/shard_map/ppermute | solution.py:719
  39.9 2.9 %collective-permute-start.8 = (f32[4,1024]{1,0:T(4,128)S(1)}, f32[4,1024]{1,0:T(4,128)S(1)}, u32[]{:S(2)}, u32[]{:S(2)}) collective-permute-start(f32[4,1024]{1,0:T(4,128)S(1)} %get-tuple-element.80.u), channel_id=1, source_target_pairs={{0,1},{1,0},{2,3},{3,2},{4,5},{5,4},{6,7},{7,6},{8,9},{9,8},{10,11... | collective-permute-start | bytes 49160 | tf_op jit(solution)/shard_map/ppermute | solution.py:719
  42.8 4.8 %collective-permute-start.11 = (f32[3,4,1024]{2,1,0:T(4,128)S(1)}, f32[3,4,1024]{2,1,0:T(4,128)S(1)}, u32[]{:S(2)}, u32[]{:S(2)}) collective-permute-start(f32[3,4,1024]{2,1,0:T(4,128)S(1)} %pad_maximum_fusion.2.um.refs_6_), channel_id=1, source_target_pairs={{16,32},{32,16},{48,64},{64,48},{80,96},{96,80},{112,128},{128,112... | collective-permute-start | bytes 147464 | tf_op jit(solution)/shard_map/ppermute | solution.py:719
  45.8 1.8 %collective-permute-start.10 = (f32[3,4,1024]{2,1,0:T(4,128)S(1)}, f32[3,4,1024]{2,1,0:T(4,128)S(1)}, u32[]{:S(2)}, u32[]{:S(2)}) collective-permute-start(f32[3,4,1024]{2,1,0:T(4,128)S(1)} %pad_maximum_fusion.2.um.refs_6_), channel_id=1, source_target_pairs={{0,16},{16,0},{32,48},{48,32},{64,80},{80,64},{96,112},{112,96},{1... | collective-permute-start | bytes 147464 | tf_op jit(solution)/shard_map/ppermute | solution.py:719
  50.2 27.8 %all-to-all-start = ((f32[256,1,16]{2,1,0:T(1,128)}), f32[256,1,16]{2,1,0:T(1,128)S(1)}, u32[]{:S(2)}, u32[]{:S(2)}) async-start(f32[256,1,16]{2,1,0:T(1,128)} %near_times.3), calls=%async_computation | async-start | bytes 262144 | tf_op jit(solution)/shard_map/all_to_all | solution.py:897
